TPU v7x, 32 devices: a whole 2x2x4 slice. The times are simulated.
32 devices in a mesh: batch: 2 (over y), branch: 2 (over core), tensor: 8 (over z, x).
Axes of the slice: x: 2, y: 2, z: 4, core: 2. Of those that a mesh axis runs over, the one named last changes fastest.
Arguments:
- tokens: bfloat16 [2, 8, 1024, 2048], P(None, ('batch', 'branch'), 'tensor'), may hold values from -6 to 6
- cotangent: bfloat16 [2, 8, 1024, 2048], P(None, ('batch', 'branch'), 'tensor'), may hold values from -6 to 6
- segments: int32 [2, 8, 1024], P(None, ('batch', 'branch')), may hold values from 0 to 3, as said below
- positions: int32 [2, 8, 1024], P(None, ('batch', 'branch')), may hold values from 0 to 1023, as said below
- ln_gain: float32 [2048], replicated, may hold values from 0.5 to 1.5
- ln_bias: float32 [2048], replicated, may hold values from -1.25 to 1.25
- qkv_weight: bfloat16 [2048, 3, 2048], P(('batch', 'branch'), None, 'tensor'), may hold values from -0.125 to 0.125
- qkv_bias: float32 [3, 2048], P(None, 'tensor'), may hold values from -1.25 to 1.25
- dense_weight: bfloat16 [2048, 2048], P('tensor', ('batch', 'branch')), may hold values from -0.5 to 0.5
- dense_bias: float32 [2048], replicated, may hold values from -1.75 to 1.75
- up_weight: bfloat16 [2048, 8192], P(('batch', 'branch'), 'tensor'), may hold values from -0.125 to 0.125
- up_bias: float32 [8192], P('tensor'), may hold values from -1.75 to 1.75
- down_weight: bfloat16 [8192, 2048], P('tensor', ('batch', 'branch')), may hold values from -0.0625 to 0.0625
- down_bias: float32 [2048], replicated, may hold values from -1.75 to 1.75
Outputs:
- mixed: bfloat16 [2, 8, 1024, 2048], P(None, ('batch', 'branch'), 'tensor')
- tokens_grad: float32 [2, 8, 1024, 2048], P(None, ('batch', 'branch'), 'tensor')
- ln_gain_grad: float32 [2048], replicated
- ln_bias_grad: float32 [2048], replicated
- qkv_weight_grad: float32 [2048, 3, 2048], P(('batch', 'branch'), None, 'tensor')
- qkv_bias_grad: float32 [3, 2048], P(None, 'tensor')
- dense_weight_grad: float32 [2048, 2048], P('tensor', ('batch', 'branch'))
- dense_bias_grad: float32 [2048], replicated
- up_weight_grad: float32 [2048, 8192], P(('batch', 'branch'), 'tensor')
- up_bias_grad: float32 [8192], P('tensor')
- down_weight_grad: float32 [8192, 2048], P('tensor', ('batch', 'branch'))
- down_bias_grad: float32 [2048], replicated
Inputs may be any that keep to these rules, and one draw needn't show every extreme that they name: `segments`: each sequence holds four documents numbered 0 to 3 in order, none empty. Within a document positions rise by one from token to token; the first document of each sequence starts at 0; the last token of each sequence has position 1023.
All inputs are finite; a program needn't handle non-finite values.
Results may differ from a plain program's by a relative error of at most 0.012.
Values may be sent and summed in bfloat16 or wider, within the bound.
No kernel may reach another device: no remote copies, remote signals or barrier semaphores. Data moves between devices by JAX's collectives and lax.ppermute only.
A program may use at most 384 MiB of HBM per device.

v0:
```python
from functools import partial

import jax
import jax.numpy as jnp
from jax import lax
from jax.sharding import PartitionSpec as P

HEAD_DIM = 64
ROT = 32


eps_norm = 1e-05
rope_base = 10000.0
masked_score = -1e30


def layer_norm(residual, norm_gain, norm_shift):
    row_mean = jnp.mean(residual, -1, keepdims=True)
    centered = residual - row_mean
    variance = jnp.mean(centered * centered, -1, keepdims=True)
    return centered * lax.rsqrt(variance + eps_norm) * norm_gain + norm_shift


def rope_tables(token_place):
    half_dims = ROT // 2
    exponent = jnp.arange(half_dims, dtype=jnp.float32) * (2.0 / ROT)
    inverse = rope_base ** (-exponent)
    angles = token_place.astype(jnp.float32)[..., None] * inverse
    return (jnp.cos(angles), jnp.sin(angles))


def rotate(values, cosine, sine_table):
    half_dims = ROT // 2
    lower_half = values[..., :half_dims]
    upper_half = values[..., half_dims:ROT]
    cos_wide = cosine[..., None, :]
    sin_wide = sine_table[..., None, :]
    return jnp.concatenate(
        [
            lower_half * cos_wide - upper_half * sin_wide,
            upper_half * cos_wide + lower_half * sin_wide,
            values[..., ROT:],
        ],
        axis=-1,
    )


def masked_scores(query_block, key_heads, row_ids, seg_ids, segment, score_scale):
    scores = (
        jnp.einsum("qhe,khe->hqk", query_block, key_heads, preferred_element_type=jnp.float32)
        * score_scale
    )
    columns = jnp.arange(key_heads.shape[0], dtype=jnp.int32)
    allowed = (columns[None, :] <= row_ids[:, None]) & (seg_ids[:, None] == segment[None, :])
    return jnp.where(allowed[None], scores, masked_score)


def split_blocks(queries, segment, block_rows):
    full_len = queries.shape[0]
    block_count = full_len // block_rows
    query_blocks = queries.reshape(block_count, block_rows, queries.shape[1], queries.shape[2])
    row_index = jnp.arange(full_len, dtype=jnp.int32).reshape(block_count, block_rows)
    return (query_blocks, row_index, segment.reshape(block_count, block_rows))


def attend_forward(queries, key_heads, value_heads, segment):
    full_len, head_count, head_size = queries.shape
    block_rows = min(512, full_len)
    score_scale = head_size ** (-0.5)
    query_blocks, row_index, seg_blocks = split_blocks(queries, segment, block_rows)

    def per_block(inputs):
        query_block, row_ids, seg_ids = inputs
        scores = masked_scores(query_block, key_heads, row_ids, seg_ids, segment, score_scale)
        row_max = jnp.max(scores, -1, keepdims=True)
        exponent = jnp.exp(scores - row_max)
        row_total = jnp.sum(exponent, -1, keepdims=True)
        probs_low = (exponent / row_total).astype(jnp.bfloat16)
        block_out = jnp.einsum(
            "hqk,khe->qhe", probs_low, value_heads, preferred_element_type=jnp.float32
        )
        return (block_out, (row_max + jnp.log(row_total))[..., 0])

    block_outs, log_totals = lax.map(per_block, (query_blocks, row_index, seg_blocks))
    return (block_outs.reshape(full_len, head_count, head_size), log_totals)


def attend_backward(queries, key_heads, value_heads, segment, log_totals, grad_attn):
    full_len, head_count, head_size = queries.shape
    block_rows = min(512, full_len)
    score_scale = head_size ** (-0.5)
    query_blocks, row_index, seg_blocks = split_blocks(queries, segment, block_rows)
    grad_blocks = grad_attn.reshape(query_blocks.shape)

    def per_block(running, inputs):
        grad_keys, grad_values = running
        query_block, row_ids, seg_ids, log_block, grad_block = inputs
        scores = masked_scores(query_block, key_heads, row_ids, seg_ids, segment, score_scale)
        attn_probs = jnp.exp(scores - log_block[..., None])
        probs_low = attn_probs.astype(jnp.bfloat16)
        grad_probs = jnp.einsum(
            "qhe,khe->hqk", grad_block, value_heads, preferred_element_type=jnp.float32
        )
        inner = jnp.sum(attn_probs * grad_probs, -1, keepdims=True)
        grad_scores = (attn_probs * (grad_probs - inner)).astype(jnp.bfloat16)
        grad_query = (
            jnp.einsum("hqk,khe->qhe", grad_scores, key_heads, preferred_element_type=jnp.float32)
            * score_scale
        )
        grad_keys = (
            grad_keys
            + jnp.einsum(
                "hqk,qhe->khe", grad_scores, query_block, preferred_element_type=jnp.float32
            )
            * score_scale
        )
        grad_values = grad_values + jnp.einsum(
            "hqk,qhe->khe", probs_low, grad_block, preferred_element_type=jnp.float32
        )
        return ((grad_keys, grad_values), grad_query)

    zero_heads = jnp.zeros((full_len, head_count, head_size), jnp.float32)
    (grad_keys, grad_values), grad_queries = lax.scan(
        per_block,
        (zero_heads, zero_heads),
        (query_blocks, row_index, seg_blocks, log_totals, grad_blocks),
    )
    return (grad_queries.reshape(full_len, head_count, head_size), grad_keys, grad_values)


def body(
    tokens,
    cotangent,
    segments,
    positions,
    ln_gain,
    ln_bias,
    qkv_weight,
    qkv_bias,
    dense_weight,
    dense_bias,
    up_weight,
    up_bias,
    down_weight,
    down_bias,
):
    micro_count, seq_count, shard_len, model_width = tokens.shape
    full_len = segments.shape[2]
    local_width = qkv_weight.shape[2]
    local_heads = local_width // HEAD_DIM
    row_count = seq_count * full_len
    weight_totals = None
    outputs = []
    input_grads = []
    bias_qkv_total = jnp.zeros((3, local_width), jnp.float32)
    bias_up_total = jnp.zeros((up_bias.shape[0],), jnp.float32)
    gain_total = jnp.zeros((model_width,), jnp.float32)
    shift_total = jnp.zeros((model_width,), jnp.float32)
    out_bias_total = jnp.zeros((model_width,), jnp.float32)
    for micro_index in range(micro_count):
        gathered = (
            lax.all_gather(qkv_weight, ("batch", "branch"), axis=0, tiled=True),
            lax.all_gather(dense_weight, ("batch", "branch"), axis=1, tiled=True),
            lax.all_gather(up_weight, ("batch", "branch"), axis=0, tiled=True),
            lax.all_gather(down_weight, ("batch", "branch"), axis=1, tiled=True),
        )
        qkv_full, dense_full, up_full, down_full = gathered
        residual = tokens[micro_index].astype(jnp.float32)
        cot_shard = cotangent[micro_index]
        normed = layer_norm(residual, ln_gain, ln_bias).astype(jnp.bfloat16)
        ln_rows = lax.all_gather(normed, "tensor", axis=1, tiled=True).reshape(
            row_count, model_width
        )
        projected = (
            jnp.einsum("nd,dce->nce", ln_rows, qkv_full, preferred_element_type=jnp.float32)
            + qkv_bias
        )
        projected = projected.reshape(seq_count, full_len, 3, local_heads, HEAD_DIM)
        cosine, sine_table = rope_tables(positions[micro_index])

        def rotate_pair(query_pre, key_pre):
            return (rotate(query_pre, cosine, sine_table), rotate(key_pre, cosine, sine_table))

        (query_rot, key_rot), rope_pull = jax.vjp(
            rotate_pair, projected[:, :, 0], projected[:, :, 1]
        )
        queries = query_rot.astype(jnp.bfloat16)
        key_heads = key_rot.astype(jnp.bfloat16)
        value_heads = projected[:, :, 2].astype(jnp.bfloat16)
        segment_rows = segments[micro_index]
        attn_heads, log_totals = lax.map(
            lambda inputs: attend_forward(*inputs), (queries, key_heads, value_heads, segment_rows)
        )
        attn_low = attn_heads.reshape(row_count, local_width).astype(jnp.bfloat16)
        hidden_pre = jnp.dot(ln_rows, up_full, preferred_element_type=jnp.float32) + up_bias
        activated = jax.nn.gelu(hidden_pre, approximate=True).astype(jnp.bfloat16)
        branch_terms = jnp.dot(attn_low, dense_full, preferred_element_type=jnp.float32) + jnp.dot(
            activated, down_full, preferred_element_type=jnp.float32
        )
        summed = lax.psum_scatter(
            branch_terms.reshape(seq_count, full_len, model_width),
            "tensor",
            scatter_dimension=1,
            tiled=True,
        )
        outputs.append((residual + summed + dense_bias + down_bias).astype(jnp.bfloat16))
        grad_rows = lax.all_gather(cot_shard, "tensor", axis=1, tiled=True).reshape(
            row_count, model_width
        )
        back_rows = lax.all_gather(
            layer_norm(residual, ln_gain, ln_bias).astype(jnp.bfloat16),
            "tensor",
            axis=1,
            tiled=True,
        ).reshape(row_count, model_width)
        grad_down = jnp.einsum(
            "nf,nd->fd", activated, grad_rows, preferred_element_type=jnp.float32
        )
        grad_act = jnp.einsum("nd,fd->nf", grad_rows, down_full, preferred_element_type=jnp.float32)
        gelu_value, gelu_pull = jax.vjp(partial(jax.nn.gelu, approximate=True), hidden_pre)
        grad_pre = gelu_pull(grad_act)[0].astype(jnp.bfloat16)
        grad_up = jnp.einsum("nd,nf->df", back_rows, grad_pre, preferred_element_type=jnp.float32)
        bias_up_total = bias_up_total + jnp.sum(grad_pre, 0, dtype=jnp.float32)
        grad_normed = jnp.einsum("nf,df->nd", grad_pre, up_full, preferred_element_type=jnp.float32)
        grad_dense = jnp.einsum(
            "ne,nd->ed", attn_low, grad_rows, preferred_element_type=jnp.float32
        )
        grad_attn = jnp.einsum(
            "nd,ed->ne", grad_rows, dense_full, preferred_element_type=jnp.float32
        ).astype(jnp.bfloat16)
        grad_attn = grad_attn.reshape(seq_count, full_len, local_heads, HEAD_DIM)
        grad_queries, grad_keys, grad_values = lax.map(
            lambda inputs: attend_backward(*inputs),
            (queries, key_heads, value_heads, segment_rows, log_totals, grad_attn),
        )
        grad_qpre, grad_kpre = rope_pull((grad_queries, grad_keys))
        grad_proj = (
            jnp.stack([grad_qpre, grad_kpre, grad_values], axis=2)
            .astype(jnp.bfloat16)
            .reshape(row_count, 3, local_width)
        )
        grad_qkv = jnp.einsum(
            "nd,nce->dce", back_rows, grad_proj, preferred_element_type=jnp.float32
        )
        bias_qkv_total = bias_qkv_total + jnp.sum(grad_proj, 0, dtype=jnp.float32)
        grad_normed = grad_normed + jnp.einsum(
            "nce,dce->nd", grad_proj, qkv_full, preferred_element_type=jnp.float32
        )
        grad_shard = lax.psum_scatter(
            grad_normed.reshape(seq_count, full_len, model_width).astype(jnp.bfloat16),
            "tensor",
            scatter_dimension=1,
            tiled=True,
        ).astype(jnp.float32)
        norm_value, norm_pull = jax.vjp(layer_norm, residual, ln_gain, ln_bias)
        grad_resid, grad_gain, grad_shift = norm_pull(grad_shard)
        input_grads.append(cot_shard.astype(jnp.float32) + grad_resid)
        gain_total = gain_total + grad_gain
        shift_total = shift_total + grad_shift
        out_bias_total = out_bias_total + jnp.sum(cot_shard, (0, 1), dtype=jnp.float32)
        local_grads = (grad_qkv, grad_dense, grad_up, grad_down)
        fresh = (
            lax.psum_scatter(
                local_grads[0].astype(jnp.bfloat16),
                ("batch", "branch"),
                scatter_dimension=0,
                tiled=True,
            ).astype(jnp.float32),
            lax.psum_scatter(
                local_grads[1].astype(jnp.bfloat16),
                ("batch", "branch"),
                scatter_dimension=1,
                tiled=True,
            ).astype(jnp.float32),
            lax.psum_scatter(
                local_grads[2].astype(jnp.bfloat16),
                ("batch", "branch"),
                scatter_dimension=0,
                tiled=True,
            ).astype(jnp.float32),
            lax.psum_scatter(
                local_grads[3].astype(jnp.bfloat16),
                ("batch", "branch"),
                scatter_dimension=1,
                tiled=True,
            ).astype(jnp.float32),
        )
        if micro_index == 0:
            weight_totals = fresh
        else:
            weight_totals = jax.tree.map(jnp.add, weight_totals, fresh)
    bias_qkv_grad, bias_up_grad = lax.psum((bias_qkv_total, bias_up_total), ("batch", "branch"))
    gain_grad, shift_grad, out_bias_grad = lax.psum(
        (gain_total, shift_total, out_bias_total), ("batch", "branch", "tensor")
    )
    mixed = jnp.stack(outputs, 0)
    tokens_grad = jnp.stack(input_grads, 0)
    return (
        mixed,
        tokens_grad,
        gain_grad,
        shift_grad,
        weight_totals[0],
        bias_qkv_grad,
        weight_totals[1],
        out_bias_grad,
        weight_totals[2],
        bias_up_grad,
        weight_totals[3],
        out_bias_grad,
    )


def solution(mesh):
    in_specs = (
        P(None, ("batch", "branch"), "tensor", None),
        P(None, ("batch", "branch"), "tensor", None),
        P(None, ("batch", "branch"), None),
        P(None, ("batch", "branch"), None),
        P(),
        P(),
        P(("batch", "branch"), None, "tensor"),
        P(None, "tensor"),
        P("tensor", ("batch", "branch")),
        P(),
        P(("batch", "branch"), "tensor"),
        P("tensor"),
        P("tensor", ("batch", "branch")),
        P(),
    )
    out_specs = (
        P(None, ("batch", "branch"), "tensor", None),
        P(None, ("batch", "branch"), "tensor", None),
        P(),
        P(),
        P(("batch", "branch"), None, "tensor"),
        P(None, "tensor"),
        P("tensor", ("batch", "branch")),
        P(),
        P(("batch", "branch"), "tensor"),
        P("tensor"),
        P("tensor", ("batch", "branch")),
        P(),
    )
    return jax.shard_map(body, mesh=mesh, in_specs=in_specs, out_specs=out_specs, check_vma=False)
```

profile of v0, /device:TPU:0, one launch (start us, length us, event | category | flops | bytes accessed | tf_op | source)
XLA Modules:
  0.0 2187.8 jit_solution(4022547574454290366)
XLA Ops:
  25.6 15.3 all-gather.13.cloned.1.call-done
  40.9 127.7 %all-gather.21.cloned.1.call-done = bf16[2,1024,2048]{2,1,0:T(8,128)(2,1)} async-done(((bf16[2,128,2048]{2,1,0:T(8,128)(2,1)}), bf16[2,1024,2048]{2,1,0:T(8,128)(2,1)}) %all-gather.21.cloned.1.call-update) | async-done | bytes 8388624 | tf_op jit(solution)/shard_map/all_gather | solution.py:171
  204.1 90.4 %all-gather.11.cloned.1.call-done = bf16[2,1024,2048]{2,1,0:T(8,128)(2,1)} async-done(((bf16[2,128,2048]{2,1,0:T(8,128)(2,1)}), bf16[2,1024,2048]{2,1,0:T(8,128)(2,1)}) %all-gather.11.cloned.1.call-update) | async-done | bytes 8388624 | tf_op jit(solution)/shard_map/all_gather | solution.py:171
  331.5 106.3 %all-gather.25.cloned.1.call-done = bf16[1,2,1024,2048]{3,2,1,0:T(8,128)(2,1)} async-done(((bf16[1,2,128,2048]{3,2,1,0:T(8,128)(2,1)}), bf16[1,2,1024,2048]{3,2,1,0:T(8,128)(2,1)}) %all-gather.25.cloned.1.call-update) | async-done | bytes 8388624 | tf_op jit(solution)/shard_map/all_gather | solution.py:207
  464.1 42.8 %while.109 = (s32[]{:T(128)}, bf16[2,1024,4,64]{3,2,1,0:T(4,128)(2,1)}, f32[2,2,4,512]{3,2,1,0:T(4,128)S(1)}, bf16[2,1024,4,64]{1,3,2,0:T(8,128)(2,1)}, s32[2,10...) while((s32[]{:T(128)}, ...), condition=%wide.region_16.17_spmd, body=%wide.region_11.16_spmd.sunk | while | flops 563609600 | bytes 37101920 | solution.py:191
  468.1 15.2 while.115
  512.0 157.7 %while.113 = (s32[]{:T(128)}, f32[2,1024,4,64]{1,0,3,2:T(2,128)}, f32[2,1024,4,64]{1,0,3,2:T(2,128)}, bf16[2,1024,4,64]{1,3,2,0:T(8,128)(2,1)}, bf16[2,1024,4,64...) while((s32[]{:T(128)}, f32[2,1024,4,64]{1,0,3,2:T(2,128)}, ...), condition=%wide.region_30.31_spmd, body=%wide.region_26.30_spmd.sunk | while | flops 1376649216 | bytes 114426472 | solution.py:232
  520.6 27.3 %while.117 = (s32[]{:T(128)}, f32[1024,4,64]{0,2,1:T(8,128)S(1)}, f32[1024,4,64]{0,2,1:T(8,128)}, f32[2,512,4,64]{1,3,2,0:T(8,128)}, bf16[2,512,4,64]{1,3,2,0:T(...) while((s32[]{:T(128)}, f32[1024,4,64]{0,2,1:T(8,128)S(1)}, ...), condition=%wide.region_29.29_spmd.clone, body=%wide.region_27.28_spmd.clone.sunk | while | flops 1376647168 | bytes 89202976 | solution.py:123
  549.0 18.8 dynamic_update_slice.91
  572.0 18.8 dynamic_update_slice.90
  599.3 27.3 %while.117 = (s32[]{:T(128)}, f32[1024,4,64]{0,2,1:T(8,128)S(1)}, f32[1024,4,64]{0,2,1:T(8,128)}, f32[2,512,4,64]{1,3,2,0:T(8,128)}, bf16[2,512,4,64]{1,3,2,0:T(...) while((s32[]{:T(128)}, f32[1024,4,64]{0,2,1:T(8,128)S(1)}, ...), condition=%wide.region_29.29_spmd.clone, body=%wide.region_27.28_spmd.clone.sunk | while | flops 1376647168 | bytes 89202976 | solution.py:123
  627.7 18.8 dynamic_update_slice.91
  650.6 18.8 dynamic_update_slice.90
  685.2 42.8 %while.107 = (s32[]{:T(128)}, bf16[2,1024,4,64]{3,2,1,0:T(4,128)(2,1)}, f32[2,2,4,512]{3,2,1,0:T(4,128)S(1)}, bf16[2,1024,4,64]{1,3,2,0:T(8,128)(2,1)}, s32[2,10...) while((s32[]{:T(128)}, ...), condition=%wide.region_7.8_spmd, body=%wide.region_2.7_spmd.sunk | while | flops 563609600 | bytes 37101920 | solution.py:191
  689.3 15.2 while.114
  795.5 157.6 %while.111 = (s32[]{:T(128)}, f32[2,1024,4,64]{1,0,3,2:T(2,128)}, f32[2,1024,4,64]{1,0,3,2:T(2,128)}, bf16[2,1024,4,64]{1,3,2,0:T(8,128)(2,1)}, bf16[2,1024,4,64...) while((s32[]{:T(128)}, f32[2,1024,4,64]{1,0,3,2:T(2,128)}, ...), condition=%wide.region_22.23_spmd, body=%wide.region_18.22_spmd.sunk | while | flops 1376649216 | bytes 114426472 | solution.py:232
  804.3 27.4 %while.116 = (s32[]{:T(128)}, f32[1024,4,64]{0,2,1:T(8,128)S(1)}, f32[1024,4,64]{0,2,1:T(8,128)}, f32[2,512,4,64]{1,3,2,0:T(8,128)}, bf16[2,512,4,64]{1,3,2,0:T(...) while((s32[]{:T(128)}, f32[1024,4,64]{0,2,1:T(8,128)S(1)}, ...), condition=%wide.region_21.21_spmd.clone, body=%wide.region_19.20_spmd.clone.sunk | while | flops 1376647168 | bytes 89202976 | solution.py:123
  832.8 18.8 dynamic_update_slice.88
  855.7 18.8 dynamic_update_slice.87
  882.9 27.3 %while.116 = (s32[]{:T(128)}, f32[1024,4,64]{0,2,1:T(8,128)S(1)}, f32[1024,4,64]{0,2,1:T(8,128)}, f32[2,512,4,64]{1,3,2,0:T(8,128)}, bf16[2,512,4,64]{1,3,2,0:T(...) while((s32[]{:T(128)}, f32[1024,4,64]{0,2,1:T(8,128)S(1)}, ...), condition=%wide.region_21.21_spmd.clone, body=%wide.region_19.20_spmd.clone.sunk | while | flops 1376647168 | bytes 89202976 | solution.py:123
  911.3 18.8 dynamic_update_slice.88
  934.1 18.8 dynamic_update_slice.87
  1029.5 26.4 %convert_reduce_fusion.1 = (f32[1024]{0:T(1024)}, bf16[2048,1024]{1,0:T(8,128)(2,1)}, f32[1024]{0:T(1024)}, bf16[2048,1024]{1,0:T(8,128)(2,1)}) fusion(f32[2048,1024]{1,0:T(8,128)} %fusion.155, f32[1024]{0:T(1024)S(1)} %copy-done.82, f32[2048,1024]{1,0:T(8,128)} %fusion.158, f32[2048,1024]{1,0:T(8,128)} %fusion.156, bf16[2048,2048]{1,0:T(8,128)(2,1)S(1)} %bitcast.509, ...), kind=kOutput, calls=%fused_computation.163 | convolution fusion | flops 8686401536 | bytes 46149632 | tf_op jit(solution)/shard_map/nd,fd->nf/dot_general | solution.py:219
  1084.4 17.2 convolution_convert_fusion
  1101.7 16.8 convolution_convert_fusion.1
  1118.6 16.3 fusion.157
  1147.4 15.8 fusion.159
  1257.5 149.1 %reduce-scatter.17.cloned.1.call-done = bf16[2,128,2048]{2,1,0:T(8,128)(2,1)} async-done(((bf16[2,1024,2048]{2,1,0:T(8,128)(2,1)}), bf16[2,128,2048]{2,1,0:T(8,128)(2,1)}) %reduce-scatter.17.cloned.1.call-update) | async-done | bytes 1048592 | tf_op jit(solution)/shard_map/reduce_scatter | solution.py:249
  1406.6 151.9 %reduce-scatter.19.cloned.1.call-done = bf16[2,128,2048]{2,1,0:T(8,128)(2,1)} async-done(((bf16[2,1024,2048]{2,1,0:T(8,128)(2,1)}), bf16[2,128,2048]{2,1,0:T(8,128)(2,1)}) %reduce-scatter.19.cloned.1.call-update) | async-done | bytes 1048592 | tf_op jit(solution)/shard_map/reduce_scatter | solution.py:249
  1561.3 282.0 %reduce-scatter.13.cloned.1.call-done = f32[2,128,2048]{2,1,0:T(8,128)} async-done(((f32[2,1024,2048]{2,1,0:T(8,128)}), f32[2,128,2048]{2,1,0:T(8,128)}) %reduce-scatter.13.cloned.1.call-update) | async-done | bytes 2097168 | tf_op jit(solution)/shard_map/reduce_scatter | solution.py:200
  1843.3 285.3 %reduce-scatter.15.cloned.1.call-done = f32[2,128,2048]{2,1,0:T(8,128)} async-done(((f32[2,1024,2048]{2,1,0:T(8,128)}), f32[2,128,2048]{2,1,0:T(8,128)}) %reduce-scatter.15.cloned.1.call-update) | async-done | bytes 2097168 | tf_op jit(solution)/shard_map/reduce_scatter | solution.py:200
  2133.8 39.3 %all-reduce.12 = (f32[2048]{0:T(1024)}, f32[2048]{0:T(1024)}, f32[2048]{0:T(1024)S(1)}) all-reduce(f32[2048]{0:T(1024)S(1)} %add.344, f32[2048]{0:T(1024)S(1)} %add.345, f32[2048]{0:T(1024)S(1)} %add.349), channel_id=1, replica_groups=mesh['batch'=2,'branch'=2,'tensor'=8] {'batch','branch','tensor'}, use_global_device_ids=true, to_apply=%region_36.37 | all-reduce | flops 6144 | bytes 49152 | tf_op jit(solution)/shard_map/psum | solution.py:293
  (636 shorter events, 709.8 us)
Async XLA Ops:
  7.2 33.7 %all-gather.13.cloned.1.call-start = ((), (), s32[]{:S(2)}) async-start(), calls=%async_computation.13 | async-start | bytes 3932160 | tf_op jit(solution)/shard_map/all_gather | solution.py:162
  7.9 160.6 %all-gather.21.cloned.1.call-start = ((), (), s32[]{:S(2)}) async-start(), calls=%async_computation.18 | async-start | bytes 9437184 | tf_op jit(solution)/shard_map/all_gather | solution.py:171
  13.4 281.1 %all-gather.11.cloned.1.call-start = ((), (), s32[]{:S(2)}) async-start(), calls=%async_computation.12 | async-start | bytes 9437184 | tf_op jit(solution)/shard_map/all_gather | solution.py:171
  14.2 317.4 %all-gather.15.cloned.1.call-start = ((), (), s32[]{:S(2)}) async-start(), calls=%async_computation.14 | async-start | bytes 1310720 | tf_op jit(solution)/shard_map/all_gather | solution.py:163
  14.8 423.0 %all-gather.25.cloned.1.call-start = ((), (), s32[]{:S(2)}) async-start(), calls=%async_computation.31 | async-start | bytes 9437184 | tf_op jit(solution)/shard_map/all_gather | solution.py:207
  18.0 720.8 %all-gather.23.cloned.1.call-start = ((), (), s32[]{:S(2)}) async-start(), calls=%async_computation.30 | async-start | bytes 9437184 | tf_op jit(solution)/shard_map/all_gather | solution.py:207
  18.6 967.7 %all-gather.19.cloned.1.call-start = ((), (), s32[]{:S(2)}) async-start(), calls=%async_computation.16 | async-start | bytes 5242880 | tf_op jit(solution)/shard_map/all_gather | solution.py:165
  19.3 981.7 %all-gather.17.cloned.1.call-start = ((), (), s32[]{:S(2)}) async-start(), calls=%async_computation.15 | async-start | bytes 5242880 | tf_op jit(solution)/shard_map/all_gather | solution.py:164
  20.1 1214.8 %reduce-scatter.27.cloned.1.call-start = ((), (), s32[]{:S(2)}) async-start(), calls=%async_computation.25 | async-start | bytes 1310720 | tf_op jit(solution)/shard_map/reduce_scatter | solution.py:269
  25.6 429.9 %copy-start.50 = (f32[2,1024,16]{1,0,2:T(2,128)}, f32[2,1024,16]{1,0,2:T(2,128)S(1)}, u32[]{:S(2)}) copy-start(f32[2,1024,16]{1,0,2:T(2,128)S(1)} %get-tuple-element.879) | copy-start | bytes 393220
  25.6 429.9 %copy-start.52 = (f32[2,1024,16]{1,0,2:T(2,128)}, f32[2,1024,16]{1,0,2:T(2,128)S(1)}, u32[]{:S(2)}) copy-start(f32[2,1024,16]{1,0,2:T(2,128)S(1)} %get-tuple-element.880) | copy-start | bytes 393220
  738.8 496.1 %reduce-scatter.25.cloned.1.call-start = ((), (), s32[]{:S(2)}) async-start(), calls=%async_computation.24 | async-start | bytes 1310720 | tf_op jit(solution)/shard_map/reduce_scatter | solution.py:269
  779.5 457.3 %reduce-scatter.23.cloned.1.call-start = ((), (), s32[]{:S(2)}) async-start(), calls=%async_computation.23 | async-start | bytes 3932160 | tf_op jit(solution)/shard_map/reduce_scatter | solution.py:263
  790.3 446.5 %reduce-scatter.21.cloned.1.call-start = ((), (), s32[]{:S(2)}) async-start(), calls=%async_computation.22 | async-start | bytes 3932160 | tf_op jit(solution)/shard_map/reduce_scatter | solution.py:263
  986.2 253.4 %reduce-scatter.29.cloned.1.call-start = ((), (), s32[]{:S(2)}) async-start(), calls=%async_computation.26 | async-start | bytes 5242880 | tf_op jit(solution)/shard_map/reduce_scatter | solution.py:275
  1069.9 169.6 %reduce-scatter.31.cloned.1.call-start = ((), (), s32[]{:S(2)}) async-start(), calls=%async_computation.27 | async-start | bytes 5242880 | tf_op jit(solution)/shard_map/reduce_scatter | solution.py:275
  1084.3 158.7 %reduce-scatter.35.cloned.1.call-start = ((), (), s32[]{:S(2)}) async-start(), calls=%async_computation.29 | async-start | bytes 5242880 | tf_op jit(solution)/shard_map/reduce_scatter | solution.py:281
  1101.6 152.7 %reduce-scatter.33.cloned.1.call-start = ((), (), s32[]{:S(2)}) async-start(), calls=%async_computation.28 | async-start | bytes 5242880 | tf_op jit(solution)/shard_map/reduce_scatter | solution.py:281
  1118.5 288.1 %reduce-scatter.17.cloned.1.call-start = ((), (), s32[]{:S(2)}) async-start(), calls=%async_computation.20 | async-start | bytes 9437184 | tf_op jit(solution)/shard_map/reduce_scatter | solution.py:249
  1147.3 411.2 %reduce-scatter.19.cloned.1.call-start = ((), (), s32[]{:S(2)}) async-start(), calls=%async_computation.21 | async-start | bytes 9437184 | tf_op jit(solution)/shard_map/reduce_scatter | solution.py:249
  1175.7 667.6 %reduce-scatter.13.cloned.1.call-start = ((), (), s32[]{:S(2)}) async-start(), calls=%async_computation.17 | async-start | bytes 18874368 | tf_op jit(solution)/shard_map/reduce_scatter | solution.py:200
  1198.2 930.3 %reduce-scatter.15.cloned.1.call-start = ((), (), s32[]{:S(2)}) async-start(), calls=%async_computation.19 | async-start | bytes 18874368 | tf_op jit(solution)/shard_map/reduce_scatter | solution.py:200
  1239.5 319.1 %copy-start.1 = (bf16[2,2,128,2048]{3,2,1,0:T(8,128)(2,1)S(1)}, bf16[2,2,128,2048]{3,2,1,0:T(8,128)(2,1)}, u32[]{:S(2)}) copy-start(bf16[2,2,128,2048]{3,2,1,0:T(8,128)(2,1)} %param.30) | copy-start | bytes 6291460
  1239.5 319.1 %copy-start.56 = (f32[2048]{0:T(1024)S(1)}, f32[2048]{0:T(1024)}, u32[]{:S(2)}) copy-start(f32[2048]{0:T(1024)} %param.34) | copy-start | bytes 24580
  1239.5 319.1 %copy-start.58 = (f32[2,128]{1,0:T(2,128)S(1)}, f32[2,128]{1,0:T(2,128)}, u32[]{:S(2)}) copy-start(f32[2,128]{1,0:T(2,128)} %copy-done.57) | copy-start | bytes 3076
  1239.5 319.1 %copy-start.60 = (f32[2,128]{1,0:T(2,128)S(1)}, f32[2,128]{1,0:T(2,128)}, u32[]{:S(2)}) copy-start(f32[2,128]{1,0:T(2,128)} %copy-done.59) | copy-start | bytes 3076
  1242.9 318.3 %copy-start.68 = (f32[2,128]{1,0:T(2,128)S(1)}, f32[2,128]{1,0:T(2,128)}, u32[]{:S(2)}) copy-start(f32[2,128]{1,0:T(2,128)} %copy-done.67) | copy-start | bytes 3076
  1242.9 885.6 %copy-start.62 = (f32[2,128]{1,0:T(2,128)S(1)}, f32[2,128]{1,0:T(2,128)}, u32[]{:S(2)}) copy-start(f32[2,128]{1,0:T(2,128)} %copy-done.61) | copy-start | bytes 3076
  1242.9 885.6 %copy-start.64 = (f32[2,128]{1,0:T(2,128)S(1)}, f32[2,128]{1,0:T(2,128)}, u32[]{:S(2)}) copy-start(f32[2,128]{1,0:T(2,128)} %copy-done.63) | copy-start | bytes 3076
  1243.0 885.6 %copy-start.72 = (f32[2048]{0:T(1024)S(1)}, f32[2048]{0:T(1024)}, u32[]{:S(2)}) copy-start(f32[2048]{0:T(1024)} %param.43) | copy-start | bytes 24580
  1243.0 885.6 %copy-start.73 = (f32[2048]{0:T(1024)S(1)}, f32[2048]{0:T(1024)}, u32[]{:S(2)}) copy-start(f32[2048]{0:T(1024)} %param.39) | copy-start | bytes 24580
  1406.6 722.0 %copy-start.17 = (bf16[2,128,2048]{2,1,0:T(8,128)(2,1)S(1)}, bf16[2,128,2048]{2,1,0:T(8,128)(2,1)}, u32[]{:S(2)}) copy-start(bf16[2,128,2048]{2,1,0:T(8,128)(2,1)} %reduce-scatter.17.cloned.1.call-done) | copy-start | bytes 3145732
  (99 other events, 1094.9 us)
Sparse Core Ops, SparseCore 0:
  9.6 31.2 all-gather.12
  43.6 124.8 all-gather.20
  171.3 123.0 all-gather.10
  295.9 14.9 all-gather.14
  312.9 124.8 all-gather.24
  439.9 123.0 all-gather.22
  564.5 32.6 all-gather.18
  598.8 34.5 all-gather.16
  738.9 23.1 reduce-scatter.26
  779.6 23.2 reduce-scatter.24
  805.4 37.9 reduce-scatter.22
  986.3 36.4 reduce-scatter.20
  1070.1 42.8 reduce-scatter.28
  1115.5 44.5 reduce-scatter.30
  1162.4 44.5 reduce-scatter.34
  1209.6 44.7 reduce-scatter.32
  1257.8 148.7 reduce-scatter.16
  1410.5 147.9 reduce-scatter.18
  1562.3 280.9 reduce-scatter.12
  1847.4 281.1 reduce-scatter.14
where the time goes:
time: 2200 us; the launch traced here: 2190 us
  waiting for transfers between devices  1220 us (55%)
  matrix products  420 us (19%)
  local copies, waits for them, and re-layouts  374 us (17%)
  other arithmetic  104 us (5%)
  blocking collectives  47.5 us (2%)
    reduce_scatter x2, waiting for transfers between devices, body(): lax.psum_scatter(branch_terms.reshape(seq_count, full_len, model_width),...  567 us
    reduce_scatter x2, waiting for transfers between devices, body(): lax.psum_scatter(grad_normed.reshape(seq_count, full_len, model_width).as...  301 us
    all_gather x2, waiting for transfers between devices, body(): lax.all_gather(normed, 'tensor', axis=1, tiled=True)  218 us
    dynamic_update_slice x28, local copies, waits for them, and re-layouts, body(): lax.map(lambda inputs: attend_forward(*inputs), (queries, key_heads, valu...  173 us
    all_gather x2, waiting for transfers between devices, body(): lax.all_gather(cot_shard, 'tensor', axis=1, tiled=True)  106 us
  transfers between devices with their start and end apart: 20, of which 9 were waited for; matrix products, arithmetic and copies ran while one was open for 40% of the time, Pallas kernels for 0%

commit v1 on v0

v1 whole, which is shorter than its diff:
```python
from functools import partial

import jax
import jax.numpy as jnp
from jax import lax
from jax.experimental import pallas as pl
from jax.experimental.pallas import tpu as pltpu
from jax.sharding import Mesh
from jax.sharding import PartitionSpec as P

HEAD_DIM = 64
ROT = 32
LANES = 128
VMEM = 60 * 2**20

eps_norm = 1e-05
rope_base = 10000.0
masked_score = -1e30
f32 = jnp.float32
bf16 = jnp.bfloat16

NN = (((1,), (0,)), ((), ()))
NT = (((1,), (1,)), ((), ()))
TN = (((0,), (0,)), ((), ()))


def mm(a, b, dims=NN):
    return lax.dot_general(a, b, dims, preferred_element_type=f32)


def rope_tables(token_place):
    full_len = token_place.shape[0]
    half = ROT // 2
    inverse = rope_base ** (-(jnp.arange(half, dtype=f32) * (2.0 / ROT)))
    angles = token_place.astype(f32)[:, None] * inverse
    c, s = jnp.cos(angles), jnp.sin(angles)
    rest = (full_len, HEAD_DIM - ROT)
    zero_half = jnp.zeros((full_len, half), f32)
    cos = jnp.concatenate([c, c, jnp.ones(rest, f32)], 1)
    sa = jnp.concatenate([-s, zero_half, jnp.zeros(rest, f32)], 1)
    sb = jnp.concatenate([zero_half, s, jnp.zeros(rest, f32)], 1)
    return tuple(jnp.tile(t, (1, LANES // HEAD_DIM)) for t in (cos, sa, sb))


def attn_kernel(
    q_ref, k_ref, v_ref, qb_ref, kb_ref, vb_ref, cos_ref, sa_ref, sb_ref, ga_ref, segr_ref, segc_ref,
    out_ref, dp_ref, db_ref, dk_acc, dv_acc,
):
    full_len = q_ref.shape[0]
    size = min(256, full_len)
    half = ROT // 2
    heads = LANES // HEAD_DIM
    cos, sa, sb = cos_ref[...], sa_ref[...], sb_ref[...]

    def rope(x):
        return x * cos + pltpu.roll(x, LANES - half, 1) * sa + pltpu.roll(x, half, 1) * sb

    def unrope(g):
        return g * cos + pltpu.roll(g * sa, half, 1) + pltpu.roll(g * sb, LANES - half, 1)

    lane = lax.broadcasted_iota(jnp.int32, (1, LANES), 1)
    q = (rope(q_ref[...] + qb_ref[...]) * (HEAD_DIM**-0.5)).astype(bf16)
    k = rope(k_ref[...] + kb_ref[...]).astype(bf16)
    v = (v_ref[...] + vb_ref[...]).astype(bf16)
    do = ga_ref[...]
    k_t = k.astype(f32).T.astype(bf16)
    v_t = v.astype(f32).T.astype(bf16)
    do_t = do.astype(f32).T
    tri = lax.broadcasted_iota(jnp.int32, (size, size), 0) <= lax.broadcasted_iota(jnp.int32, (size, size), 1)
    zero = jnp.zeros((), bf16)
    dq_blocks = []
    for j in range(full_len // size):
        cols = slice(j * size, (j + 1) * size)
        seg_q = segr_ref[:, cols]
        out_rows, dq_rows, queries, grads = [], [], [], []
        low = [[None] * heads for _ in range(j + 1)]
        gs = [[None] * heads for _ in range(j + 1)]
        for h in range(heads):
            mine = (lane >= h * HEAD_DIM) & (lane < (h + 1) * HEAD_DIM)
            span = slice(h * HEAD_DIM, (h + 1) * HEAD_DIM)
            qh = jnp.where(mine, q[cols], zero)
            gh = jnp.where(mine, do[cols], zero)
            queries.append(qh)
            grads.append(gh)
            tiles, top, total, out, dq = [], None, None, None, None
            for i in range(j + 1):
                rows = slice(i * size, (i + 1) * size)
                ok = segc_ref[rows] == seg_q
                if i == j:
                    ok = ok & tri
                s = jnp.where(ok, mm(k[rows], qh, NT), masked_score)
                m = jnp.max(s, 0, keepdims=True)
                top = m if top is None else jnp.maximum(top, m)
                tiles.append(s)
            for i in range(j + 1):
                tiles[i] = jnp.exp(tiles[i] - top)
                t = jnp.sum(tiles[i], 0, keepdims=True)
                total = t if total is None else total + t
            inverse = 1.0 / total
            for i in range(j + 1):
                tiles[i] = tiles[i] * inverse
                low[i][h] = tiles[i].astype(bf16)
                t = mm(v_t[span, i * size : (i + 1) * size], low[i][h])
                out = t if out is None else out + t
            inner = jnp.sum(out * do_t[span, cols], 0, keepdims=True)
            for i in range(j + 1):
                dprob = mm(v[i * size : (i + 1) * size], gh, NT)
                gs[i][h] = (tiles[i] * (dprob - inner)).astype(bf16)
                t = mm(k_t[span, i * size : (i + 1) * size], gs[i][h])
                dq = t if dq is None else dq + t
            out_rows.append(out)
            dq_rows.append(dq)
        for i in range(j + 1):
            rows = slice(i * size, (i + 1) * size)
            dv = sum(mm(low[i][h], grads[h]) for h in range(heads))
            dk = sum(mm(gs[i][h], queries[h]) for h in range(heads))
            if i == j:
                dv_acc[rows] = dv
                dk_acc[rows] = dk
            else:
                dv_acc[rows] += dv
                dk_acc[rows] += dk
        out_ref[cols] = jnp.concatenate(out_rows, 0).T.astype(bf16)
        dq_blocks.append((jnp.concatenate(dq_rows, 0) * (HEAD_DIM**-0.5)).T)
    dq = unrope(jnp.concatenate(dq_blocks, 0)).astype(bf16)
    dk = unrope(dk_acc[...]).astype(bf16)
    dv = dv_acc[...].astype(bf16)
    for part, g in enumerate((dq, dk, dv)):
        dp_ref[part] = g
        db_ref[part : part + 1] = jnp.sum(g.astype(f32), 0, keepdims=True)


def attention(proj, bias, tables, grad_attn, segment):
    full_len, wide = proj.shape
    width = wide // 3
    pairs = width // LANES
    bias = bias.reshape(1, wide)

    def part(c):
        return pl.BlockSpec((full_len, LANES), lambda p: (0, c * pairs + p))

    def bias_part(c):
        return pl.BlockSpec((1, LANES), lambda p: (0, c * pairs + p))

    def whole(*shape):
        return pl.BlockSpec(shape, lambda p: (0, 0))

    table = whole(full_len, LANES)
    cols = pl.BlockSpec((full_len, LANES), lambda p: (0, p))
    return pl.pallas_call(
        attn_kernel,
        grid=(pairs,),
        in_specs=[part(0), part(1), part(2), bias_part(0), bias_part(1), bias_part(2), table, table, table, cols,
                  whole(1, full_len), whole(full_len, 1)],
        out_specs=[cols, pl.BlockSpec((3, full_len, LANES), lambda p: (0, 0, p)), pl.BlockSpec((8, LANES), lambda p: (0, p))],
        out_shape=[
            jax.ShapeDtypeStruct((full_len, width), bf16),
            jax.ShapeDtypeStruct((3, full_len, width), bf16),
            jax.ShapeDtypeStruct((8, width), f32),
        ],
        scratch_shapes=[pltpu.VMEM((full_len, LANES), f32), pltpu.VMEM((full_len, LANES), f32)],
        compiler_params=pltpu.CompilerParams(vmem_limit_bytes=VMEM),
        name="attention",
    )(proj, proj, proj, bias, bias, bias, *tables, grad_attn, segment.reshape(1, -1), segment.reshape(-1, 1))


def mlp_kernel(n_ref, c_ref, up_ref, down_ref, bias_ref, act_ref, pre_ref, sum_ref):
    rows = n_ref.shape[0]
    step = min(256, rows)
    k0 = 0.7978845608028654
    k1 = k0 * 0.044715
    total = None
    for i in range(rows // step):
        at = slice(i * step, (i + 1) * step)
        v = mm(n_ref[at], up_ref[...]) + bias_ref[...]
        g = mm(c_ref[at], down_ref[...], NT)
        v2 = v * v
        t = jnp.tanh(v * (k0 + k1 * v2))
        h = 0.5 * t + 0.5
        act_ref[at] = (v * h).astype(bf16)
        slope = h + v * (1.0 - t * t) * (0.5 * k0 + 1.5 * k1 * v2)
        p = (g * slope).astype(bf16)
        pre_ref[at] = p
        s = jnp.sum(p.astype(f32), 0, keepdims=True)
        total = s if total is None else total + s
    sum_ref[...] = jnp.broadcast_to(total, sum_ref.shape)


def mlp(n, c, up, down, bias):
    rows, depth = n.shape
    hidden = up.shape[1]
    br, bh = min(1024, rows), min(512, hidden)
    row = pl.BlockSpec((br, depth), lambda j, i: (i, 0))
    out = pl.BlockSpec((br, bh), lambda j, i: (i, j))
    act, pre, sums = pl.pallas_call(
        mlp_kernel,
        grid=(hidden // bh, rows // br),
        in_specs=[row, row, pl.BlockSpec((depth, bh), lambda j, i: (0, j)), pl.BlockSpec((bh, depth), lambda j, i: (j, 0)),
                  pl.BlockSpec((1, bh), lambda j, i: (0, j))],
        out_specs=[out, out, pl.BlockSpec((8, bh), lambda j, i: (i, j))],
        out_shape=[
            jax.ShapeDtypeStruct((rows, hidden), bf16),
            jax.ShapeDtypeStruct((rows, hidden), bf16),
            jax.ShapeDtypeStruct((rows // br * 8, hidden), f32),
        ],
        compiler_params=pltpu.CompilerParams(vmem_limit_bytes=VMEM),
        name="mlp",
    )(n, c, up, down, bias.reshape(1, hidden))
    return act, pre, jnp.sum(sums.reshape(-1, 8, hidden)[:, 0], 0)


def mixed_kernel(act_ref, attn_ref, down_ref, dense_ref, out_ref):
    rows = act_ref.shape[0]
    step = min(512, rows)
    for i in range(rows // step):
        at = slice(i * step, (i + 1) * step)
        out_ref[at] = (mm(act_ref[at], down_ref[...]) + mm(attn_ref[at], dense_ref[...])).astype(bf16)


def mixed_part(act, attn, down, dense):
    rows, hidden = act.shape
    width = attn.shape[1]
    depth = down.shape[1]
    br, bn = min(1024, rows), min(1024, depth)
    return pl.pallas_call(
        mixed_kernel,
        grid=(depth // bn, rows // br),
        in_specs=[pl.BlockSpec((br, hidden), lambda j, i: (i, 0)), pl.BlockSpec((br, width), lambda j, i: (i, 0)),
                  pl.BlockSpec((hidden, bn), lambda j, i: (0, j)), pl.BlockSpec((width, bn), lambda j, i: (0, j))],
        out_specs=pl.BlockSpec((br, bn), lambda j, i: (i, j)),
        out_shape=jax.ShapeDtypeStruct((rows, depth), bf16),
        compiler_params=pltpu.CompilerParams(vmem_limit_bytes=VMEM),
        name="mixed_part",
    )(act, attn, down, dense)


def back_kernel(pre_ref, dp_ref, up_ref, qkv_ref, out_ref):
    rows = pre_ref.shape[0]
    step = min(512, rows)
    for i in range(rows // step):
        at = slice(i * step, (i + 1) * step)
        total = mm(pre_ref[at], up_ref[...], NT)
        for c in range(3):
            total = total + mm(dp_ref[c, at], qkv_ref[c], NT)
        out_ref[at] = total.astype(bf16)


def back_part(pre, dp, up, qkv):
    rows, hidden = pre.shape
    width = dp.shape[2]
    depth = up.shape[0]
    br, bn = min(1024, rows), min(1024, depth)
    return pl.pallas_call(
        back_kernel,
        grid=(depth // bn, rows // br),
        in_specs=[pl.BlockSpec((br, hidden), lambda j, i: (i, 0)), pl.BlockSpec((3, br, width), lambda j, i: (0, i, 0)),
                  pl.BlockSpec((bn, hidden), lambda j, i: (j, 0)), pl.BlockSpec((3, bn, width), lambda j, i: (0, j, 0))],
        out_specs=pl.BlockSpec((br, bn), lambda j, i: (i, j)),
        out_shape=jax.ShapeDtypeStruct((rows, depth), bf16),
        compiler_params=pltpu.CompilerParams(vmem_limit_bytes=VMEM),
        name="back_part",
    )(pre, dp, up, qkv)


def weight_grad(x, y, split_rows, split_cols):
    rows, m = x.shape
    n = y.shape[1]
    bm, bn = m // split_rows, n // split_cols
    tile = min(bn, 512)

    def kernel(x_ref, y_ref, out_ref):
        out_ref[...] = mm(x_ref[...], y_ref[...], TN).astype(bf16).reshape(out_ref.shape)

    return pl.pallas_call(
        kernel,
        grid=(n // tile,),
        in_specs=[pl.BlockSpec((rows, m), lambda j: (0, 0), pipeline_mode=pl.Buffered(1)), pl.BlockSpec((rows, tile), lambda j: (0, j))],
        out_specs=pl.BlockSpec((split_rows, 1, bm, tile), lambda j: (0, j // (bn // tile), 0, j % (bn // tile))),
        out_shape=jax.ShapeDtypeStruct((split_rows, split_cols, bm, bn), bf16),
        compiler_params=pltpu.CompilerParams(vmem_limit_bytes=VMEM),
        name="weight_grad",
    )(x, y)


def body(
    tokens,
    cotangent,
    segments,
    positions,
    ln_gain,
    ln_bias,
    qkv_weight,
    qkv_bias,
    dense_weight,
    dense_bias,
    up_weight,
    up_bias,
    down_weight,
    down_bias,
):
    micros, seqs, shard, depth = tokens.shape
    full_len = segments.shape[2]
    parts, width = qkv_weight.shape[1:]
    hidden = up_weight.shape[1]
    quarter = qkv_weight.shape[0]
    quarters = depth // quarter
    fold = ("batch", "branch")
    mine = lax.axis_index("near")
    first = mine == 0
    swap = [(0, 1), (1, 0)]

    def to_group(a):
        got = lax.ppermute(jnp.where(first, a[1], a[0]), "near", swap)
        kept = jnp.where(first, a[0], a[1])
        return jnp.concatenate([jnp.where(first, kept, got), jnp.where(first, got, kept)], 1)

    def from_group(a):
        lo, hi = a[:, :shard], a[:, shard:]
        got = lax.ppermute(jnp.where(first, hi, lo), "near", swap)
        kept = jnp.where(first, lo, hi)
        return jnp.stack([jnp.where(first, kept, got), jnp.where(first, got, kept)], 0)

    cot_group = to_group(cotangent)
    residual = tokens.astype(f32)
    centered = residual - jnp.mean(residual, -1, keepdims=True)
    scale = lax.rsqrt(jnp.mean(centered * centered, -1, keepdims=True) + eps_norm)
    unit = centered * scale
    normed = (unit * ln_gain + ln_bias).astype(bf16)
    normed_group = to_group(normed)

    spread = ("near",) + fold
    qkv_all = lax.all_gather(qkv_weight.transpose(1, 0, 2), spread, axis=0, tiled=False)
    up_all = lax.all_gather(up_weight, spread, axis=0, tiled=False)
    down_all = lax.all_gather(down_weight, spread, axis=0, tiled=False)
    dense_all = lax.all_gather(dense_weight, spread, axis=0, tiled=False)
    qkv = qkv_all.reshape(2, quarters, parts, quarter, width).transpose(2, 1, 3, 0, 4).reshape(parts, depth, 2 * width)
    up = up_all.reshape(2, depth, hidden).transpose(1, 0, 2).reshape(depth, 2 * hidden)
    down = down_all.reshape(2, quarters, hidden, quarter).transpose(0, 2, 1, 3).reshape(2 * hidden, depth)
    dense = dense_all.reshape(2, quarters, width, quarter).transpose(0, 2, 1, 3).reshape(2 * width, depth)
    bias_qkv = lax.all_gather(qkv_bias, "near", axis=1, tiled=True)
    bias_up = lax.all_gather(up_bias, "near", axis=0, tiled=True)
    segment = jnp.where(first, segments[0], segments[1])
    place = jnp.where(first, positions[0], positions[1])

    rows_n, rows_c, acts, pres, attns, dps = [], [], [], [], [], []
    mixed_sums, back_sums = [], []
    sum_qkv, sum_up = 0.0, 0.0
    for s in range(seqs):
        n = lax.all_gather(normed_group[s], "line", axis=0, tiled=True)
        c = lax.all_gather(cot_group[s], "line", axis=0, tiled=True)
        proj = jnp.concatenate([mm(n, qkv[p]) for p in range(parts)], 1)
        grad_attn = mm(c, dense, NT).astype(bf16)
        attn, dp, db = attention(proj, bias_qkv, rope_tables(place[s]), grad_attn, segment[s])
        act, pre, up_sum = mlp(n, c, up, down, bias_up)
        mixed_sums.append(lax.psum_scatter(mixed_part(act, attn, down, dense), "line", scatter_dimension=0, tiled=True))
        back_sums.append(lax.psum_scatter(back_part(pre, dp, up, qkv), "line", scatter_dimension=0, tiled=True))
        sum_qkv = sum_qkv + db[:parts]
        sum_up = sum_up + up_sum
        rows_n.append(n)
        rows_c.append(c)
        acts.append(act)
        pres.append(pre)
        attns.append(attn)
        dps.append(dp)
    rows_n, rows_c, acts, pres, attns = (jnp.concatenate(a, 0) for a in (rows_n, rows_c, acts, pres, attns))
    dps = jnp.concatenate(dps, 1)

    def scatter(g):
        return lax.psum_scatter(g.reshape(2 * quarters, *g.shape[2:]), spread, scatter_dimension=0, tiled=False)

    grad_down = scatter(weight_grad(acts, rows_c, 2, quarters)).astype(f32)
    grad_up = weight_grad(rows_n, pres, quarters, 2)
    grad_up = scatter(grad_up.transpose(1, 0, 2, 3)).astype(f32)
    grad_dense = scatter(weight_grad(attns, rows_c, 2, quarters)).astype(f32)
    grad_qkv = jnp.stack([weight_grad(rows_n, dps[p], quarters, 1)[:, 0] for p in range(parts)], 1)
    grad_qkv = grad_qkv.reshape(quarters, parts, quarter, 2, width).transpose(3, 0, 1, 2, 4)
    grad_qkv = scatter(grad_qkv).transpose(1, 0, 2).astype(f32)

    summed = from_group(jnp.stack(mixed_sums, 0))
    mixed = (residual + summed.astype(f32) + dense_bias + down_bias).astype(bf16)
    grad_normed = from_group(jnp.stack(back_sums, 0)).astype(f32)
    w = grad_normed * ln_gain
    tokens_grad = cotangent.astype(f32) + scale * (
        w - jnp.mean(w, -1, keepdims=True) - unit * jnp.mean(w * unit, -1, keepdims=True)
    )
    everyone = fold + ("line", "near")
    gain_grad, shift_grad, out_bias_grad = lax.psum(
        (
            jnp.sum(grad_normed * unit, (0, 1, 2)),
            jnp.sum(grad_normed, (0, 1, 2)),
            jnp.sum(cotangent, (0, 1, 2), dtype=f32),
        ),
        everyone,
    )
    bias_sums = lax.psum((sum_qkv, sum_up), spread)
    qkv_bias_grad = lax.dynamic_slice_in_dim(bias_sums[0], mine * width, width, 1)
    up_bias_grad = lax.dynamic_slice_in_dim(bias_sums[1], mine * hidden, hidden, 0)
    return (
        mixed,
        tokens_grad,
        gain_grad,
        shift_grad,
        grad_qkv,
        qkv_bias_grad,
        grad_dense,
        out_bias_grad,
        grad_up,
        up_bias_grad,
        grad_down,
        out_bias_grad,
    )


def solution(mesh):
    batch, branch, tensor = (mesh.shape[a] for a in ("batch", "branch", "tensor"))
    inner = Mesh(mesh.devices.reshape(batch, branch, tensor // 2, 2), ("batch", "branch", "line", "near"))
    fold = ("batch", "branch")
    tensor = ("line", "near")
    rows = P(None, fold, tensor, None)
    first = P(fold, None, tensor)
    weights = (first, P(None, tensor), P(tensor, fold), P(), P(fold, tensor), P(tensor), P(tensor, fold), P())
    return jax.shard_map(
        body,
        mesh=inner,
        in_specs=(rows, rows, P(None, fold, None), P(None, fold, None), P(), P(), *weights),
        out_specs=(rows, rows, P(), P(), *weights),
        check_vma=False,
    )
```

time: 2200 us -> 1150 us (0.52)
  waiting for transfers between devices: 1220 us -> 507 us
  matrix products: 420 us -> 31 us
  Pallas kernels: 0 us -> 288 us
  local copies, waits for them, and re-layouts: 374 us -> 127 us
  blocking collectives: 47.5 us -> 94 us
  other arithmetic: 104 us -> 75.6 us
    reduce_scatter x12 -> x8, waiting for transfers between devices: 880 us -> 185 us  [the longest x2 110 us: body(): lax.psum_scatter(mixed_part(act, attn, down, dense), 'line', scatter_dime...]
    dot_general x80 -> x8, matrix products: 420 us -> 31 us  [mm(): return lax.dot_general(a, b, dims, preferred_element_type=f32)]
    pallas_call x0 -> x14, Pallas kernels: none -> 288 us  [the longest x6 87.4 us: weight_grad(): pl.pallas_call(kernel, grid=(n // tile,), in_specs=[pl.BlockSpec((rows, m...]
    dynamic_update_slice x28 -> x0, local copies, waits for them, and re-layouts: 173 us -> none  [body(): lax.map(lambda inputs: attend_forward(*inputs), (queries, key_heads, valu...]
    all_gather x8, waiting for transfers between devices: 340 us -> 248 us  [the longest x2 113 us: body(): c = lax.all_gather(cot_group[s], 'line', axis=0, tiled=True)]
    ppermute x0 -> x4, waiting for transfers between devices: none -> 69.7 us  [the longest x2 50.2 us: to_group(): got = lax.ppermute(jnp.where(first, a[1], a[0]), 'near', swap)]
    while x100 -> x0, local copies, waits for them, and re-layouts: 41 us -> none
    psum x2, blocking collectives: 47.5 us -> 85 us  [the longest x1 43.4 us: body(): bias_sums = lax.psum((sum_qkv, sum_up), spread)]
  transfers between devices with their start and end apart: 20 -> 20, of which waited for: 9 -> 13; matrix products, arithmetic and copies ran while one was open for 40% -> 20% of each run, Pallas kernels for 0% -> 25%
where the time goes in v1:
time: 1150 us
  waiting for transfers between devices  507 us (44%)
  Pallas kernels  288 us (25%)
  local copies, waits for them, and re-layouts  127 us (11%)
  blocking collectives  94 us (8%)
  other arithmetic  75.6 us (7%)
  matrix products  31 us (3%)
  between operations  14.8 us (1%)
    all_gather x2, waiting for transfers between devices, body(): c = lax.all_gather(cot_group[s], 'line', axis=0, tiled=True)  113 us
    reduce_scatter x2, waiting for transfers between devices, body(): lax.psum_scatter(mixed_part(act, attn, down, dense), 'line', scatter_dime...  110 us
    all_gather x2, waiting for transfers between devices, body(): n = lax.all_gather(normed_group[s], 'line', axis=0, tiled=True)  95 us
    pallas_call x6, Pallas kernels, weight_grad(): pl.pallas_call(kernel, grid=(n // tile,), in_specs=[pl.BlockSpec((rows, m...  87.4 us
    reduce_scatter x4, waiting for transfers between devices, scatter(): lax.psum_scatter(g.reshape(2 * quarters, *g.shape[2:]), spread, scatter_d...  74.6 us
    pallas_call x2, Pallas kernels, attention(): pl.pallas_call(attn_kernel, grid=(pairs,), in_specs=[part(0), part(1), pa...  69.8 us
    pallas_call x2, Pallas kernels, mlp(): pl.pallas_call(mlp_kernel, grid=(hidden // bh, rows // br), in_specs=[row...  53.4 us
    ppermute x2, waiting for transfers between devices, to_group(): got = lax.ppermute(jnp.where(first, a[1], a[0]), 'near', swap)  50.2 us
  transfers between devices with their start and end apart: 20, of which 13 were waited for; matrix products, arithmetic and copies ran while one was open for 20% of the time, Pallas kernels for 25%

profile of v1, /device:TPU:0, one launch (start us, length us, event | category | flops | bytes accessed | tf_op | source)
XLA Modules:
  0.0 1147.4 jit_solution(6176410032843758014)
XLA Ops:
  12.6 30.1 %collective-permute-done.1 = bf16[2,128,2048]{2,1,0:T(8,128)(2,1)S(1)} collective-permute-done((bf16[2,128,2048]{2,1,0:T(8,128)(2,1)S(1)}, bf16[2,128,2048]{2,1,0:T(8,128)(2,1)S(1)}, u32[]{:S(2)}, u32[]{:S(2)}) %collective-permute-start.1) | collective-permute-done | bytes 1048608 | tf_op jit(solution)/shard_map/ppermute | solution.py:313
  50.5 20.1 %collective-permute-done = bf16[2,128,2048]{2,1,0:T(8,128)(2,1)S(1)} collective-permute-done((bf16[2,128,2048]{2,1,0:T(8,128)(2,1)S(1)}, bf16[2,128,2048]{2,1,0:T(8,128)(2,1)S(1)}, u32[]{:S(2)}, u32[]{:S(2)}) %collective-permute-start) | collective-permute-done | bytes 1048608 | tf_op jit(solution)/shard_map/ppermute | solution.py:313
  93.5 36.7 %all-gather.31.cloned.1.call-done = bf16[1,1024,2048]{2,1,0:T(8,128)(2,1)} async-done(((bf16[1,256,2048]{2,1,0:T(8,128)(2,1)}), bf16[1,1024,2048]{2,1,0:T(8,128)(2,1)}) %all-gather.31.cloned.1.call-update) | async-done | bytes 4194320 | tf_op jit(solution)/shard_map/all_gather | solution.py:350
  135.7 76.0 %all-gather.19.cloned.1.call-done = bf16[1,1024,2048]{2,1,0:T(8,128)(2,1)} async-done(((bf16[1,256,2048]{2,1,0:T(8,128)(2,1)}), bf16[1,1024,2048]{2,1,0:T(8,128)(2,1)}) %all-gather.19.cloned.1.call-update) | async-done | bytes 4194320 | tf_op jit(solution)/shard_map/all_gather | solution.py:350
  226.3 31.1 %all-gather.25.cloned.1.call-done = bf16[24,512,256]{2,1,0:T(8,128)(2,1)} async-done(((bf16[3,512,256]{2,1,0:T(8,128)(2,1)}), bf16[24,512,256]{2,1,0:T(8,128)(2,1)}) %all-gather.25.cloned.1.call-update) | async-done | bytes 6291472 | tf_op jit(solution)/shard_map/all_gather | solution.py:332
  257.5 12.4 %copy.91 = bf16[2,4,3,512,256]{4,0,3,1,2:T(2,128)(2,1)S(1)} copy(bf16[2,4,3,512,256]{4,3,2,1,0:T(8,128)(2,1)} %bitcast.165) | data formatting | bytes 12582912 | tf_op jit(solution)/shard_map/reshape | solution.py:336
  278.6 61.7 %all-gather.17.cloned.1.call-done = bf16[1,1024,2048]{2,1,0:T(8,128)(2,1)} async-done(((bf16[1,256,2048]{2,1,0:T(8,128)(2,1)}), bf16[1,1024,2048]{2,1,0:T(8,128)(2,1)}) %all-gather.17.cloned.1.call-update) | async-done | bytes 4194320 | tf_op jit(solution)/shard_map/all_gather | solution.py:349
  353.5 34.8 %attention.2 = (bf16[1024,512]{1,0:T(8,128)(2,1)}, bf16[3,1024,512]{2,1,0:T(8,128)(2,1)}, f32[8,512]{1,0:T(8,128)}) custom-call(f32[1024,1536]{1,0:T(8,128)} %pad_maximum_fusion.4.q_ref.k_ref.v_ref, f32[1024,1536]{1,0:T(8,128)} %pad_maximum_fusion.4.q_ref.k_ref.v_ref, f32[1024,1536]{1,0:T(8,128)} %pad_maximum_fusion.4.q_ref.k_ref.v_ref, ...), custom_call_target="tpu_custom_call" | custom-call | tf_op jit(solution)/shard_map/attention/pallas_call | solution.py:150
  388.3 33.3 %all-gather.29.cloned.1.call-done = bf16[1,1024,2048]{2,1,0:T(8,128)(2,1)} async-done(((bf16[1,256,2048]{2,1,0:T(8,128)(2,1)}), bf16[1,1024,2048]{2,1,0:T(8,128)(2,1)}) %all-gather.29.cloned.1.call-update) | async-done | bytes 4194320 | tf_op jit(solution)/shard_map/all_gather | solution.py:349
  434.8 35.0 %attention.3 = (bf16[1024,512]{1,0:T(8,128)(2,1)}, bf16[3,1024,512]{2,1,0:T(8,128)(2,1)}, f32[8,512]{1,0:T(8,128)}) custom-call(f32[1024,1536]{1,0:T(8,128)} %pad_maximum_fusion.5.q_ref.k_ref.v_ref, f32[1024,1536]{1,0:T(8,128)} %pad_maximum_fusion.5.q_ref.k_ref.v_ref, f32[1024,1536]{1,0:T(8,128)} %pad_maximum_fusion.5.q_ref.k_ref.v_ref, ...), custom_call_target="tpu_custom_call" | custom-call | tf_op jit(solution)/shard_map/attention/pallas_call | solution.py:150
  485.8 11.2 reshape.193.qkv_ref
  497.1 16.4 %copy.57 = bf16[2,2048,1024]{2,0,1:T(2,128)(2,1)} copy(bf16[2,2048,1024]{2,1,0:T(8,128)(2,1)} %bitcast.158) | data formatting | bytes 16777216 | tf_op jit(solution)/shard_map/reshape | solution.py:337
  513.5 10.3 copy.83
  532.8 12.1 %copy.58 = bf16[2,4,1024,512]{3,1,2,0:T(4,128)(2,1)} copy(bf16[2,4,1024,512]{3,2,1,0:T(8,128)(2,1)} %bitcast.159) | data formatting | bytes 16777216 | tf_op jit(solution)/shard_map/reshape | solution.py:338
  545.0 10.7 copy.84
  555.7 26.8 %mlp.2 = (bf16[1024,2048]{1,0:T(8,128)(2,1)}, bf16[1024,2048]{1,0:T(8,128)(2,1)}, f32[8,2048]{1,0:T(8,128)}) custom-call(bf16[1024,2048]{1,0:T(8,128)(2,1)} %bitcast.154, bf16[1024,2048]{1,0:T(8,128)(2,1)} %bitcast.153, bf16[2048,2048]{1,0:T(8,128)(2,1)} %bitcast.133, bf16[2048,2048]{1,0:T(8,128)(2,1)} %bitcast.129, f32[1,2048]{1,0:T(1,128)} %bitcast.194), custom_call_target="tpu_custom_call" | custom-call | tf_op jit(solution)/shard_map/mlp/pallas_call | solution.py:195
  582.5 22.2 %back_part.2 = bf16[1024,2048]{1,0:T(8,128)(2,1)} custom-call(bf16[1024,2048]{1,0:T(8,128)(2,1)} %get-tuple-element.28.pre_ref, bf16[3,1024,512]{2,1,0:T(8,128)(2,1)} %get-tuple-element.29.dp_ref, bf16[2048,2048]{1,0:T(8,128)(2,1)} %bitcast.134, bf16[3,2048,512]{2,1,0:T(8,128)(2,1)} %reshape.193.qkv_ref), custom_call_target="tpu_custom_call" | custom-call | tf_op jit(solution)/shard_map/back_part/pallas_call | solution.py:253
  604.8 26.6 %mlp.3 = (bf16[1024,2048]{1,0:T(8,128)(2,1)}, bf16[1024,2048]{1,0:T(8,128)(2,1)}, f32[8,2048]{1,0:T(8,128)}) custom-call(bf16[1024,2048]{1,0:T(8,128)(2,1)} %bitcast.156, bf16[1024,2048]{1,0:T(8,128)(2,1)} %bitcast.151, bf16[2048,2048]{1,0:T(8,128)(2,1)} %bitcast.135, bf16[2048,2048]{1,0:T(8,128)(2,1)} %bitcast.130, f32[1,2048]{1,0:T(1,128)} %bitcast.195), custom_call_target="tpu_custom_call" | custom-call | tf_op jit(solution)/shard_map/mlp/pallas_call | solution.py:195
  631.3 22.2 %back_part.3 = bf16[1024,2048]{1,0:T(8,128)(2,1)} custom-call(bf16[1024,2048]{1,0:T(8,128)(2,1)} %get-tuple-element.30.pre_ref, bf16[3,1024,512]{2,1,0:T(8,128)(2,1)} %get-tuple-element.31.dp_ref, bf16[2048,2048]{1,0:T(8,128)(2,1)} %bitcast.136, bf16[3,2048,512]{2,1,0:T(8,128)(2,1)} %reshape.193.qkv_ref), custom_call_target="tpu_custom_call" | custom-call | tf_op jit(solution)/shard_map/back_part/pallas_call | solution.py:253
  667.7 10.0 weight_grad.8
  687.5 11.0 weight_grad.6
  720.5 16.6 %mixed_part.2 = bf16[1024,2048]{1,0:T(8,128)(2,1)} custom-call(bf16[1024,2048]{1,0:T(8,128)(2,1)} %get-tuple-element.24.act_ref, bf16[1024,512]{1,0:T(8,128)(2,1)} %get-tuple-element.25.attn_ref, bf16[2048,2048]{1,0:T(8,128)(2,1)} %bitcast.131, bf16[512,2048]{1,0:T(8,128)(2,1)} %bitcast.148), custom_call_target="tpu_custom_call" | custom-call | tf_op jit(solution)/shard_map/mixed_part/pallas_call | solution.py:225
  737.1 16.6 %mixed_part.3 = bf16[1024,2048]{1,0:T(8,128)(2,1)} custom-call(bf16[1024,2048]{1,0:T(8,128)(2,1)} %get-tuple-element.26.act_ref, bf16[1024,512]{1,0:T(8,128)(2,1)} %get-tuple-element.27.attn_ref, bf16[2048,2048]{1,0:T(8,128)(2,1)} %bitcast.132, bf16[512,2048]{1,0:T(8,128)(2,1)} %bitcast.149), custom_call_target="tpu_custom_call" | custom-call | tf_op jit(solution)/shard_map/mixed_part/pallas_call | solution.py:225
  754.0 11.6 %pad_maximum_fusion.2 = (bf16[2048,2048]{1,0:T(8,128)(2,1)}, bf16[2048,2048]{1,0:T(8,128)(2,1)}) fusion(bf16[1024,2048]{1,0:T(8,128)(2,1)} %get-tuple-element.30.pre_ref, bf16[1024,2048]{1,0:T(8,128)(2,1)} %get-tuple-element.28.pre_ref, bf16[1024,2048]{1,0:T(8,128)(2,1)} %get-tuple-element.26.act_ref, bf16[1024,2048]{1,0:T(8,128)(2,1)} %get-tuple-element.24.act_ref), kind=kLoop, calls=%fused_computation.2 | loop fusion | flops 33554432 | bytes 33554432 | tf_op jit(solution)/shard_map/concatenate | solution.py:365
  765.6 23.9 %weight_grad.10 = bf16[4,2,512,1024]{3,2,1,0:T(8,128)(2,1)} custom-call(bf16[2048,2048]{1,0:T(8,128)(2,1)} %pad_maximum_fusion.x_ref, bf16[2048,2048]{1,0:T(8,128)(2,1)} %get-tuple-element.89.y_ref), custom_call_target="tpu_custom_call" | custom-call | tf_op jit(solution)/shard_map/weight_grad/pallas_call | solution.py:274
  797.5 23.8 %weight_grad.11 = bf16[2,4,1024,512]{3,2,1,0:T(8,128)(2,1)} custom-call(bf16[2048,2048]{1,0:T(8,128)(2,1)} %get-tuple-element.90.x_ref, bf16[2048,2048]{1,0:T(8,128)(2,1)} %pad_maximum_fusion.1.y_ref), custom_call_target="tpu_custom_call" | custom-call | tf_op jit(solution)/shard_map/weight_grad/pallas_call | solution.py:274
  828.3 43.4 %all-reduce.1 = (f32[3,512]{1,0:T(4,128)S(1)}, f32[2048]{0:T(1024)S(1)}) all-reduce(f32[3,512]{1,0:T(4,128)S(1)} %slice_add_fusion.1, f32[2048]{0:T(1024)S(1)} %bitcast.196), channel_id=1, replica_groups=mesh['batch'=2,'branch'=2,'line'=4,'near'=2] {'near','batch','branch'}, use_global_device_ids=true, to_apply=%region_13.14 | all-reduce | flops 3584 | bytes 28672 | tf_op jit(solution)/shard_map/psum | solution.py:395
  875.4 30.8 %reduce-scatter.9.cloned.1.call-done = bf16[256,2048]{1,0:T(8,128)(2,1)} async-done(((bf16[1024,2048]{1,0:T(8,128)(2,1)}), bf16[256,2048]{1,0:T(8,128)(2,1)}) %reduce-scatter.9.cloned.1.call-update) | async-done | bytes 1048592 | tf_op jit(solution)/shard_map/reduce_scatter | solution.py:355
  906.2 79.5 %reduce-scatter.11.cloned.1.call-done = bf16[256,2048]{1,0:T(8,128)(2,1)} async-done(((bf16[1024,2048]{1,0:T(8,128)(2,1)}), bf16[256,2048]{1,0:T(8,128)(2,1)}) %reduce-scatter.11.cloned.1.call-update) | async-done | bytes 1048592 | tf_op jit(solution)/shard_map/reduce_scatter | solution.py:355
  993.2 19.5 %collective-permute-done.2 = bf16[2,128,2048]{2,1,0:T(8,128)(2,1)S(1)} collective-permute-done((bf16[2,128,2048]{2,1,0:T(8,128)(2,1)S(1)}, bf16[2,128,2048]{2,1,0:T(8,128)(2,1)S(1)}, u32[]{:S(2)}, u32[]{:S(2)}) %collective-permute-start.2) | collective-permute-done | bytes 1048608 | tf_op jit(solution)/shard_map/ppermute | solution.py:319
  1018.3 41.5 %all-reduce = (f32[2048]{0:T(1024)}, f32[2048]{0:T(1024)}, f32[2048]{0:T(1024)S(1)}) all-reduce(f32[2048]{0:T(1024)S(1)} %get-tuple-element.36, f32[2048]{0:T(1024)S(1)} %get-tuple-element.39, f32[2048]{0:T(1024)S(1)} %get-tuple-element.59), channel_id=1, replica_groups=mesh['batch'=2,'branch'=2,'line'=4,'near'=2] {'batch','branch','line','n..., use_global_device_ids=true, to_apply=%region_9.10 | all-reduce | flops 6144 | bytes 49152 | tf_op jit(solution)/shard_map/psum | solution.py:387
  1064.9 72.2 %reduce-scatter.23.cloned.1.call-done = bf16[1,1024,512]{2,1,0:T(8,128)(2,1)} async-done(((bf16[8,1024,512]{2,1,0:T(8,128)(2,1)}), bf16[1,1024,512]{2,1,0:T(8,128)(2,1)}) %reduce-scatter.23.cloned.1.call-update) | async-done | bytes 1048592 | tf_op jit(solution)/shard_map/reduce_scatter | solution.py:369
  (198 shorter events, 202.2 us)
Async XLA Ops:
  7.2 35.6 %copy-start.4 = (bf16[2,2,128,2048]{3,2,1,0:T(8,128)(2,1)S(1)}, bf16[2,2,128,2048]{3,2,1,0:T(8,128)(2,1)}, u32[]{:S(2)}) copy-start(bf16[2,2,128,2048]{3,2,1,0:T(8,128)(2,1)} %param.15) | copy-start | bytes 6291460
  7.2 82.5 %all-gather.27.cloned.1.call-start = ((), (), s32[]{:S(2)}) async-start(), calls=%async_computation.21 | async-start | bytes 2359296 | tf_op jit(solution)/shard_map/all_gather | solution.py:335
  7.9 122.3 %all-gather.31.cloned.1.call-start = ((), (), s32[]{:S(2)}) async-start(), calls=%async_computation.23 | async-start | bytes 5242880 | tf_op jit(solution)/shard_map/all_gather | solution.py:350
  9.6 33.1 %collective-permute-start.1 = (bf16[2,128,2048]{2,1,0:T(8,128)(2,1)S(1)}, bf16[2,128,2048]{2,1,0:T(8,128)(2,1)S(1)}, u32[]{:S(2)}, u32[]{:S(2)}) collective-permute-start(bf16[2,128,2048]{2,1,0:T(8,128)(2,1)S(1)} %select_bitcast_fusion.4), channel_id=1, source_target_pairs={{0,1},{1,0},{2,3},{3,2},{4,5},{5,4},{6,7},{7,6},{8,9},{9,8},{10,11... | collective-permute-start | bytes 3145736 | tf_op jit(solution)/shard_map/ppermute | solution.py:313
  44.5 167.2 %all-gather.19.cloned.1.call-start = ((), (), s32[]{:S(2)}) async-start(), calls=%async_computation.17 | async-start | bytes 5242880 | tf_op jit(solution)/shard_map/all_gather | solution.py:350
  45.2 212.3 %all-gather.25.cloned.1.call-start = ((), (), s32[]{:S(2)}) async-start(), calls=%async_computation.20 | async-start | bytes 7077888 | tf_op jit(solution)/shard_map/all_gather | solution.py:332
  45.8 294.5 %all-gather.17.cloned.1.call-start = ((), (), s32[]{:S(2)}) async-start(), calls=%async_computation.16 | async-start | bytes 5242880 | tf_op jit(solution)/shard_map/all_gather | solution.py:349
  47.9 22.6 %collective-permute-start = (bf16[2,128,2048]{2,1,0:T(8,128)(2,1)S(1)}, bf16[2,128,2048]{2,1,0:T(8,128)(2,1)S(1)}, u32[]{:S(2)}, u32[]{:S(2)}) collective-permute-start(bf16[2,128,2048]{2,1,0:T(8,128)(2,1)S(1)} %select_bitcast_fusion.5), channel_id=1, source_target_pairs={{0,1},{1,0},{2,3},{3,2},{4,5},{5,4},{6,7},{7,6},{8,9},{9,8},{10,11... | collective-permute-start | bytes 3145736 | tf_op jit(solution)/shard_map/ppermute | solution.py:313
  72.2 349.4 %all-gather.29.cloned.1.call-start = ((), (), s32[]{:S(2)}) async-start(), calls=%async_computation.22 | async-start | bytes 5242880 | tf_op jit(solution)/shard_map/all_gather | solution.py:349
  72.8 424.3 %all-gather.21.cloned.1.call-start = ((), (), s32[]{:S(2)}) async-start(), calls=%async_computation.18 | async-start | bytes 9437184 | tf_op jit(solution)/shard_map/all_gather | solution.py:333
  73.6 459.3 %all-gather.23.cloned.1.call-start = ((), (), s32[]{:S(2)}) async-start(), calls=%async_computation.19 | async-start | bytes 9437184 | tf_op jit(solution)/shard_map/all_gather | solution.py:334
  74.3 747.7 %reduce-scatter.19.cloned.1.call-start = ((), (), s32[]{:S(2)}) async-start(), calls=%async_computation.13 | async-start | bytes 2359296 | tf_op jit(solution)/shard_map/reduce_scatter | solution.py:369
  93.5 118.2 %copy-start.3 = (bf16[64,8,4,512]{3,1,2,0:T(8,128)(2,1)}, bf16[64,8,4,512]{3,1,2,0:T(8,128)(2,1)S(1)}, u32[]{:S(2)}) copy-start(bf16[64,8,4,512]{3,1,2,0:T(8,128)(2,1)S(1)} %copy.89) | copy-start | bytes 6291460
  434.8 35.0 %copy-start.11 = (bf16[1024,512]{1,0:T(8,128)(2,1)S(1)}, bf16[1024,512]{1,0:T(8,128)(2,1)}, u32[]{:S(2)}) copy-start(bf16[1024,512]{1,0:T(8,128)(2,1)} %get-tuple-element.25.attn_ref) | copy-start | bytes 3145732
  481.3 342.5 %reduce-scatter.13.cloned.1.call-start = ((), (), s32[]{:S(2)}) async-start(), calls=%async_computation.10 | async-start | bytes 5242880 | tf_op jit(solution)/shard_map/reduce_scatter | solution.py:356
  604.7 219.1 %reduce-scatter.15.cloned.1.call-start = ((), (), s32[]{:S(2)}) async-start(), calls=%async_computation.11 | async-start | bytes 5242880 | tf_op jit(solution)/shard_map/reduce_scatter | solution.py:356
  653.5 219.4 %reduce-scatter.17.cloned.1.call-start = ((), (), s32[]{:S(2)}) async-start(), calls=%async_computation.12 | async-start | bytes 7077888 | tf_op jit(solution)/shard_map/reduce_scatter | solution.py:369
  687.5 11.0 copy-start.10
  720.5 185.7 %reduce-scatter.9.cloned.1.call-start = ((), (), s32[]{:S(2)}) async-start(), calls=%async_computation.8 | async-start | bytes 5242880 | tf_op jit(solution)/shard_map/reduce_scatter | solution.py:355
  737.1 248.6 %reduce-scatter.11.cloned.1.call-start = ((), (), s32[]{:S(2)}) async-start(), calls=%async_computation.9 | async-start | bytes 5242880 | tf_op jit(solution)/shard_map/reduce_scatter | solution.py:355
  753.7 308.4 %reduce-scatter.21.cloned.1.call-start = ((), (), s32[]{:S(2)}) async-start(), calls=%async_computation.14 | async-start | bytes 9437184 | tf_op jit(solution)/shard_map/reduce_scatter | solution.py:369
  797.4 339.8 %reduce-scatter.23.cloned.1.call-start = ((), (), s32[]{:S(2)}) async-start(), calls=%async_computation.15 | async-start | bytes 9437184 | tf_op jit(solution)/shard_map/reduce_scatter | solution.py:369
  825.8 163.5 %copy-start.12 = (bf16[256,2048]{1,0:T(8,128)(2,1)S(1)}, bf16[256,2048]{1,0:T(8,128)(2,1)}, u32[]{:S(2)}) copy-start(bf16[256,2048]{1,0:T(8,128)(2,1)} %reduce-scatter.13.cloned.1.call-done) | copy-start | bytes 3145732
  825.8 163.4 %copy-start.13 = (bf16[256,2048]{1,0:T(8,128)(2,1)S(1)}, bf16[256,2048]{1,0:T(8,128)(2,1)}, u32[]{:S(2)}) copy-start(bf16[256,2048]{1,0:T(8,128)(2,1)} %reduce-scatter.15.cloned.1.call-done) | copy-start | bytes 3145732
  825.8 163.4 %collective-permute-start.3 = (bf16[2,128,2048]{2,1,0:T(8,128)(2,1)S(1)}, bf16[2,128,2048]{2,1,0:T(8,128)(2,1)}, u32[]{:S(2)}, u32[]{:S(2)}) collective-permute-start(bf16[2,128,2048]{2,1,0:T(8,128)(2,1)S(1)} %broadcast_select_fusion.2), channel_id=1, source_target_pairs={{0,1},{1,0},{2,3},{3,2},{4,5},{5,4},{6,7},{7,6},{8,9},{9,8},{10,11... | collective-permute-start | bytes 3145736 | tf_op jit(solution)/shard_map/ppermute | solution.py:319
  987.7 25.0 %collective-permute-start.2 = (bf16[2,128,2048]{2,1,0:T(8,128)(2,1)S(1)}, bf16[2,128,2048]{2,1,0:T(8,128)(2,1)S(1)}, u32[]{:S(2)}, u32[]{:S(2)}) collective-permute-start(bf16[2,128,2048]{2,1,0:T(8,128)(2,1)S(1)} %broadcast_select_fusion.4), channel_id=1, source_target_pairs={{0,1},{1,0},{2,3},{3,2},{4,5},{5,4},{6,7},{7,6},{8,9},{9,8},{10,11... | collective-permute-start | bytes 3145736 | tf_op jit(solution)/shard_map/ppermute | solution.py:319
  991.0 21.7 %copy-start.14 = (bf16[256,2048]{1,0:T(8,128)(2,1)S(1)}, bf16[256,2048]{1,0:T(8,128)(2,1)}, u32[]{:S(2)}) copy-start(bf16[256,2048]{1,0:T(8,128)(2,1)} %reduce-scatter.9.cloned.1.call-done) | copy-start | bytes 3145732
  991.0 21.7 %copy-start.15 = (bf16[256,2048]{1,0:T(8,128)(2,1)S(1)}, bf16[256,2048]{1,0:T(8,128)(2,1)}, u32[]{:S(2)}) copy-start(bf16[256,2048]{1,0:T(8,128)(2,1)} %reduce-scatter.11.cloned.1.call-done) | copy-start | bytes 3145732
  993.1 20.3 %copy-start.5 = (bf16[2,2,128,2048]{3,2,1,0:T(8,128)(2,1)S(1)}, bf16[2,2,128,2048]{3,2,1,0:T(8,128)(2,1)}, u32[]{:S(2)}) copy-start(bf16[2,2,128,2048]{3,2,1,0:T(8,128)(2,1)} %param.15) | copy-start | bytes 6291460
  993.1 20.3 %copy-start.27 = (f32[2048]{0:T(1024)S(1)}, f32[2048]{0:T(1024)}, u32[]{:S(2)}) copy-start(f32[2048]{0:T(1024)} %param.27) | copy-start | bytes 24580
  993.1 20.3 %copy-start.28 = (f32[2048]{0:T(1024)S(1)}, f32[2048]{0:T(1024)}, u32[]{:S(2)}) copy-start(f32[2048]{0:T(1024)} %param.23) | copy-start | bytes 24580
  1059.8 80.2 %copy-start.29 = (f32[2048]{0:T(1024)}, f32[2048]{0:T(1024)S(1)}, u32[]{:S(2)}) copy-start(f32[2048]{0:T(1024)S(1)} %get-tuple-element.114) | copy-start | bytes 24580
  (22 other events, 82.3 us)
Sparse Core Ops, SparseCore 0:
  9.9 35.7 all-gather.26
  47.9 82.2 all-gather.30
  132.3 79.2 all-gather.18
  213.4 44.0 all-gather.24
  259.5 80.7 all-gather.16
  342.3 79.2 all-gather.28
  423.5 52.9 all-gather.20
  478.3 54.4 all-gather.22
  536.1 41.2 reduce-scatter.18
  604.8 76.7 reduce-scatter.12
  683.9 77.2 reduce-scatter.14
  764.8 62.2 reduce-scatter.16
  829.4 76.7 reduce-scatter.8
  908.4 77.2 reduce-scatter.10
  989.0 73.0 reduce-scatter.20
  1065.9 71.2 reduce-scatter.22

commit v2 on v1

v2 whole, which is shorter than its diff:
```python
from functools import partial

import jax
import jax.numpy as jnp
from jax import lax
from jax.experimental import pallas as pl
from jax.experimental.pallas import tpu as pltpu
from jax.sharding import Mesh
from jax.sharding import PartitionSpec as P

HEAD_DIM = 64
ROT = 32
LANES = 128
VMEM = 60 * 2**20
COST = {"attention": 100, "attention_grad": 23, "mlp_act": 17, "mlp_pre": 14, "mixed_part": 16, "back_part": 22, "weight_grad": 100,
        "heads_grad": 28, "project": 9, "line_step": 3, "assemble": 8, "assemble_heads": 14}


def cost(units):
    return pl.CostEstimate(flops=units * 250000000 + 1, bytes_accessed=units * 250000 + 1, transcendentals=0)


eps_norm = 1e-05
rope_base = 10000.0
masked_score = -1e30
f32 = jnp.float32
bf16 = jnp.bfloat16

NN = (((1,), (0,)), ((), ()))
NT = (((1,), (1,)), ((), ()))
TN = (((0,), (0,)), ((), ()))


def mm(a, b, dims=NN):
    return lax.dot_general(a, b, dims, preferred_element_type=f32)


def call(kernel, deps, args, *, grid, in_specs, out_specs, out_shape, name, scratch=(), prefetch=0):
    deps = list(deps)
    inputs = prefetch + len(in_specs)

    def run(*refs):
        kernel(*refs[:inputs], *refs[inputs + len(deps) :])

    spec = pltpu.PrefetchScalarGridSpec(
        num_scalar_prefetch=prefetch,
        grid=grid,
        in_specs=list(in_specs) + [pl.BlockSpec(memory_space=pl.ANY)] * len(deps),
        out_specs=out_specs,
        scratch_shapes=list(scratch),
    )
    return pl.pallas_call(
        run,
        grid_spec=spec,
        out_shape=out_shape,
        compiler_params=pltpu.CompilerParams(vmem_limit_bytes=VMEM),
        cost_estimate=cost(COST[name]),
        name=name,
    )(*args, *deps)


def tie(a, *deps, units=0):
    return pl.pallas_call(
        lambda *refs: None,
        in_specs=[pl.BlockSpec(memory_space=pl.ANY)] * (1 + len(deps)),
        out_specs=pl.BlockSpec(memory_space=pl.ANY),
        out_shape=jax.ShapeDtypeStruct(a.shape, a.dtype),
        input_output_aliases={0: 0},
        cost_estimate=cost(units),
        name="tie",
    )(a, *deps)


def project_kernel(a_ref, w_ref, out_ref):
    rows = a_ref.shape[0]
    step = min(512, rows)
    for i in range(rows // step):
        at = slice(i * step, (i + 1) * step)
        out_ref[at] = mm(a_ref[at], w_ref[...]).astype(out_ref.dtype)


def project(a, w, dtype, deps=()):
    rows, depth = a.shape
    cols = w.shape[1]
    bn = 256 if cols % 256 == 0 else 128
    return call(
        project_kernel,
        deps,
        (a, w),
        grid=(cols // bn,),
        in_specs=[pl.BlockSpec((rows, depth), lambda j: (0, 0)), pl.BlockSpec((depth, bn), lambda j: (0, j))],
        out_specs=pl.BlockSpec((rows, bn), lambda j: (0, j)),
        out_shape=jax.ShapeDtypeStruct((rows, cols), dtype),
        name="project",
    )


def rope_tables(token_place):
    full_len = token_place.shape[0]
    half = ROT // 2
    inverse = rope_base ** (-(jnp.arange(half, dtype=f32) * (2.0 / ROT)))
    angles = token_place.astype(f32)[:, None] * inverse
    c, s = jnp.cos(angles), jnp.sin(angles)
    rest = (full_len, HEAD_DIM - ROT)
    zero_half = jnp.zeros((full_len, half), f32)
    cos = jnp.concatenate([c, c, jnp.ones(rest, f32)], 1)
    sa = jnp.concatenate([-s, zero_half, jnp.zeros(rest, f32)], 1)
    sb = jnp.concatenate([zero_half, s, jnp.zeros(rest, f32)], 1)
    return tuple(jnp.tile(t, (1, LANES // HEAD_DIM)) for t in (cos, sa, sb))


def attn_kernel(
    q_ref, k_ref, v_ref, qb_ref, kb_ref, vb_ref, cos_ref, sa_ref, sb_ref, segr_ref, segc_ref, out_ref, keep_ref, log_ref
):
    full_len = q_ref.shape[0]
    size = min(256, full_len)
    half = ROT // 2
    heads = LANES // HEAD_DIM
    cos, sa, sb = cos_ref[...], sa_ref[...], sb_ref[...]

    def rope(x):
        return x * cos + pltpu.roll(x, LANES - half, 1) * sa + pltpu.roll(x, half, 1) * sb

    lane = lax.broadcasted_iota(jnp.int32, (1, LANES), 1)
    q = (rope(q_ref[...] + qb_ref[...]) * (HEAD_DIM**-0.5)).astype(bf16)
    k = rope(k_ref[...] + kb_ref[...]).astype(bf16)
    v = (v_ref[...] + vb_ref[...]).astype(bf16)
    keep_ref[0] = q
    keep_ref[1] = k
    keep_ref[2] = v
    v_t = v.astype(f32).T.astype(bf16)
    tri = lax.broadcasted_iota(jnp.int32, (size, size), 0) <= lax.broadcasted_iota(jnp.int32, (size, size), 1)
    zero = jnp.zeros((), bf16)
    for j in range(full_len // size):
        cols = slice(j * size, (j + 1) * size)
        seg_q = segr_ref[:, cols]
        out_rows = []
        for h in range(heads):
            mine = (lane >= h * HEAD_DIM) & (lane < (h + 1) * HEAD_DIM)
            span = slice(h * HEAD_DIM, (h + 1) * HEAD_DIM)
            qh = jnp.where(mine, q[cols], zero)
            tiles, top, total, out = [], None, None, None
            for i in range(j + 1):
                rows = slice(i * size, (i + 1) * size)
                ok = segc_ref[rows] == seg_q
                if i == j:
                    ok = ok & tri
                s = jnp.where(ok, mm(k[rows], qh, NT), masked_score)
                m = jnp.max(s, 0, keepdims=True)
                top = m if top is None else jnp.maximum(top, m)
                tiles.append(s)
            for i in range(j + 1):
                e = jnp.exp(tiles[i] - top)
                t = jnp.sum(e, 0, keepdims=True)
                total = t if total is None else total + t
                t = mm(v_t[span, i * size : (i + 1) * size], e.astype(bf16))
                out = t if out is None else out + t
            out_rows.append(out * (1.0 / total))
            log_ref[h : h + 1, cols] = top + jnp.log(total)
        out_ref[cols] = jnp.concatenate(out_rows, 0).T.astype(bf16)


def attention(proj, bias, tables, segment, deps=()):
    full_len, wide = proj.shape
    width = wide // 3
    pairs = width // LANES
    bias = bias.reshape(1, wide)

    def part(c):
        return pl.BlockSpec((full_len, LANES), lambda p: (0, c * pairs + p))

    def bias_part(c):
        return pl.BlockSpec((1, LANES), lambda p: (0, c * pairs + p))

    def whole(*shape):
        return pl.BlockSpec(shape, lambda p: (0, 0))

    table = whole(full_len, LANES)
    return call(
        attn_kernel,
        deps,
        (proj, proj, proj, bias, bias, bias, *tables, segment.reshape(1, -1), segment.reshape(-1, 1)),
        grid=(pairs,),
        in_specs=[part(0), part(1), part(2), bias_part(0), bias_part(1), bias_part(2), table, table, table,
                  whole(1, full_len), whole(full_len, 1)],
        out_specs=[
            pl.BlockSpec((full_len, LANES), lambda p: (0, p)),
            pl.BlockSpec((3, full_len, LANES), lambda p: (0, 0, p)),
            pl.BlockSpec((8, full_len), lambda p: (p, 0)),
        ],
        out_shape=[
            jax.ShapeDtypeStruct((full_len, width), bf16),
            jax.ShapeDtypeStruct((3, full_len, width), bf16),
            jax.ShapeDtypeStruct((8 * pairs, full_len), f32),
        ],
        name="attention",
    )


def attn_grad_kernel(
    keep_ref, log_ref, ao_ref, ga_ref, cos_ref, sa_ref, sb_ref, segr_ref, segc_ref, dp_ref, db_ref, dk_acc, dv_acc
):
    full_len = ao_ref.shape[0]
    size = min(256, full_len)
    half = ROT // 2
    heads = LANES // HEAD_DIM
    cos, sa, sb = cos_ref[...], sa_ref[...], sb_ref[...]

    def unrope(g):
        return g * cos + pltpu.roll(g * sa, half, 1) + pltpu.roll(g * sb, LANES - half, 1)

    lane = lax.broadcasted_iota(jnp.int32, (1, LANES), 1)
    q, k, v, do = keep_ref[0], keep_ref[1], keep_ref[2], ga_ref[...]
    k_t = k.astype(f32).T.astype(bf16)
    inner_t = (do.astype(f32) * ao_ref[...].astype(f32)).T
    tri = lax.broadcasted_iota(jnp.int32, (size, size), 0) <= lax.broadcasted_iota(jnp.int32, (size, size), 1)
    zero = jnp.zeros((), bf16)
    dq_blocks = []
    for j in range(full_len // size):
        cols = slice(j * size, (j + 1) * size)
        seg_q = segr_ref[:, cols]
        spans, masks, queries, grads, logs, inners = [], [], [], [], [], []
        for h in range(heads):
            mine = (lane >= h * HEAD_DIM) & (lane < (h + 1) * HEAD_DIM)
            spans.append(slice(h * HEAD_DIM, (h + 1) * HEAD_DIM))
            queries.append(jnp.where(mine, q[cols], zero))
            grads.append(jnp.where(mine, do[cols], zero))
            logs.append(log_ref[h : h + 1, cols])
            inners.append(jnp.sum(inner_t[spans[h], cols], 0, keepdims=True))
        dq = [None] * heads
        for i in range(j + 1):
            rows = slice(i * size, (i + 1) * size)
            ok = segc_ref[rows] == seg_q
            if i == j:
                ok = ok & tri
            dv = dk = None
            for h in range(heads):
                p = jnp.exp(jnp.where(ok, mm(k[rows], queries[h], NT) - logs[h], masked_score))
                g = (p * (mm(v[rows], grads[h], NT) - inners[h])).astype(bf16)
                t = mm(p.astype(bf16), grads[h])
                dv = t if dv is None else dv + t
                t = mm(g, queries[h])
                dk = t if dk is None else dk + t
                t = mm(k_t[spans[h], rows], g)
                dq[h] = t if dq[h] is None else dq[h] + t
            if i == j:
                dv_acc[rows] = dv
                dk_acc[rows] = dk
            else:
                dv_acc[rows] += dv
                dk_acc[rows] += dk
        dq_blocks.append((jnp.concatenate(dq, 0) * (HEAD_DIM**-0.5)).T)
    dq = unrope(jnp.concatenate(dq_blocks, 0)).astype(bf16)
    dk = unrope(dk_acc[...]).astype(bf16)
    dv = dv_acc[...].astype(bf16)
    for part, g in enumerate((dq, dk, dv)):
        dp_ref[part] = g
        db_ref[part : part + 1] = jnp.sum(g.astype(f32), 0, keepdims=True)


def attention_grad(keep, logs, attn, grad_attn, tables, segment, deps=()):
    _, full_len, width = keep.shape

    def whole(*shape):
        return pl.BlockSpec(shape, lambda p: (0, 0))

    table = whole(full_len, LANES)
    cols = pl.BlockSpec((full_len, LANES), lambda p: (0, p))
    three = pl.BlockSpec((3, full_len, LANES), lambda p: (0, 0, p))
    return call(
        attn_grad_kernel,
        deps,
        (keep, logs, attn, grad_attn, *tables, segment.reshape(1, -1), segment.reshape(-1, 1)),
        grid=(width // LANES,),
        in_specs=[three, pl.BlockSpec((8, full_len), lambda p: (p, 0)), cols, cols, table, table, table,
                  whole(1, full_len), whole(full_len, 1)],
        out_specs=[three, pl.BlockSpec((8, LANES), lambda p: (0, p))],
        out_shape=[jax.ShapeDtypeStruct((3, full_len, width), bf16), jax.ShapeDtypeStruct((8, width), f32)],
        scratch=[pltpu.VMEM((full_len, LANES), f32), pltpu.VMEM((full_len, LANES), f32)],
        name="attention_grad",
    )


def act_kernel(n_ref, up_ref, bias_ref, act_ref, slope_ref):
    rows = n_ref.shape[0]
    step = min(256, rows)
    k0 = 0.7978845608028654
    k1 = k0 * 0.044715
    for i in range(rows // step):
        at = slice(i * step, (i + 1) * step)
        v = mm(n_ref[at], up_ref[...]) + bias_ref[...]
        v2 = v * v
        t = jnp.tanh(v * (k0 + k1 * v2))
        h = 0.5 * t + 0.5
        act_ref[at] = (v * h).astype(bf16)
        slope_ref[at] = (h + v * (1.0 - t * t) * (0.5 * k0 + 1.5 * k1 * v2)).astype(bf16)


def mlp_act(n, up, bias, deps=()):
    rows, depth = n.shape
    near, _, hidden = up.shape
    br, bh = min(1024, rows), min(512, hidden)
    per = hidden // bh
    out = pl.BlockSpec((br, bh), lambda j, i: (i, j))
    shape = jax.ShapeDtypeStruct((rows, near * hidden), bf16)
    return call(
        act_kernel,
        deps,
        (n, up, bias.reshape(1, -1)),
        grid=(near * per, rows // br),
        in_specs=[pl.BlockSpec((br, depth), lambda j, i: (i, 0)),
                  pl.BlockSpec((None, depth, bh), lambda j, i: (j // per, 0, j % per)),
                  pl.BlockSpec((1, bh), lambda j, i: (0, j))],
        out_specs=[out, out],
        out_shape=[shape, shape],
        name="mlp_act",
    )


def pre_kernel(c_ref, down_ref, slope_ref, pre_ref, sum_ref):
    rows = c_ref.shape[0]
    step = min(256, rows)
    total = None
    for i in range(rows // step):
        at = slice(i * step, (i + 1) * step)
        p = (mm(c_ref[at], down_ref[...]) * slope_ref[at].astype(f32)).astype(bf16)
        pre_ref[at] = p
        s = jnp.sum(p.astype(f32), 0, keepdims=True)
        total = s if total is None else total + s
    sum_ref[...] = jnp.broadcast_to(total, sum_ref.shape)


def mlp_pre(c, down_t, slope, deps=()):
    rows, depth = c.shape
    near, _, hidden = down_t.shape
    br, bh = min(1024, rows), min(512, hidden)
    per = hidden // bh
    out = pl.BlockSpec((br, bh), lambda j, i: (i, j))
    pre, sums = call(
        pre_kernel,
        deps,
        (c, down_t, slope),
        grid=(near * per, rows // br),
        in_specs=[pl.BlockSpec((br, depth), lambda j, i: (i, 0)),
                  pl.BlockSpec((None, depth, bh), lambda j, i: (j // per, 0, j % per)), out],
        out_specs=[out, pl.BlockSpec((8, bh), lambda j, i: (i, j))],
        out_shape=[
            jax.ShapeDtypeStruct((rows, near * hidden), bf16),
            jax.ShapeDtypeStruct((rows // br * 8, near * hidden), f32),
        ],
        name="mlp_pre",
    )
    return pre, jnp.sum(sums.reshape(-1, 8, near * hidden)[:, 0], 0)


def mixed_kernel(act_ref, attn_ref, down_ref, dense_ref, out_ref):
    rows = act_ref.shape[0]
    near, _, hidden = down_ref.shape
    step = min(512, rows)
    for i in range(rows // step):
        at = slice(i * step, (i + 1) * step)
        total = mm(attn_ref[at], dense_ref[...], NT)
        for r in range(near):
            total = total + mm(act_ref[at, r * hidden : (r + 1) * hidden], down_ref[r], NT)
        out_ref[at] = total.astype(bf16)


def mixed_part(act, attn, down_t, dense_t, deps=()):
    rows = act.shape[0]
    width = attn.shape[1]
    near, depth, hidden = down_t.shape
    br, bn = min(1024, rows), min(512, depth)
    return call(
        mixed_kernel,
        deps,
        (act, attn, down_t, dense_t),
        grid=(depth // bn, rows // br),
        in_specs=[pl.BlockSpec((br, near * hidden), lambda j, i: (i, 0)), pl.BlockSpec((br, width), lambda j, i: (i, 0)),
                  pl.BlockSpec((near, bn, hidden), lambda j, i: (0, j, 0)), pl.BlockSpec((bn, width), lambda j, i: (j, 0))],
        out_specs=pl.BlockSpec((br, bn), lambda j, i: (i, j)),
        out_shape=jax.ShapeDtypeStruct((rows, depth), bf16),
        name="mixed_part",
    )


def back_kernel(pre_ref, dp_ref, up_ref, qkv_ref, n_ref, out_ref, sum_ref):
    rows = pre_ref.shape[0]
    near, _, hidden = up_ref.shape
    parts, _, width = dp_ref.shape
    step = min(512, rows)
    plain = scaled = None
    for i in range(rows // step):
        at = slice(i * step, (i + 1) * step)
        total = None
        for r in range(near):
            t = mm(pre_ref[at, r * hidden : (r + 1) * hidden], up_ref[r], NT)
            total = t if total is None else total + t
        for c in range(parts):
            total = total + mm(dp_ref[c, at], qkv_ref[:, c * width : (c + 1) * width], NT)
        out_ref[at] = total.astype(bf16)
        a = jnp.sum(total, 0, keepdims=True)
        b = jnp.sum(total * n_ref[at].astype(f32), 0, keepdims=True)
        plain = a if plain is None else plain + a
        scaled = b if scaled is None else scaled + b
    sum_ref[0:1] = plain
    sum_ref[1:2] = scaled


def back_part(pre, dp, up, qkv, n, deps=()):
    rows = pre.shape[0]
    parts, _, width = dp.shape
    near, depth, hidden = up.shape
    br, bn = min(1024, rows), min(512, depth)
    out, sums = call(
        back_kernel,
        deps,
        (pre, dp, up, qkv, n),
        grid=(depth // bn, rows // br),
        in_specs=[pl.BlockSpec((br, near * hidden), lambda j, i: (i, 0)), pl.BlockSpec((parts, br, width), lambda j, i: (0, i, 0)),
                  pl.BlockSpec((near, bn, hidden), lambda j, i: (0, j, 0)), pl.BlockSpec((bn, parts * width), lambda j, i: (j, 0)),
                  pl.BlockSpec((br, bn), lambda j, i: (i, j))],
        out_specs=[pl.BlockSpec((br, bn), lambda j, i: (i, j)), pl.BlockSpec((8, bn), lambda j, i: (i, j))],
        out_shape=[jax.ShapeDtypeStruct((rows, depth), bf16), jax.ShapeDtypeStruct((rows // br * 8, depth), f32)],
        name="back_part",
    )
    return out, jnp.sum(sums.reshape(-1, 8, depth)[:, :2], 0)


def store_quarters(at_ref, total, held, keep_ref, send_ref):
    held[...] = total.astype(bf16)
    rows = held.shape[0] // 4
    y, core = at_ref[0], at_ref[1]
    for d in range(2):
        row = 2 * (1 - y if d else y)
        keep_ref[d] = held[pl.ds(pl.multiple_of((row + core) * rows, rows), rows)]
        send_ref[d] = held[pl.ds(pl.multiple_of((row + 1 - core) * rows, rows), rows)]


def weight_grad(at, xs, ys, deps=()):
    rows, m = xs[0].shape
    hidden = ys[0].shape[1] // 2
    tile = min(hidden, 512)
    per = hidden // tile
    count = len(xs)

    def kernel(at_ref, *refs):
        total = None
        for x, y in zip(refs[:count], refs[count : 2 * count], strict=True):
            t = mm(x[...], y[...], TN)
            total = t if total is None else total + t
        keep_ref, send_ref, held = refs[2 * count :]
        store_quarters(at_ref, total, held, keep_ref, send_ref)

    x_spec = pl.BlockSpec((rows, m), lambda j, at: (0, 0), pipeline_mode=pl.Buffered(1))
    y_spec = pl.BlockSpec((rows, tile), lambda j, at: (0, j))
    out = pl.BlockSpec((None, 2, m // 4, tile), lambda j, at: (j // per, 0, 0, j % per))
    shape = jax.ShapeDtypeStruct((2, 2, m // 4, hidden), bf16)
    return call(
        kernel,
        deps,
        (at, *xs, *ys),
        grid=(2 * per,),
        in_specs=[x_spec] * count + [y_spec] * count,
        out_specs=[out, out],
        out_shape=[shape, shape],
        scratch=[pltpu.VMEM((m, tile), bf16)],
        prefetch=1,
        name="weight_grad",
    )


def heads_grad(at, ns, dps, cs, attns, deps=()):
    parts, rows, wide = dps[0].shape
    m = ns[0].shape[1]
    width = wide // 2
    count = len(ns)
    out_cols = (parts + 1) * width
    if width % LANES:
        blocks = [sum(mm(n, dp[c], TN) for n, dp in zip(ns, dps, strict=True)) for c in range(parts)]
        blocks.append(sum(mm(c, a, TN) for c, a in zip(cs, attns, strict=True)))
        g = jnp.stack([jnp.concatenate([b[:, r * width : (r + 1) * width] for b in blocks], 1) for r in range(2)], 0)
        g = g.astype(bf16).reshape(2, 2, 2, m // 4, out_cols)
        g = jnp.where(at[0] == 0, g, g[:, ::-1])
        return jnp.where(at[1] == 0, g[:, :, 0], g[:, :, 1]), jnp.where(at[1] == 0, g[:, :, 1], g[:, :, 0])

    def kernel(at_ref, *refs):
        n_refs, dp_refs, c_refs, a_refs = (refs[i * count : (i + 1) * count] for i in range(4))
        keep_ref, send_ref, held = refs[4 * count :]
        part = pl.program_id(0)

        def store(total):
            for d in range(2):
                store_quarters(at_ref, total[:, d * width : (d + 1) * width], held, keep_ref.at[d], send_ref.at[d])

        @pl.when(part < parts)
        def _():
            store(sum(mm(n[...], d[...], TN) for n, d in zip(n_refs, dp_refs, strict=True)))

        @pl.when(part == parts)
        def _():
            store(sum(mm(c[...], a[...], TN) for c, a in zip(c_refs, a_refs, strict=True)))

    x_spec = pl.BlockSpec((rows, m), lambda p, at: (0, 0), pipeline_mode=pl.Buffered(1))
    dp_spec = pl.BlockSpec((None, rows, wide), lambda p, at: (jnp.minimum(p, parts - 1), 0, 0))
    a_spec = pl.BlockSpec((rows, wide), lambda p, at: (0, 0))
    out = pl.BlockSpec((2, 2, m // 4, width), lambda p, at: (0, 0, 0, p))
    shape = jax.ShapeDtypeStruct((2, 2, m // 4, out_cols), bf16)
    return call(
        kernel,
        deps,
        (at, *ns, *dps, *cs, *attns),
        grid=(parts + 1,),
        in_specs=[x_spec] * count + [dp_spec] * count + [x_spec] * count + [a_spec] * count,
        out_specs=[out, out],
        out_shape=[shape, shape],
        scratch=[pltpu.VMEM((m, width), bf16)],
        prefetch=1,
        name="heads_grad",
    )


SWAP = [(0, 1), (1, 0)]
FOLD = ("batch", "branch")


def flip(a, axis):
    return lax.ppermute(a, axis, SWAP)


def pick(a, index, axis=0):
    return lax.dynamic_index_in_dim(a, index, axis, keepdims=False)


def block_row(at_ref, k):
    y, core = at_ref[0], at_ref[1]
    chip, other = k // 2, k % 2
    return chip % 2, 2 * (1 - y if chip // 2 else y) + (1 - core if other else core)


def assemble(blocks, at, deps=()):
    rows, cols = blocks[0].shape
    tile = 256 if cols % 256 == 0 else cols

    def kernel(at_ref, *refs):
        for k in range(8):
            d, row = block_row(at_ref, k)
            refs[8][d, pl.ds(pl.multiple_of(row * rows, rows), rows)] = refs[k][...]

    return call(
        kernel,
        deps,
        (at, *blocks),
        grid=(cols // tile,),
        in_specs=[pl.BlockSpec((rows, tile), lambda j, at: (0, j))] * 8,
        out_specs=pl.BlockSpec((2, 4 * rows, tile), lambda j, at: (0, 0, j)),
        out_shape=jax.ShapeDtypeStruct((2, 4 * rows, cols), blocks[0].dtype),
        prefetch=1,
        name="assemble",
    )


def assemble_heads(blocks, at, parts, width):
    rows, cols = blocks[0].shape
    hidden = cols - (parts + 1) * width
    if width % LANES:
        w = assemble(blocks, at)
        columns = [w[r, :, c * width : (c + 1) * width] for c in range(parts + 1) for r in range(2)]
        return jnp.concatenate(columns[: 2 * parts], 1), jnp.concatenate(columns[2 * parts :], 1), w[:, :, cols - hidden :]

    def kernel(at_ref, *refs):
        qkv_ref, dense_ref, up_ref = refs[8:]
        j = pl.program_id(0)
        for k in range(8):
            d, row = block_row(at_ref, k)
            at = pl.ds(pl.multiple_of(row * rows, rows), rows)
            for d_k in range(2):
                if d_k != d:
                    continue

                @pl.when(j < parts)
                def _():
                    qkv_ref[at, d_k * width : (d_k + 1) * width] = refs[k][...]

                @pl.when(j == parts)
                def _():
                    dense_ref[at, d_k * width : (d_k + 1) * width] = refs[k][...]

                @pl.when(j > parts)
                def _():
                    up_ref[d_k, at] = refs[k][...]

    depth = 4 * rows
    return call(
        kernel,
        (),
        (at, *blocks),
        grid=(cols // width,),
        in_specs=[pl.BlockSpec((rows, width), lambda j, at: (0, j))] * 8,
        out_specs=[
            pl.BlockSpec((depth, 2 * width), lambda j, at: (0, jnp.minimum(j, parts - 1))),
            pl.BlockSpec((depth, 2 * width), lambda j, at: (0, 0)),
            pl.BlockSpec((2, depth, width), lambda j, at: (0, 0, jnp.maximum(j - parts - 1, 0))),
        ],
        out_shape=[
            jax.ShapeDtypeStruct((depth, 2 * parts * width), bf16),
            jax.ShapeDtypeStruct((depth, 2 * width), bf16),
            jax.ShapeDtypeStruct((2, depth, hidden), bf16),
        ],
        prefetch=1,
        name="assemble_heads",
    )


class Gather:
    def __init__(self, w):
        self.w = w
        self.half = w.shape[0] // 2
        self.blocks = [w, flip(w, "branch")]

    def first(self, *deps):
        w = tie(self.w, *deps) if deps else self.w
        self.x, self.y = flip(w, "near"), flip(w, "batch")

    def second(self, *deps):
        if deps:
            self.x, self.y = (tie(a, *deps) for a in (self.x, self.y))
        self.halves = self.y[: self.half], self.x[self.half :]
        self.corner = flip(self.halves[0], "near"), flip(self.halves[1], "batch")

    def third(self):
        for b in (self.x, self.y, jnp.concatenate(self.corner, 0)):
            self.blocks += [b, flip(b, "branch")]
        return self.blocks


class Scatter:
    def __init__(self, keep, send):
        self.keep, self.got = keep, flip(send, "branch")
        self.half = keep.shape[2] // 2

    def first(self, *deps):
        g = (tie(self.keep, *deps) if deps else self.keep) + self.got
        corner = g[1, 1]
        self.own, self.to_y, self.to_x = g[0, 0], g[0, 1], g[1, 0]
        self.got = flip(corner[: self.half], "near"), flip(corner[self.half :], "batch")
        return (self.own,)

    def second(self, *deps):
        h = self.half
        got = tuple(tie(a, *deps) for a in self.got) if deps else self.got
        to_y = jnp.concatenate([self.to_y[:h] + got[0], self.to_y[h:]], 0)
        to_x = jnp.concatenate([self.to_x[:h], self.to_x[h:] + got[1]], 0)
        self.got = flip(to_x, "near"), flip(to_y, "batch")
        return to_x, to_y

    def result(self):
        return self.own.astype(f32) + self.got[0].astype(f32) + self.got[1].astype(f32)


def body(
    line_size,
    tokens,
    cotangent,
    segments,
    positions,
    ln_gain,
    ln_bias,
    qkv_weight,
    qkv_bias,
    dense_weight,
    dense_bias,
    up_weight,
    up_bias,
    down_weight,
    down_bias,
):
    micros, seqs, shard, depth = tokens.shape
    full_len = segments.shape[2]
    quarter, parts, width = qkv_weight.shape
    hidden = up_weight.shape[1]
    x, y, core, z = (lax.axis_index(a) for a in ("near", "batch", "branch", "line"))
    first = x == 0

    def to_group(a, start=(), end=()):
        send = jnp.where(first, a[1], a[0])
        got = flip(tie(send, *start) if start else send, "near")
        kept = jnp.where(first, a[0], a[1])
        got = tie(got, *end) if end else got
        return jnp.concatenate([jnp.where(first, kept, got), jnp.where(first, got, kept)], 0)

    def from_group(a, end=()):
        lo, hi = a[:shard], a[shard:]
        got = flip(jnp.where(first, hi, lo), "near")
        got = tie(got, *end) if end else got
        kept = jnp.where(first, lo, hi)
        return jnp.where(first, kept, got), jnp.where(first, got, kept)

    at = jnp.stack([y, core]).astype(jnp.int32)

    units, scales, groups_n, groups_c = [], [], [], []
    for s in range(seqs):
        r = tokens[:, s].astype(f32)
        centered = r - jnp.mean(r, -1, keepdims=True)
        scales.append(lax.rsqrt(jnp.mean(centered * centered, -1, keepdims=True) + eps_norm))
        units.append(centered * scales[s])

    def normed(s):
        return (units[s] * ln_gain + ln_bias).astype(bf16)

    def gather_rows(group):
        return lax.all_gather(group, "line", axis=0, tiled=True)

    n_0 = to_group(normed(0))
    early = Gather(jnp.concatenate([qkv_weight.reshape(quarter, parts * width), dense_weight.T, up_weight], 1))
    late = Gather(down_weight.T)
    early.first(n_0)
    early.second()
    late.first(*early.corner)
    qkv, dense_t, up = assemble_heads(early.third(), at, parts, width)
    c_0 = to_group(cotangent[:, 0], early.corner, (dense_t,))
    rows_n, rows_c = [gather_rows(n_0)], [gather_rows(c_0)]
    late.second(dense_t)
    bias_qkv = jnp.concatenate([qkv_bias, flip(qkv_bias, "near")], 1)
    bias_up = jnp.concatenate([up_bias, flip(up_bias, "near")], 0)
    segment = jnp.where(first, segments[0], segments[1])
    place = jnp.where(first, positions[0], positions[1])
    tables = [rope_tables(place[s]) for s in range(seqs)]

    def scatter_rows(part):
        return lax.psum_scatter(part, "line", scatter_dimension=0, tiled=True)

    proj = project(rows_n[0], qkv, f32, (c_0,))
    n_1 = to_group(normed(1), (proj,), (proj,))
    rows_n.append(gather_rows(n_1))
    attn_0, keep, log = attention(proj, bias_qkv, tables[0], segment[0], (n_1,))
    late.second(attn_0)
    c_1 = to_group(cotangent[:, 1], (attn_0,), (attn_0,))
    rows_c.append(gather_rows(c_1))
    act_0, slope = mlp_act(rows_n[0], up, bias_up, (*late.halves, c_1))
    down_t = assemble(late.third(), at, (act_0,))
    part = mixed_part(act_0, attn_0, down_t, dense_t)
    mixed_0 = scatter_rows(part)
    grad_attn = project(rows_c[0], dense_t, bf16, (part,))
    dp_0, db_0 = attention_grad(keep, log, attn_0, grad_attn, tables[0], segment[0])
    pre_0, up_0 = mlp_pre(rows_c[0], down_t, slope, (dp_0,))
    part, back_0 = back_part(pre_0, dp_0, up, qkv, rows_n[0])
    back_sum_0 = scatter_rows(part)
    proj = project(rows_n[1], qkv, f32, (part,))
    attn_1, keep, log = attention(proj, bias_qkv, tables[1], segment[1])
    act_1, slope = mlp_act(rows_n[1], up, bias_up, (attn_1,))
    part = mixed_part(act_1, attn_1, down_t, dense_t)
    mixed_1 = scatter_rows(part)
    grad_attn = project(rows_c[1], dense_t, bf16, (part,))
    dp_1, db_1 = attention_grad(keep, log, attn_1, grad_attn, tables[1], segment[1])
    pre_1, up_1 = mlp_pre(rows_c[1], down_t, slope, (dp_1,))
    part, back_1 = back_part(pre_1, dp_1, up, qkv, rows_n[1])
    back_sum_1 = scatter_rows(part)
    grad_up = Scatter(*weight_grad(at, rows_n, (pre_0, pre_1), (part,)))
    grad_down = Scatter(*weight_grad(at, rows_c, (act_0, act_1), (grad_up.keep,)))
    mixed_0 = from_group(tie(mixed_0, grad_up.keep), (grad_down.keep,))
    sends = (*grad_up.first(grad_down.keep), *mixed_0)
    sum_qkv = (db_0 + db_1)[:parts].reshape(parts, 2, width)
    sum_up = (up_0 + up_1).reshape(2, hidden)
    out_bias = jnp.sum(cotangent, (0, 1, 2), dtype=f32)
    own, other = (jnp.concatenate([sum_qkv[:, d].reshape(-1), sum_up[d]]) for d in range(2))
    rest = jnp.concatenate([(back_0 + back_1).reshape(-1), out_bias])
    size = own.shape[0]
    sums = jnp.concatenate([other, rest])
    got = flip(sums, "near")
    sends = (*sends, sums)
    grad_heads = Scatter(*heads_grad(at, rows_n, (dp_0, dp_1), rows_c, (attn_0, attn_1), sends))
    done = grad_heads.keep
    got = tie(got, done)
    sends = (*grad_up.second(done), *grad_down.first(done))
    sums = tie(jnp.concatenate([own, rest]) + got, *sends)
    sums = sums + flip(sums, "batch")
    sends = (*grad_down.second(), *grad_heads.first(sums))
    back_sum_0 = from_group(tie(back_sum_0, *sends))
    sums = tie(sums, *sends)
    sums = sums + flip(sums, "branch")
    sends = grad_heads.second(sums)
    bias_sums, rest = sums[:size], sums[size:]
    reach = 1
    while reach < line_size:
        rest = rest + lax.ppermute(rest, "line", [(i, i ^ reach) for i in range(line_size)])
        reach *= 2
    rest = rest.reshape(3, depth)
    shift_grad = rest[0]
    gain_grad = (rest[1] - ln_bias * shift_grad) / ln_gain
    grad_up = grad_up.result()
    grad_down = grad_down.result().T
    grad_heads = grad_heads.result()
    grad_qkv = grad_heads[:, : parts * width].reshape(quarter, parts, width)
    grad_dense = grad_heads[:, parts * width :].T

    mixed, tokens_grad = [], []
    mixed_1 = from_group(tie(mixed_1, grad_qkv, grad_dense, grad_up, grad_down))
    back_sum_1 = from_group(tie(back_sum_1, *mixed_1))
    for s, (m, g) in enumerate(((mixed_0, back_sum_0), (mixed_1, back_sum_1))):
        mixed.append((tokens[:, s].astype(f32) + jnp.stack(m, 0).astype(f32) + dense_bias + down_bias).astype(bf16))
        w = jnp.stack(g, 0).astype(f32) * ln_gain
        u = units[s]
        tokens_grad.append(
            cotangent[:, s].astype(f32)
            + scales[s] * (w - jnp.mean(w, -1, keepdims=True) - u * jnp.mean(w * u, -1, keepdims=True))
        )

    return (
        jnp.stack(mixed, 1),
        jnp.stack(tokens_grad, 1),
        gain_grad,
        shift_grad,
        grad_qkv,
        bias_sums[: parts * width].reshape(parts, width),
        grad_dense,
        rest[2],
        grad_up,
        bias_sums[parts * width :],
        grad_down,
        rest[2],
    )


def solution(mesh):
    batch, branch, tensor = (mesh.shape[a] for a in ("batch", "branch", "tensor"))
    inner = Mesh(mesh.devices.reshape(batch, branch, tensor // 2, 2), ("batch", "branch", "line", "near"))
    tensor = ("line", "near")
    rows = P(None, FOLD, tensor, None)
    first = P(FOLD, None, tensor)
    weights = (first, P(None, tensor), P(tensor, FOLD), P(), P(FOLD, tensor), P(tensor), P(tensor, FOLD), P())
    return jax.shard_map(
        partial(body, inner.shape["line"]),
        mesh=inner,
        in_specs=(rows, rows, P(None, FOLD, None), P(None, FOLD, None), P(), P(), *weights),
        out_specs=(rows, rows, P(), P(), *weights),
        check_vma=False,
    )
```

time: 1150 us -> 780 us (0.68)
  waiting for transfers between devices: 507 us -> 209 us
  blocking collectives: 94 us -> 0 us
  Pallas kernels: 288 us -> 357 us
  local copies, waits for them, and re-layouts: 127 us -> 58.1 us
  starting transfers between devices: 9.98 us -> 47 us
  matrix products: 31 us -> 0 us
    all_gather x8 -> x4, waiting for transfers between devices: 248 us -> 0.05 us  [gather_rows(): return lax.all_gather(group, 'line', axis=0, tiled=True)]
    reduce_scatter x8 -> x4, waiting for transfers between devices: 185 us -> 0.07 us  [scatter_rows(): return lax.psum_scatter(part, 'line', scatter_dimension=0, tiled=True)]
    ppermute x4 -> x46, waiting for transfers between devices: 69.7 us -> 209 us  [the longest x44 209 us: flip(): return lax.ppermute(a, axis, SWAP)]
    psum x2 -> x0, blocking collectives: 85 us -> none  [the longest x1 43.4 us: body(): bias_sums = lax.psum((sum_qkv, sum_up), spread)]
    pallas_call x14 -> x48, Pallas kernels: 288 us -> 357 us  [the longest x21 357 us: call(): pl.pallas_call(run, grid_spec=spec, out_shape=out_shape, compiler_params=...]
    reshape x6 -> x3, local copies, waits for them, and re-layouts: 65.2 us -> 2.3 us  [the longest x1 2.01 us: body(): grad_qkv = grad_heads[:, :parts * width].reshape(quarter, parts, width)]
    ppermute x4 -> x46, starting transfers between devices: 8.72 us -> 45.9 us  [the longest x44 41.9 us: flip(): return lax.ppermute(a, axis, SWAP)]
    add x2 -> x16, other arithmetic: 0.88 us -> 32.4 us  [the longest x3 16.7 us: first(): g = (tie(self.keep, *deps) if deps else self.keep) + self.got]
  transfers between devices with their start and end apart: 20 -> 54, of which waited for: 13 -> 23; matrix products, arithmetic and copies ran while one was open for 20% -> 15% of each run, Pallas kernels for 25% -> 46%
where the time goes in v2:
time: 780 us; the launch traced here: 770 us
  Pallas kernels  357 us (46%)
  waiting for transfers between devices  209 us (27%)
  other arithmetic  83 us (11%)
  local copies, waits for them, and re-layouts  58.1 us (7%)
  starting transfers between devices  47 us (6%)
  between operations  15.8 us (2%)
    pallas_call x21, Pallas kernels, call(): pl.pallas_call(run, grid_spec=spec, out_shape=out_shape, compiler_params=...  357 us
    ppermute x44, waiting for transfers between devices, flip(): return lax.ppermute(a, axis, SWAP)  209 us
    ppermute x44, starting transfers between devices, flip(): return lax.ppermute(a, axis, SWAP)  41.9 us
    unnamed x154, local copies, waits for them, and re-layouts  26.4 us
    add x3, other arithmetic, first(): g = (tie(self.keep, *deps) if deps else self.keep) + self.got  16.7 us
  transfers between devices with their start and end apart: 54, of which 23 were waited for; matrix products, arithmetic and copies ran while one was open for 15% of the time, Pallas kernels for 46%

profile of v2, /device:TPU:0, one launch (start us, length us, event | category | flops | bytes accessed | tf_op | source)
XLA Modules:
  0.0 769.9 jit_solution(7342420489345941021)
XLA Ops:
  33.6 43.7 %collective-permute-done.4.refs_5_ = bf16[512,2048]{1,0:T(8,128)(2,1)S(1)} collective-permute-done((bf16[512,2048]{1,0:T(8,128)(2,1)}, bf16[512,2048]{1,0:T(8,128)(2,1)S(1)}, u32[]{:S(2)}, u32[]{:S(2)}) %collective-permute-start.4) | collective-permute-done | bytes 2097184 | tf_op jit(solution)/shard_map/ppermute | solution.py:527
  82.3 18.7 %collective-permute-done.6.refs_1_ = bf16[256,2048]{1,0:T(8,128)(2,1)S(1)} collective-permute-done((bf16[256,2048]{1,0:T(8,128)(2,1)S(1)}, bf16[256,2048]{1,0:T(8,128)(2,1)S(1)}, u32[]{:S(2)}, u32[]{:S(2)}) %collective-permute-start.6) | collective-permute-done | bytes 1048608 | tf_op jit(solution)/shard_map/ppermute | solution.py:527
  110.1 14.5 %assemble_heads.1 = (bf16[2048,1536]{1,0:T(8,128)(2,1)}, bf16[2048,512]{1,0:T(8,128)(2,1)}, bf16[2,2048,1024]{2,1,0:T(8,128)(2,1)}) custom-call(s32[2]{0:T(128)} %pad_add_fusion.refs_0_, bf16[512,2048]{1,0:T(8,128)(2,1)} %pad_maximum_fusion.1.refs_1_, bf16[512,2048]{1,0:T(8,128)(2,1)} %collective-permute-done.1.refs_2_, ...), custom_call_target="tpu_custom_call" | custom-call | flops 3500000000 | bytes 3500001 | tf_op jit(solution)/shard_map/assemble_heads/pallas_call | solution.py:52
  127.7 12.0 %project.4.refs_1_.refs_0_.refs_2_ = f32[1024,1536]{1,0:T(8,128)} custom-call(bf16[1024,2048]{1,0:T(8,128)(2,1)} %all-gather.5.cloned.1.call-done.refs_0_.refs_4_.refs_1_, bf16[2048,1536]{1,0:T(8,128)(2,1)} %get-tuple-element.45.refs_1_.refs_3_, bf16[256,2048]{1,0:T(8,128)(2,1)} %pad_maximum_fusion.4.refs_2_), custom_call_target="tpu_custom_call" | custom-call | flops 2250000128 | bytes 2250001 | tf_op jit(solution)/shard_map/project/pallas_call | solution.py:52
  140.9 13.2 %collective-permute-done.13.refs_0_ = bf16[128,2048]{1,0:T(8,128)(2,1)} collective-permute-done((bf16[128,2048]{1,0:T(8,128)(2,1)}, bf16[128,2048]{1,0:T(8,128)(2,1)}, u32[]{:S(2)}, u32[]{:S(2)}) %collective-permute-start.13) | collective-permute-done | bytes 524320 | tf_op jit(solution)/shard_map/ppermute | solution.py:527
  166.6 17.3 %attention.2 = (bf16[1024,512]{1,0:T(8,128)(2,1)}, bf16[3,1024,512]{2,1,0:T(8,128)(2,1)}, f32[32,1024]{1,0:T(8,128)}) custom-call(f32[1024,1536]{1,0:T(8,128)} %project.4.refs_1_.refs_0_.refs_2_, f32[1024,1536]{1,0:T(8,128)} %project.4.refs_1_.refs_0_.refs_2_, f32[1024,1536]{1,0:T(8,128)} %project.4.refs_1_.refs_0_.refs_2_, f32[1,1536]{1,0:T(1,128)} %bitcast.245, ...), custom_call_target="tpu_custom_call" | custom-call | flops 24999999488 | bytes 25000000 | tf_op jit(solution)/shard_map/attention/pallas_call | solution.py:52
  184.8 12.2 %collective-permute-done.15.refs_0_ = bf16[128,2048]{1,0:T(8,128)(2,1)S(1)} collective-permute-done((bf16[128,2048]{1,0:T(8,128)(2,1)}, bf16[128,2048]{1,0:T(8,128)(2,1)S(1)}, u32[]{:S(2)}, u32[]{:S(2)}) %collective-permute-start.15) | collective-permute-done | bytes 524320 | tf_op jit(solution)/shard_map/ppermute | solution.py:527
  205.5 21.5 %collective-permute-done.10.refs_0_ = bf16[512,1024]{1,0:T(8,128)(2,1)} collective-permute-done((bf16[512,1024]{1,0:T(8,128)(2,1)}, bf16[512,1024]{1,0:T(8,128)(2,1)}, u32[]{:S(2)}, u32[]{:S(2)}) %collective-permute-start.10) | collective-permute-done | bytes 1048608 | tf_op jit(solution)/shard_map/ppermute | solution.py:527
  233.7 6.6 collective-permute-done.19
  247.8 17.5 %mlp_act.2 = (bf16[1024,2048]{1,0:T(8,128)(2,1)}, bf16[1024,2048]{1,0:T(8,128)(2,1)}) custom-call(bf16[1024,2048]{1,0:T(8,128)(2,1)} %all-gather.5.cloned.1.call-done.refs_0_.refs_4_.refs_1_, bf16[2,2048,1024]{2,1,0:T(8,128)(2,1)} %get-tuple-element.43.refs_1_.refs_2_, f32[1,2048]{1,0:T(1,128)} %bitcast.243, bf16[256,1024]{1,0:T(8,128)(2,1)} %slice.447.refs_3_, ...), custom_call_target="tpu_custom_call" | custom-call | flops 4250000128 | bytes 4250001 | tf_op jit(solution)/shard_map/mlp_act/pallas_call | solution.py:52
  265.4 7.8 %assemble.1.refs_2_.refs_1_ = bf16[2,2048,1024]{2,1,0:T(8,128)(2,1)} custom-call(s32[2]{0:T(128)} %pad_add_fusion.refs_0_, bf16[512,1024]{1,0:T(8,128)(2,1)} %bitcast.223, bf16[512,1024]{1,0:T(8,128)(2,1)} %collective-permute-done.16.refs_2_, bf16[512,1024]{1,0:T(8,128)(2,1)} %tie.36.refs_3_, bf16[512,1024]{1,0:T(8,128)(2,1)} %collective-permute-done.17.refs_4_, ...), custom_call_target="tpu_custom_call" | custom-call | flops 2000000000 | bytes 2000001 | tf_op jit(solution)/shard_map/assemble/pallas_call | solution.py:52
  273.1 16.0 %mixed_part.2.refs_2_ = bf16[1024,2048]{1,0:T(8,128)(2,1)} custom-call(bf16[1024,2048]{1,0:T(8,128)(2,1)} %get-tuple-element.47.refs_9_.refs_0_.refs_3_, bf16[1024,512]{1,0:T(8,128)(2,1)} %get-tuple-element.46.refs_1_.refs_2_.refs_7_, bf16[2,2048,1024]{2,1,0:T(8,128)(2,1)} %assemble.1.refs_2_.refs_1_, bf16[2048,512]{1,0:T(8,128)(2,1)} %get-tuple-element.44.refs_1_.refs_3_), custom_call_target="tpu_custom_call" | custom-call | flops 4000000000 | bytes 4000001 | tf_op jit(solution)/shard_map/mixed_part/pallas_call | solution.py:52
  289.2 5.8 project.5.refs_3_
  295.0 23.0 %attention_grad.2 = (bf16[3,1024,512]{2,1,0:T(8,128)(2,1)}, f32[8,512]{1,0:T(8,128)}) custom-call(bf16[3,1024,512]{2,1,0:T(8,128)(2,1)} %get-tuple-element.49.refs_0_, f32[32,1024]{1,0:T(8,128)} %get-tuple-element.50.refs_1_, bf16[1024,512]{1,0:T(8,128)(2,1)} %get-tuple-element.46.refs_1_.refs_2_.refs_7_, bf16[1024,512]{1,0:T(8,128)(2,1)} %project.5.refs_3_, ...), custom_call_target="tpu_custom_call" | custom-call | flops 5750000128 | bytes 5750001 | tf_op jit(solution)/shard_map/attention_grad/pallas_call | solution.py:52
  318.0 14.0 %mlp_pre.2 = (bf16[1024,2048]{1,0:T(8,128)(2,1)}, f32[8,2048]{1,0:T(8,128)}) custom-call(bf16[1024,2048]{1,0:T(8,128)(2,1)} %all-gather.9.cloned.1.call-done.refs_0_.refs_1_.refs_5_, bf16[2,2048,1024]{2,1,0:T(8,128)(2,1)} %assemble.1.refs_2_.refs_1_, bf16[1024,2048]{1,0:T(8,128)(2,1)} %get-tuple-element.48.refs_2_, ...), custom_call_target="tpu_custom_call" | custom-call | flops 3500000000 | bytes 3500001 | tf_op jit(solution)/shard_map/mlp_pre/pallas_call | solution.py:52
  332.0 22.0 %back_part.2 = (bf16[1024,2048]{1,0:T(8,128)(2,1)}, f32[8,2048]{1,0:T(8,128)}) custom-call(bf16[1024,2048]{1,0:T(8,128)(2,1)} %get-tuple-element.52.refs_0_.refs_3_, bf16[3,1024,512]{2,1,0:T(8,128)(2,1)} %get-tuple-element.51.refs_3_.refs_1_, bf16[2,2048,1024]{2,1,0:T(8,128)(2,1)} %get-tuple-element.43.refs_1_.refs_2_, ...), custom_call_target="tpu_custom_call" | custom-call | flops 5500000256 | bytes 5500001 | tf_op jit(solution)/shard_map/back_part/pallas_call | solution.py:52
  358.8 11.9 %project.6.refs_0_.refs_1_.refs_2_ = f32[1024,1536]{1,0:T(8,128)} custom-call(bf16[1024,2048]{1,0:T(8,128)(2,1)} %all-gather.7.cloned.1.call-done.refs_0_.refs_4_.refs_2_, bf16[2048,1536]{1,0:T(8,128)(2,1)} %get-tuple-element.45.refs_1_.refs_3_, bf16[1024,2048]{1,0:T(8,128)(2,1)} %get-tuple-element.53.refs_2_), custom_call_target="tpu_custom_call" | custom-call | flops 2250000128 | bytes 2250001 | tf_op jit(solution)/shard_map/project/pallas_call | solution.py:52
  370.8 17.3 %attention.3 = (bf16[1024,512]{1,0:T(8,128)(2,1)}, bf16[3,1024,512]{2,1,0:T(8,128)(2,1)}, f32[32,1024]{1,0:T(8,128)}) custom-call(f32[1024,1536]{1,0:T(8,128)} %project.6.refs_0_.refs_1_.refs_2_, f32[1024,1536]{1,0:T(8,128)} %project.6.refs_0_.refs_1_.refs_2_, f32[1024,1536]{1,0:T(8,128)} %project.6.refs_0_.refs_1_.refs_2_, f32[1,1536]{1,0:T(1,128)} %bitcast.248, ...), custom_call_target="tpu_custom_call" | custom-call | flops 24999999488 | bytes 25000000 | tf_op jit(solution)/shard_map/attention/pallas_call | solution.py:52
  388.1 17.6 %mlp_act.3 = (bf16[1024,2048]{1,0:T(8,128)(2,1)}, bf16[1024,2048]{1,0:T(8,128)(2,1)}) custom-call(bf16[1024,2048]{1,0:T(8,128)(2,1)} %all-gather.7.cloned.1.call-done.refs_0_.refs_4_.refs_2_, bf16[2,2048,1024]{2,1,0:T(8,128)(2,1)} %get-tuple-element.43.refs_1_.refs_2_, f32[1,2048]{1,0:T(1,128)} %bitcast.244, ...), custom_call_target="tpu_custom_call" | custom-call | flops 4250000128 | bytes 4250001 | tf_op jit(solution)/shard_map/mlp_act/pallas_call | solution.py:52
  405.7 16.1 %mixed_part.3.refs_2_ = bf16[1024,2048]{1,0:T(8,128)(2,1)} custom-call(bf16[1024,2048]{1,0:T(8,128)(2,1)} %get-tuple-element.58.refs_0_.refs_4_, bf16[1024,512]{1,0:T(8,128)(2,1)} %get-tuple-element.54.refs_3_.refs_1_.refs_2_.refs_8_, bf16[2,2048,1024]{2,1,0:T(8,128)(2,1)} %assemble.1.refs_2_.refs_1_, bf16[2048,512]{1,0:T(8,128)(2,1)} %get-tuple-element.44.refs_1_.refs_3_), custom_call_target="tpu_custom_call" | custom-call | flops 4000000000 | bytes 4000001 | tf_op jit(solution)/shard_map/mixed_part/pallas_call | solution.py:52
  422.0 5.9 project.7.refs_3_
  428.0 22.7 %attention_grad.3 = (bf16[3,1024,512]{2,1,0:T(8,128)(2,1)}, f32[8,512]{1,0:T(8,128)}) custom-call(bf16[3,1024,512]{2,1,0:T(8,128)(2,1)} %get-tuple-element.56.refs_0_, f32[32,1024]{1,0:T(8,128)} %get-tuple-element.57.refs_1_, bf16[1024,512]{1,0:T(8,128)(2,1)} %get-tuple-element.54.refs_3_.refs_1_.refs_2_.refs_8_, bf16[1024,512]{1,0:T(8,128)(2,1)} %project.7.refs_3_, ...), custom_call_target="tpu_custom_call" | custom-call | flops 5750000128 | bytes 5750001 | tf_op jit(solution)/shard_map/attention_grad/pallas_call | solution.py:52
  450.7 14.2 %mlp_pre.3 = (bf16[1024,2048]{1,0:T(8,128)(2,1)}, f32[8,2048]{1,0:T(8,128)}) custom-call(bf16[1024,2048]{1,0:T(8,128)(2,1)} %all-gather.11.cloned.1.call-done.refs_0_.refs_2_.refs_6_, bf16[2,2048,1024]{2,1,0:T(8,128)(2,1)} %assemble.1.refs_2_.refs_1_, bf16[1024,2048]{1,0:T(8,128)(2,1)} %get-tuple-element.55.refs_2_, ...), custom_call_target="tpu_custom_call" | custom-call | flops 3500000000 | bytes 3500001 | tf_op jit(solution)/shard_map/mlp_pre/pallas_call | solution.py:52
  464.9 21.9 %back_part.3 = (bf16[1024,2048]{1,0:T(8,128)(2,1)}, f32[8,2048]{1,0:T(8,128)}) custom-call(bf16[1024,2048]{1,0:T(8,128)(2,1)} %get-tuple-element.60.refs_0_.refs_4_, bf16[3,1024,512]{2,1,0:T(8,128)(2,1)} %get-tuple-element.59.refs_3_.refs_1_.refs_4_, bf16[2,2048,1024]{2,1,0:T(8,128)(2,1)} %get-tuple-element.43.refs_1_.refs_2_, ...), custom_call_target="tpu_custom_call" | custom-call | flops 5500000256 | bytes 5500001 | tf_op jit(solution)/shard_map/back_part/pallas_call | solution.py:52
  486.8 25.7 %weight_grad.2 = (bf16[2,2,512,1024]{3,2,1,0:T(8,128)(2,1)}, bf16[2,2,512,1024]{3,2,1,0:T(8,128)(2,1)}) custom-call(s32[2]{0:T(128)} %pad_add_fusion.refs_0_, bf16[1024,2048]{1,0:T(8,128)(2,1)} %all-gather.5.cloned.1.call-done.refs_0_.refs_4_.refs_1_, bf16[1024,2048]{1,0:T(8,128)(2,1)} %all-gather.7.cloned.1.call-done.refs_0_.refs_4_.refs_2_, ...), custom_call_target="tpu_custom_call" | custom-call | flops 24999999488 | bytes 25000000 | tf_op jit(solution)/shard_map/weight_grad/pallas_call | solution.py:52
  512.5 25.1 %weight_grad.3 = (bf16[2,2,512,1024]{3,2,1,0:T(8,128)(2,1)}, bf16[2,2,512,1024]{3,2,1,0:T(8,128)(2,1)}) custom-call(s32[2]{0:T(128)} %pad_add_fusion.refs_0_, bf16[1024,2048]{1,0:T(8,128)(2,1)} %all-gather.9.cloned.1.call-done.refs_0_.refs_1_.refs_5_, bf16[1024,2048]{1,0:T(8,128)(2,1)} %all-gather.11.cloned.1.call-done.refs_0_.refs_2_.refs_6_, ...), custom_call_target="tpu_custom_call" | custom-call | flops 24999999488 | bytes 25000000 | tf_op jit(solution)/shard_map/weight_grad/pallas_call | solution.py:52
  543.2 11.9 %collective-permute-done.22.refs_0_ = bf16[128,2048]{1,0:T(8,128)(2,1)S(1)} collective-permute-done((bf16[128,2048]{1,0:T(8,128)(2,1)S(1)}, bf16[128,2048]{1,0:T(8,128)(2,1)S(1)}, u32[]{:S(2)}, u32[]{:S(2)}) %collective-permute-start.22) | collective-permute-done | bytes 524320 | tf_op jit(solution)/shard_map/ppermute | solution.py:527
  566.7 28.9 %heads_grad.1 = (bf16[2,2,512,1024]{3,2,1,0:T(8,128)(2,1)}, bf16[2,2,512,1024]{3,2,1,0:T(8,128)(2,1)}) custom-call(s32[2]{0:T(128)} %pad_add_fusion.refs_0_, bf16[1024,2048]{1,0:T(8,128)(2,1)} %all-gather.5.cloned.1.call-done.refs_0_.refs_4_.refs_1_, bf16[1024,2048]{1,0:T(8,128)(2,1)} %all-gather.7.cloned.1.call-done.refs_0_.refs_4_.refs_2_, ...), custom_call_target="tpu_custom_call" | custom-call | flops 7000000000 | bytes 7000001 | tf_op jit(solution)/shard_map/heads_grad/pallas_call | solution.py:52
  613.5 7.3 collective-permute-done.32
  639.9 14.3 %collective-permute-done.28 = f32[7936]{0:T(1024)S(1)} collective-permute-done((f32[7936]{0:T(1024)}, f32[7936]{0:T(1024)S(1)}, u32[]{:S(2)}, u32[]{:S(2)}) %collective-permute-start.28) | collective-permute-done | bytes 31776 | tf_op jit(solution)/shard_map/ppermute | solution.py:527
  671.0 15.9 %collective-permute-done.35.refs_0_ = bf16[256,1024]{1,0:T(8,128)(2,1)} collective-permute-done((bf16[256,1024]{1,0:T(8,128)(2,1)}, bf16[256,1024]{1,0:T(8,128)(2,1)}, u32[]{:S(2)}, u32[]{:S(2)}) %collective-permute-start.35) | collective-permute-done | bytes 524320 | tf_op jit(solution)/shard_map/ppermute | solution.py:527
  716.4 5.8 collective-permute-done.34
  (407 shorter events, 225.9 us)
Async XLA Ops:
  7.2 120.6 %all-gather.5.cloned.1.call-start = ((), (), s32[]{:S(2)}) async-start(), calls=%async_computation.4 | async-start | bytes 5242880 | tf_op jit(solution)/shard_map/all_gather | solution.py:711
  30.3 47.0 %collective-permute-start.4 = (bf16[512,2048]{1,0:T(8,128)(2,1)}, bf16[512,2048]{1,0:T(8,128)(2,1)S(1)}, u32[]{:S(2)}, u32[]{:S(2)}) collective-permute-start(bf16[512,2048]{1,0:T(8,128)(2,1)} %tie.27), channel_id=1, source_target_pairs={{0,16},{16,0},{1,17},{17,1},{2,18},{18,2},{3,19},{19,3},{4,20},{20... | collective-permute-start | bytes 6291464 | tf_op jit(solution)/shard_map/ppermute | solution.py:527
  32.0 46.9 %collective-permute-start.2 = (bf16[512,2048]{1,0:T(8,128)(2,1)}, bf16[512,2048]{1,0:T(8,128)(2,1)}, u32[]{:S(2)}, u32[]{:S(2)}) collective-permute-start(bf16[512,2048]{1,0:T(8,128)(2,1)} %tie.27), channel_id=1, source_target_pairs={{0,1},{1,0},{2,3},{3,2},{4,5},{5,4},{6,7},{7,6},{8,9},{9,8},{10,11... | collective-permute-start | bytes 6291464 | tf_op jit(solution)/shard_map/ppermute | solution.py:527
  33.6 255.6 %all-gather.9.cloned.1.call-start = ((), (), s32[]{:S(2)}) async-start(), calls=%async_computation.7 | async-start | bytes 5242880 | tf_op jit(solution)/shard_map/all_gather | solution.py:711
  77.4 23.6 %collective-permute-start.6 = (bf16[256,2048]{1,0:T(8,128)(2,1)S(1)}, bf16[256,2048]{1,0:T(8,128)(2,1)S(1)}, u32[]{:S(2)}, u32[]{:S(2)}) collective-permute-start(bf16[256,2048]{1,0:T(8,128)(2,1)S(1)} %slice.441), channel_id=1, source_target_pairs={{0,1},{1,0},{2,3},{3,2},{4,5},{5,4},{6,7},{7,6},{8,9},{9,8},{10,11... | collective-permute-start | bytes 3145736 | tf_op jit(solution)/shard_map/ppermute | solution.py:527
  80.2 23.3 %collective-permute-start.7 = (bf16[256,2048]{1,0:T(8,128)(2,1)S(1)}, bf16[256,2048]{1,0:T(8,128)(2,1)S(1)}, u32[]{:S(2)}, u32[]{:S(2)}) collective-permute-start(bf16[256,2048]{1,0:T(8,128)(2,1)S(1)} %slice.442), channel_id=1, source_target_pairs={{0,16},{16,0},{1,17},{17,1},{2,18},{18,2},{3,19},{19,3},{4,20},{20... | collective-permute-start | bytes 3145736 | tf_op jit(solution)/shard_map/ppermute | solution.py:527
  81.8 26.6 %collective-permute-start.1 = (bf16[512,2048]{1,0:T(8,128)(2,1)}, bf16[512,2048]{1,0:T(8,128)(2,1)}, u32[]{:S(2)}, u32[]{:S(2)}) collective-permute-start(bf16[512,2048]{1,0:T(8,128)(2,1)} %pad_maximum_fusion.1.refs_1_), channel_id=1, source_target_pairs={{0,8},{8,0},{1,9},{9,1},{2,10},{10,2},{3,11},{11,3},{4,12},{12,4},... | collective-permute-start | bytes 6291464 | tf_op jit(solution)/shard_map/ppermute | solution.py:527
  81.8 26.6 %collective-permute-start.5 = (bf16[512,2048]{1,0:T(8,128)(2,1)}, bf16[512,2048]{1,0:T(8,128)(2,1)}, u32[]{:S(2)}, u32[]{:S(2)}) collective-permute-start(bf16[512,2048]{1,0:T(8,128)(2,1)} %copy-done.21), channel_id=1, source_target_pairs={{0,8},{8,0},{1,9},{9,1},{2,10},{10,2},{3,11},{11,3},{4,12},{12,4},... | collective-permute-start | bytes 6291464 | tf_op jit(solution)/shard_map/ppermute | solution.py:527
  82.3 26.0 %collective-permute-start.3 = (bf16[512,2048]{1,0:T(8,128)(2,1)}, bf16[512,2048]{1,0:T(8,128)(2,1)}, u32[]{:S(2)}, u32[]{:S(2)}) collective-permute-start(bf16[512,2048]{1,0:T(8,128)(2,1)} %collective-permute-done.2.refs_3_), channel_id=1, source_target_pairs={{0,8},{8,0},{1,9},{9,1},{2,10},{10,2},{3,11},{11,3},{4,12},{12,4},... | collective-permute-start | bytes 6291464 | tf_op jit(solution)/shard_map/ppermute | solution.py:527
  126.8 232.0 %all-gather.7.cloned.1.call-start = ((), (), s32[]{:S(2)}) async-start(), calls=%async_computation.6 | async-start | bytes 5242880 | tf_op jit(solution)/shard_map/all_gather | solution.py:711
  156.3 265.7 %all-gather.11.cloned.1.call-start = ((), (), s32[]{:S(2)}) async-start(), calls=%async_computation.8 | async-start | bytes 5242880 | tf_op jit(solution)/shard_map/all_gather | solution.py:711
  200.1 339.9 %reduce-scatter.5.cloned.1.call-start = ((), (), s32[]{:S(2)}) async-start(), calls=%async_computation.5 | async-start | bytes 5242880 | tf_op jit(solution)/shard_map/reduce_scatter | solution.py:730
  203.3 23.6 %collective-permute-start.10 = (bf16[512,1024]{1,0:T(8,128)(2,1)}, bf16[512,1024]{1,0:T(8,128)(2,1)}, u32[]{:S(2)}, u32[]{:S(2)}) collective-permute-start(bf16[512,1024]{1,0:T(8,128)(2,1)} %tie.28), channel_id=1, source_target_pairs={{0,16},{16,0},{1,17},{17,1},{2,18},{18,2},{3,19},{19,3},{4,20},{20... | collective-permute-start | bytes 3145736 | tf_op jit(solution)/shard_map/ppermute | solution.py:527
  204.8 24.8 %collective-permute-start.14 = (bf16[512,1024]{1,0:T(8,128)(2,1)}, bf16[512,1024]{1,0:T(8,128)(2,1)S(1)}, u32[]{:S(2)}, u32[]{:S(2)}) collective-permute-start(bf16[512,1024]{1,0:T(8,128)(2,1)} %tie.28), channel_id=1, source_target_pairs={{0,1},{1,0},{2,3},{3,2},{4,5},{5,4},{6,7},{7,6},{8,9},{9,8},{10,11... | collective-permute-start | bytes 3145736 | tf_op jit(solution)/shard_map/ppermute | solution.py:527
  233.2 32.1 %collective-permute-start.16 = (bf16[512,1024]{1,0:T(8,128)(2,1)S(1)}, bf16[512,1024]{1,0:T(8,128)(2,1)}, u32[]{:S(2)}, u32[]{:S(2)}) collective-permute-start(bf16[512,1024]{1,0:T(8,128)(2,1)S(1)} %bitcast.224), channel_id=1, source_target_pairs={{0,8},{8,0},{1,9},{9,1},{2,10},{10,2},{3,11},{11,3},{4,12},{12,4},... | collective-permute-start | bytes 3145736 | tf_op jit(solution)/shard_map/ppermute | solution.py:527
  233.2 32.1 %collective-permute-start.18 = (bf16[512,1024]{1,0:T(8,128)(2,1)}, bf16[512,1024]{1,0:T(8,128)(2,1)}, u32[]{:S(2)}, u32[]{:S(2)}) collective-permute-start(bf16[512,1024]{1,0:T(8,128)(2,1)} %tie.34.refs_5_), channel_id=1, source_target_pairs={{0,8},{8,0},{1,9},{9,1},{2,10},{10,2},{3,11},{11,3},{4,12},{12,4},... | collective-permute-start | bytes 3145736 | tf_op jit(solution)/shard_map/ppermute | solution.py:527
  233.7 31.6 %collective-permute-start.17 = (bf16[512,1024]{1,0:T(8,128)(2,1)}, bf16[512,1024]{1,0:T(8,128)(2,1)}, u32[]{:S(2)}, u32[]{:S(2)}) collective-permute-start(bf16[512,1024]{1,0:T(8,128)(2,1)} %tie.36.refs_3_), channel_id=1, source_target_pairs={{0,8},{8,0},{1,9},{9,1},{2,10},{10,2},{3,11},{11,3},{4,12},{12,4},... | collective-permute-start | bytes 3145736 | tf_op jit(solution)/shard_map/ppermute | solution.py:527
  289.1 413.6 %reduce-scatter.9.cloned.1.call-start = ((), (), s32[]{:S(2)}) async-start(), calls=%async_computation.10 | async-start | bytes 5242880 | tf_op jit(solution)/shard_map/reduce_scatter | solution.py:730
  354.0 374.3 %reduce-scatter.7.cloned.1.call-start = ((), (), s32[]{:S(2)}) async-start(), calls=%async_computation.9 | async-start | bytes 5242880 | tf_op jit(solution)/shard_map/reduce_scatter | solution.py:730
  421.8 321.3 %reduce-scatter.11.cloned.1.call-start = ((), (), s32[]{:S(2)}) async-start(), calls=%async_computation.11 | async-start | bytes 5242880 | tf_op jit(solution)/shard_map/reduce_scatter | solution.py:730
  512.5 45.6 %collective-permute-start.23 = (bf16[2,2,512,1024]{3,2,1,0:T(8,128)(2,1)}, bf16[2,2,512,1024]{3,2,1,0:T(8,128)(2,1)}, u32[]{:S(2)}, u32[]{:S(2)}) collective-permute-start(bf16[2,2,512,1024]{3,2,1,0:T(8,128)(2,1)} %get-tuple-element.64), channel_id=1, source_target_pairs={{0,8},{8,0},{1,9},{9,1},{2,10},{10,2},{3,11},{11,3},{4,12},{12,4},... | collective-permute-start | bytes 12582920 | tf_op jit(solution)/shard_map/ppermute | solution.py:527
  537.6 59.9 %collective-permute-start.27 = (bf16[2,2,512,1024]{3,2,1,0:T(8,128)(2,1)}, bf16[2,2,512,1024]{3,2,1,0:T(8,128)(2,1)}, u32[]{:S(2)}, u32[]{:S(2)}) collective-permute-start(bf16[2,2,512,1024]{3,2,1,0:T(8,128)(2,1)} %get-tuple-element.72), channel_id=1, source_target_pairs={{0,8},{8,0},{1,9},{9,1},{2,10},{10,2},{3,11},{11,3},{4,12},{12,4},... | collective-permute-start | bytes 12582920 | tf_op jit(solution)/shard_map/ppermute | solution.py:527
  595.6 61.3 %collective-permute-start.29 = (bf16[2,2,512,1024]{3,2,1,0:T(8,128)(2,1)}, bf16[2,2,512,1024]{3,2,1,0:T(8,128)(2,1)}, u32[]{:S(2)}, u32[]{:S(2)}) collective-permute-start(bf16[2,2,512,1024]{3,2,1,0:T(8,128)(2,1)} %get-tuple-element.73), channel_id=1, source_target_pairs={{0,8},{8,0},{1,9},{9,1},{2,10},{10,2},{3,11},{11,3},{4,12},{12,4},... | collective-permute-start | bytes 12582920 | tf_op jit(solution)/shard_map/ppermute | solution.py:527
  622.9 42.5 %collective-permute-start.39 = (bf16[512,1024]{1,0:T(8,128)(2,1)S(1)}, bf16[512,1024]{1,0:T(8,128)(2,1)}, u32[]{:S(2)}, u32[]{:S(2)}) collective-permute-start(bf16[512,1024]{1,0:T(8,128)(2,1)S(1)} %pad_maximum_fusion.9.refs_1_), channel_id=1, source_target_pairs={{0,1},{1,0},{2,3},{3,2},{4,5},{5,4},{6,7},{7,6},{8,9},{9,8},{10,11... | collective-permute-start | bytes 3145736 | tf_op jit(solution)/shard_map/ppermute | solution.py:527
  624.8 42.1 %collective-permute-start.40 = (bf16[512,1024]{1,0:T(8,128)(2,1)S(1)}, bf16[512,1024]{1,0:T(8,128)(2,1)}, u32[]{:S(2)}, u32[]{:S(2)}) collective-permute-start(bf16[512,1024]{1,0:T(8,128)(2,1)S(1)} %pad_maximum_fusion.10.refs_2_), channel_id=1, source_target_pairs={{0,16},{16,0},{1,17},{17,1},{2,18},{18,2},{3,19},{19,3},{4,20},{20... | collective-permute-start | bytes 3145736 | tf_op jit(solution)/shard_map/ppermute | solution.py:527
  639.3 57.9 %collective-permute-start.37 = (bf16[512,1024]{1,0:T(8,128)(2,1)}, bf16[512,1024]{1,0:T(8,128)(2,1)}, u32[]{:S(2)}, u32[]{:S(2)}) collective-permute-start(bf16[512,1024]{1,0:T(8,128)(2,1)} %pad_maximum_fusion.7.refs_1_), channel_id=1, source_target_pairs={{0,1},{1,0},{2,3},{3,2},{4,5},{5,4},{6,7},{7,6},{8,9},{9,8},{10,11... | collective-permute-start | bytes 3145736 | tf_op jit(solution)/shard_map/ppermute | solution.py:527
  655.6 41.6 %collective-permute-start.38 = (bf16[512,1024]{1,0:T(8,128)(2,1)S(1)}, bf16[512,1024]{1,0:T(8,128)(2,1)}, u32[]{:S(2)}, u32[]{:S(2)}) collective-permute-start(bf16[512,1024]{1,0:T(8,128)(2,1)S(1)} %copy-done.24), channel_id=1, source_target_pairs={{0,16},{16,0},{1,17},{17,1},{2,18},{18,2},{3,19},{19,3},{4,20},{20... | collective-permute-start | bytes 3145736 | tf_op jit(solution)/shard_map/ppermute | solution.py:527
  665.3 25.2 %collective-permute-start.30 = (bf16[256,1024]{1,0:T(8,128)(2,1)}, bf16[256,1024]{1,0:T(8,128)(2,1)}, u32[]{:S(2)}, u32[]{:S(2)}) collective-permute-start(bf16[256,1024]{1,0:T(8,128)(2,1)} %get-tuple-element.119), channel_id=1, source_target_pairs={{0,16},{16,0},{1,17},{17,1},{2,18},{18,2},{3,19},{19,3},{4,20},{20... | collective-permute-start | bytes 1572872 | tf_op jit(solution)/shard_map/ppermute | solution.py:527
  669.4 33.3 %collective-permute-start.44 = (f32[6144]{0:T(1024)S(1)}, f32[6144]{0:T(1024)S(1)}, u32[]{:S(2)}, u32[]{:S(2)}) collective-permute-start(f32[6144]{0:T(1024)S(1)} %slice.492), channel_id=1, source_target_pairs={{0,2},{2,0},{4,6},{6,4},{1,3},{3,1},{5,7},{7,5},{8,10},{10,8},{12,... | collective-permute-start | bytes 73736 | tf_op jit(solution)/shard_map/ppermute | solution.py:785
  693.4 23.0 %collective-permute-start.36 = (bf16[512,1024]{1,0:T(8,128)(2,1)}, bf16[512,1024]{1,0:T(8,128)(2,1)}, u32[]{:S(2)}, u32[]{:S(2)}) collective-permute-start(bf16[512,1024]{1,0:T(8,128)(2,1)} %pad_maximum_fusion.12), channel_id=1, source_target_pairs={{0,16},{16,0},{1,17},{17,1},{2,18},{18,2},{3,19},{19,3},{4,20},{20... | collective-permute-start | bytes 3145736 | tf_op jit(solution)/shard_map/ppermute | solution.py:527
  695.8 26.4 %collective-permute-start.34 = (bf16[512,1024]{1,0:T(8,128)(2,1)}, bf16[512,1024]{1,0:T(8,128)(2,1)}, u32[]{:S(2)}, u32[]{:S(2)}) collective-permute-start(bf16[512,1024]{1,0:T(8,128)(2,1)} %pad_maximum_fusion.11), channel_id=1, source_target_pairs={{0,1},{1,0},{2,3},{3,2},{4,5},{5,4},{6,7},{7,6},{8,9},{9,8},{10,11... | collective-permute-start | bytes 3145736 | tf_op jit(solution)/shard_map/ppermute | solution.py:527
  708.0 25.5 %collective-permute-start.42 = (bf16[128,2048]{1,0:T(8,128)(2,1)}, bf16[128,2048]{1,0:T(8,128)(2,1)}, u32[]{:S(2)}, u32[]{:S(2)}) collective-permute-start(bf16[128,2048]{1,0:T(8,128)(2,1)} %broadcast_select_fusion.10), channel_id=1, source_target_pairs={{0,1},{1,0},{2,3},{3,2},{4,5},{5,4},{6,7},{7,6},{8,9},{9,8},{10,11... | collective-permute-start | bytes 1572872 | tf_op jit(solution)/shard_map/ppermute | solution.py:527
  (94 other events, 672.3 us)
Sparse Core Ops, SparseCore 0:
  33.7 80.1 all-gather.4
  127.0 81.6 all-gather.8
  210.8 79.2 all-gather.6
  291.5 79.2 all-gather.10
  373.0 75.3 reduce-scatter.4
  450.6 77.2 reduce-scatter.8
  530.2 77.2 reduce-scatter.6
  609.8 77.7 reduce-scatter.10

commit v3 on v2

--- a/solution.py
+++ b/solution.py
@@ -12,8 +12,8 @@
 ROT = 32
 LANES = 128
 VMEM = 60 * 2**20
-COST = {"attention": 100, "attention_grad": 23, "mlp_act": 17, "mlp_pre": 14, "mixed_part": 16, "back_part": 22, "weight_grad": 100,
-        "heads_grad": 28, "project": 9, "line_step": 3, "assemble": 8, "assemble_heads": 14}
+COST = {"attention": 100, "attention_grad": 100, "mlp_act": 100, "mlp_pre": 60, "mixed_part": 60, "back_part": 100,
+        "weight_grad": 100, "heads_grad": 100, "project": 50, "assemble": 8, "assemble_heads": 14}
 
 
 def cost(units):
@@ -559,7 +559,7 @@
     )
 
 
-def assemble_heads(blocks, at, parts, width):
+def assemble_heads(blocks, at, parts, width, deps=()):
     rows, cols = blocks[0].shape
     hidden = cols - (parts + 1) * width
     if width % LANES:
@@ -592,7 +592,7 @@
     depth = 4 * rows
     return call(
         kernel,
-        (),
+        deps,
         (at, *blocks),
         grid=(cols // width,),
         in_specs=[pl.BlockSpec((rows, width), lambda j, at: (0, j))] * 8,
@@ -639,7 +639,7 @@
         self.half = keep.shape[2] // 2
 
     def first(self, *deps):
-        g = (tie(self.keep, *deps) if deps else self.keep) + self.got
+        g = self.keep + (tie(self.got, *deps) if deps else self.got)
         corner = g[1, 1]
         self.own, self.to_y, self.to_x = g[0, 0], g[0, 1], g[1, 0]
         self.got = flip(corner[: self.half], "near"), flip(corner[self.half :], "batch")
@@ -653,8 +653,9 @@
         self.got = flip(to_x, "near"), flip(to_y, "batch")
         return to_x, to_y
 
-    def result(self):
-        return self.own.astype(f32) + self.got[0].astype(f32) + self.got[1].astype(f32)
+    def result(self, *deps):
+        got = tuple(tie(a, *deps) for a in self.got) if deps else self.got
+        return self.own.astype(f32) + got[0].astype(f32) + got[1].astype(f32)
 
 
 def body(
@@ -688,12 +689,17 @@
         got = tie(got, *end) if end else got
         return jnp.concatenate([jnp.where(first, kept, got), jnp.where(first, got, kept)], 0)
 
-    def from_group(a, end=()):
+    def from_group(a):
         lo, hi = a[:shard], a[shard:]
-        got = flip(jnp.where(first, hi, lo), "near")
-        got = tie(got, *end) if end else got
-        kept = jnp.where(first, lo, hi)
-        return jnp.where(first, kept, got), jnp.where(first, got, kept)
+        send = jnp.where(first, hi, lo)
+        got = flip(send, "near")
+
+        def finish(*deps):
+            other = tie(got, *deps) if deps else got
+            kept = jnp.where(first, lo, hi)
+            return jnp.where(first, kept, other), jnp.where(first, other, kept)
+
+        return send, finish
 
     at = jnp.stack([y, core]).astype(jnp.int32)
 
@@ -710,37 +716,36 @@
     def gather_rows(group):
         return lax.all_gather(group, "line", axis=0, tiled=True)
 
-    n_0 = to_group(normed(0))
-    early = Gather(jnp.concatenate([qkv_weight.reshape(quarter, parts * width), dense_weight.T, up_weight], 1))
-    late = Gather(down_weight.T)
-    early.first(n_0)
-    early.second()
-    late.first(*early.corner)
-    qkv, dense_t, up = assemble_heads(early.third(), at, parts, width)
-    c_0 = to_group(cotangent[:, 0], early.corner, (dense_t,))
-    rows_n, rows_c = [gather_rows(n_0)], [gather_rows(c_0)]
-    late.second(dense_t)
-    bias_qkv = jnp.concatenate([qkv_bias, flip(qkv_bias, "near")], 1)
-    bias_up = jnp.concatenate([up_bias, flip(up_bias, "near")], 0)
     segment = jnp.where(first, segments[0], segments[1])
     place = jnp.where(first, positions[0], positions[1])
     tables = [rope_tables(place[s]) for s in range(seqs)]
+    n_0 = to_group(normed(0))
+    c_0 = to_group(cotangent[:, 0], (n_0,))
+    rows_n, rows_c = [gather_rows(n_0)], [gather_rows(c_0)]
+    early = Gather(jnp.concatenate([qkv_weight.reshape(quarter, parts * width), dense_weight.T, up_weight], 1))
+    late = Gather(down_weight.T)
+    early.first(c_0)
+    early.second(*tables[0], *tables[1])
+    late.first(*early.corner)
+    qkv, dense_t, up = assemble_heads(early.third(), at, parts, width)
+    bias_qkv = jnp.concatenate([qkv_bias, flip(qkv_bias, "near")], 1)
+    bias_up = jnp.concatenate([up_bias, flip(up_bias, "near")], 0)
 
     def scatter_rows(part):
         return lax.psum_scatter(part, "line", scatter_dimension=0, tiled=True)
 
-    proj = project(rows_n[0], qkv, f32, (c_0,))
-    n_1 = to_group(normed(1), (proj,), (proj,))
+    proj = project(rows_n[0], qkv, f32)
+    n_1 = to_group(normed(1), early.corner, (dense_t,))
+    late.second(proj)
+    attn_0, keep, log = attention(proj, bias_qkv, tables[0], segment[0], (n_1, *late.halves))
     rows_n.append(gather_rows(n_1))
-    attn_0, keep, log = attention(proj, bias_qkv, tables[0], segment[0], (n_1,))
-    late.second(attn_0)
-    c_1 = to_group(cotangent[:, 1], (attn_0,), (attn_0,))
-    rows_c.append(gather_rows(c_1))
-    act_0, slope = mlp_act(rows_n[0], up, bias_up, (*late.halves, c_1))
+    act_0, slope = mlp_act(rows_n[0], up, bias_up, (attn_0, *late.corner))
     down_t = assemble(late.third(), at, (act_0,))
     part = mixed_part(act_0, attn_0, down_t, dense_t)
     mixed_0 = scatter_rows(part)
-    grad_attn = project(rows_c[0], dense_t, bf16, (part,))
+    c_1 = to_group(cotangent[:, 1], (act_0,), (part,))
+    rows_c.append(gather_rows(c_1))
+    grad_attn = project(rows_c[0], dense_t, bf16, (part, c_1))
     dp_0, db_0 = attention_grad(keep, log, attn_0, grad_attn, tables[0], segment[0])
     pre_0, up_0 = mlp_pre(rows_c[0], down_t, slope, (dp_0,))
     part, back_0 = back_part(pre_0, dp_0, up, qkv, rows_n[0])
@@ -748,37 +753,42 @@
     proj = project(rows_n[1], qkv, f32, (part,))
     attn_1, keep, log = attention(proj, bias_qkv, tables[1], segment[1])
     act_1, slope = mlp_act(rows_n[1], up, bias_up, (attn_1,))
-    part = mixed_part(act_1, attn_1, down_t, dense_t)
+    pre_1, up_1 = mlp_pre(rows_c[1], down_t, slope)
+    grad_up = Scatter(*weight_grad(at, rows_n, (pre_0, pre_1)))
+    grad_down = Scatter(*weight_grad(at, rows_c, (act_0, act_1), (grad_up.keep,)))
+    sends = grad_up.first(grad_down.keep)
+    part = mixed_part(act_1, attn_1, down_t, dense_t, sends)
     mixed_1 = scatter_rows(part)
-    grad_attn = project(rows_c[1], dense_t, bf16, (part,))
+    send, finish = from_group(tie(mixed_0, part))
+    grad_attn = project(rows_c[1], dense_t, bf16, (part, send))
     dp_1, db_1 = attention_grad(keep, log, attn_1, grad_attn, tables[1], segment[1])
-    pre_1, up_1 = mlp_pre(rows_c[1], down_t, slope, (dp_1,))
-    part, back_1 = back_part(pre_1, dp_1, up, qkv, rows_n[1])
+    mixed_0 = finish(dp_1)
+    sends = (*grad_up.second(dp_1), *grad_down.first(dp_1))
+    part, back_1 = back_part(pre_1, dp_1, up, qkv, rows_n[1], (*sends, *mixed_0))
     back_sum_1 = scatter_rows(part)
-    grad_up = Scatter(*weight_grad(at, rows_n, (pre_0, pre_1), (part,)))
-    grad_down = Scatter(*weight_grad(at, rows_c, (act_0, act_1), (grad_up.keep,)))
-    mixed_0 = from_group(tie(mixed_0, grad_up.keep), (grad_down.keep,))
-    sends = (*grad_up.first(grad_down.keep), *mixed_0)
+    sends = grad_down.second(part)
+    grad_up = grad_up.result()
+    grad_heads = Scatter(*heads_grad(at, rows_n, (dp_0, dp_1), rows_c, (attn_0, attn_1), (*sends, grad_up)))
+    grad_down = grad_down.result(grad_heads.keep)
+    own_heads = grad_heads.first(tie(grad_down[:8, :LANES], units=200))
+    _, finish = from_group(tie(back_sum_0, *own_heads))
+    sends = grad_heads.second()
+    back_sum_0 = finish(*sends)
+    mixed_1 = from_group(tie(mixed_1, *back_sum_0))[1]()
+    grad_down = grad_down.T
+    grad_heads = grad_heads.result()
+    grad_qkv = grad_heads[:, : parts * width].reshape(quarter, parts, width)
+    grad_dense = grad_heads[:, parts * width :].T
     sum_qkv = (db_0 + db_1)[:parts].reshape(parts, 2, width)
     sum_up = (up_0 + up_1).reshape(2, hidden)
     out_bias = jnp.sum(cotangent, (0, 1, 2), dtype=f32)
     own, other = (jnp.concatenate([sum_qkv[:, d].reshape(-1), sum_up[d]]) for d in range(2))
     rest = jnp.concatenate([(back_0 + back_1).reshape(-1), out_bias])
     size = own.shape[0]
-    sums = jnp.concatenate([other, rest])
-    got = flip(sums, "near")
-    sends = (*sends, sums)
-    grad_heads = Scatter(*heads_grad(at, rows_n, (dp_0, dp_1), rows_c, (attn_0, attn_1), sends))
-    done = grad_heads.keep
-    got = tie(got, done)
-    sends = (*grad_up.second(done), *grad_down.first(done))
-    sums = tie(jnp.concatenate([own, rest]) + got, *sends)
-    sums = sums + flip(sums, "batch")
-    sends = (*grad_down.second(), *grad_heads.first(sums))
-    back_sum_0 = from_group(tie(back_sum_0, *sends))
-    sums = tie(sums, *sends)
-    sums = sums + flip(sums, "branch")
-    sends = grad_heads.second(sums)
+    sums = tie(jnp.concatenate([other, rest]), grad_heads, *mixed_1)
+    sums = jnp.concatenate([own, rest]) + flip(sums, "near")
+    for axis in FOLD:
+        sums = sums + flip(sums, axis)
     bias_sums, rest = sums[:size], sums[size:]
     reach = 1
     while reach < line_size:
@@ -787,15 +797,9 @@
     rest = rest.reshape(3, depth)
     shift_grad = rest[0]
     gain_grad = (rest[1] - ln_bias * shift_grad) / ln_gain
-    grad_up = grad_up.result()
-    grad_down = grad_down.result().T
-    grad_heads = grad_heads.result()
-    grad_qkv = grad_heads[:, : parts * width].reshape(quarter, parts, width)
-    grad_dense = grad_heads[:, parts * width :].T
 
     mixed, tokens_grad = [], []
-    mixed_1 = from_group(tie(mixed_1, grad_qkv, grad_dense, grad_up, grad_down))
-    back_sum_1 = from_group(tie(back_sum_1, *mixed_1))
+    back_sum_1 = from_group(tie(back_sum_1, *mixed_1, rest))[1]()
     for s, (m, g) in enumerate(((mixed_0, back_sum_0), (mixed_1, back_sum_1))):
         mixed.append((tokens[:, s].astype(f32) + jnp.stack(m, 0).astype(f32) + dense_bias + down_bias).astype(bf16))
         w = jnp.stack(g, 0).astype(f32) * ln_gain

time: 780 us -> 717 us (0.919)
  waiting for transfers between devices: 209 us -> 129 us
  local copies, waits for them, and re-layouts: 58.1 us -> 82 us
    ppermute x44, waiting for transfers between devices: 209 us -> 123 us  [flip(): return lax.ppermute(a, axis, SWAP)]
    another operation x12, local copies, waits for them, and re-layouts: 7.32 us -> 21.2 us  [rope_tables(): return tuple((jnp.tile(t, (1, LANES // HEAD_DIM)) for t in (cos, sa, sb)))]
    unnamed x154 -> x124, local copies, waits for them, and re-layouts: 26.4 us -> 34.5 us
  transfers between devices with their start and end apart: 54 -> 54, of which waited for: 23 -> 19; matrix products, arithmetic and copies ran while one was open for 15% -> 20% of each run, Pallas kernels for 46% -> 50%
where the time goes in v3:
time: 717 us; the launch traced here: 708 us
  Pallas kernels  357 us (50%)
  waiting for transfers between devices  129 us (18%)
  other arithmetic  82.9 us (12%)
  local copies, waits for them, and re-layouts  82 us (11%)
  starting transfers between devices  41.9 us (6%)
  between operations  15.6 us (2%)
    pallas_call x21, Pallas kernels, call(): pl.pallas_call(run, grid_spec=spec, out_shape=out_shape, compiler_params=...  357 us
    ppermute x44, waiting for transfers between devices, flip(): return lax.ppermute(a, axis, SWAP)  123 us
    ppermute x44, starting transfers between devices, flip(): return lax.ppermute(a, axis, SWAP)  40.7 us
    unnamed x124, local copies, waits for them, and re-layouts  34.5 us
    another operation x12, local copies, waits for them, and re-layouts, rope_tables(): return tuple((jnp.tile(t, (1, LANES // HEAD_DIM)) for t in (cos, sa, sb)))  21.2 us
    add x3, other arithmetic, first(): g = self.keep + (tie(self.got, *deps) if deps else self.got)  19 us
  transfers between devices with their start and end apart: 54, of which 19 were waited for; matrix products, arithmetic and copies ran while one was open for 20% of the time, Pallas kernels for 50%

profile of v3, /device:TPU:0, one launch (start us, length us, event | category | flops | bytes accessed | tf_op | source)
XLA Modules:
  0.0 708.4 jit_solution(8388590941777177160)
XLA Ops:
  14.1 11.9 %collective-permute-done = bf16[128,2048]{1,0:T(8,128)(2,1)S(1)} collective-permute-done((bf16[128,2048]{1,0:T(8,128)(2,1)S(1)}, bf16[128,2048]{1,0:T(8,128)(2,1)S(1)}, u32[]{:S(2)}, u32[]{:S(2)}) %collective-permute-start) | collective-permute-done | bytes 524320 | tf_op jit(solution)/shard_map/ppermute | solution.py:527
  70.9 21.0 %collective-permute-done.5.refs_0_ = bf16[512,2048]{1,0:T(8,128)(2,1)} collective-permute-done((bf16[512,2048]{1,0:T(8,128)(2,1)}, bf16[512,2048]{1,0:T(8,128)(2,1)}, u32[]{:S(2)}, u32[]{:S(2)}) %collective-permute-start.5) | collective-permute-done | bytes 2097184 | tf_op jit(solution)/shard_map/ppermute | solution.py:527
  97.9 19.6 %collective-permute-done.7.refs_1_ = bf16[256,2048]{1,0:T(8,128)(2,1)} collective-permute-done((bf16[256,2048]{1,0:T(8,128)(2,1)}, bf16[256,2048]{1,0:T(8,128)(2,1)}, u32[]{:S(2)}, u32[]{:S(2)}) %collective-permute-start.7) | collective-permute-done | bytes 1048608 | tf_op jit(solution)/shard_map/ppermute | solution.py:527
  137.0 14.6 %assemble_heads.1 = (bf16[2048,1536]{1,0:T(8,128)(2,1)}, bf16[2048,512]{1,0:T(8,128)(2,1)}, bf16[2,2048,1024]{2,1,0:T(8,128)(2,1)}) custom-call(s32[2]{0:T(128)} %pad_add_fusion.refs_0_, bf16[512,2048]{1,0:T(8,128)(2,1)} %pad_maximum_fusion.1.refs_1_, bf16[512,2048]{1,0:T(8,128)(2,1)} %collective-permute-done.1.refs_2_, bf16[512,2048]{1,0:T(8,128)(2,1)} %tie.30.refs_3_, ...), custom_call_target="tpu_custom_call" | custom-call | flops 3500000000 | bytes 3500001 | tf_op jit(solution)/shard_map/assemble_heads/pallas_call | solution.py:52
  154.4 11.9 %project.4.refs_1_.refs_0_.refs_2_ = f32[1024,1536]{1,0:T(8,128)} custom-call(bf16[1024,2048]{1,0:T(8,128)(2,1)} %all-gather.5.cloned.1.call-done.refs_0_.refs_4_.refs_1_, bf16[2048,1536]{1,0:T(8,128)(2,1)} %get-tuple-element.44.refs_1_.refs_3_), custom_call_target="tpu_custom_call" | custom-call | flops 12499999744 | bytes 12500001 | tf_op jit(solution)/shard_map/project/pallas_call | solution.py:52
  173.3 17.3 %attention.2 = (bf16[1024,512]{1,0:T(8,128)(2,1)}, bf16[3,1024,512]{2,1,0:T(8,128)(2,1)}, f32[32,1024]{1,0:T(8,128)}) custom-call(f32[1024,1536]{1,0:T(8,128)} %project.4.refs_1_.refs_0_.refs_2_, f32[1024,1536]{1,0:T(8,128)} %project.4.refs_1_.refs_0_.refs_2_, f32[1024,1536]{1,0:T(8,128)} %project.4.refs_1_.refs_0_.refs_2_, f32[1,1536]{1,0:T(1,128)} %bitcast.244, ...), custom_call_target="tpu_custom_call" | custom-call | flops 24999999488 | bytes 25000000 | tf_op jit(solution)/shard_map/attention/pallas_call | solution.py:52
  192.5 17.5 %mlp_act.2 = (bf16[1024,2048]{1,0:T(8,128)(2,1)}, bf16[1024,2048]{1,0:T(8,128)(2,1)}) custom-call(bf16[1024,2048]{1,0:T(8,128)(2,1)} %all-gather.5.cloned.1.call-done.refs_0_.refs_4_.refs_1_, bf16[2,2048,1024]{2,1,0:T(8,128)(2,1)} %get-tuple-element.43.refs_1_.refs_2_, f32[1,2048]{1,0:T(1,128)} %bitcast.242, ...), custom_call_target="tpu_custom_call" | custom-call | flops 24999999488 | bytes 25000000 | tf_op jit(solution)/shard_map/mlp_act/pallas_call | solution.py:52
  210.4 7.8 %assemble.1.refs_2_.refs_1_ = bf16[2,2048,1024]{2,1,0:T(8,128)(2,1)} custom-call(s32[2]{0:T(128)} %pad_add_fusion.refs_0_, bf16[512,1024]{1,0:T(8,128)(2,1)} %bitcast.217, bf16[512,1024]{1,0:T(8,128)(2,1)} %collective-permute-done.17.refs_2_, bf16[512,1024]{1,0:T(8,128)(2,1)} %tie.36.refs_3_, bf16[512,1024]{1,0:T(8,128)(2,1)} %collective-permute-done.18.refs_4_, ...), custom_call_target="tpu_custom_call" | custom-call | flops 2000000000 | bytes 2000001 | tf_op jit(solution)/shard_map/assemble/pallas_call | solution.py:52
  218.2 16.0 %mixed_part.2.refs_1_.refs_2_ = bf16[1024,2048]{1,0:T(8,128)(2,1)} custom-call(bf16[1024,2048]{1,0:T(8,128)(2,1)} %get-tuple-element.47.refs_9_.refs_0_.refs_1_.refs_3_, bf16[1024,512]{1,0:T(8,128)(2,1)} %get-tuple-element.46.refs_3_.refs_1_.refs_2_.refs_7_, bf16[2,2048,1024]{2,1,0:T(8,128)(2,1)} %assemble.1.refs_2_.refs_1_, ...), custom_call_target="tpu_custom_call" | custom-call | flops 15000000512 | bytes 15000001 | tf_op jit(solution)/shard_map/mixed_part/pallas_call | solution.py:52
  238.3 5.9 project.5.refs_3_
  244.2 22.7 %attention_grad.2 = (bf16[3,1024,512]{2,1,0:T(8,128)(2,1)}, f32[8,512]{1,0:T(8,128)}) custom-call(bf16[3,1024,512]{2,1,0:T(8,128)(2,1)} %get-tuple-element.49.refs_0_, f32[32,1024]{1,0:T(8,128)} %get-tuple-element.50.refs_1_, bf16[1024,512]{1,0:T(8,128)(2,1)} %get-tuple-element.46.refs_3_.refs_1_.refs_2_.refs_7_, bf16[1024,512]{1,0:T(8,128)(2,1)} %project.5.refs_3_, ...), custom_call_target="tpu_custom_call" | custom-call | flops 24999999488 | bytes 25000000 | tf_op jit(solution)/shard_map/attention_grad/pallas_call | solution.py:52
  266.9 14.0 %mlp_pre.2 = (bf16[1024,2048]{1,0:T(8,128)(2,1)}, f32[8,2048]{1,0:T(8,128)}) custom-call(bf16[1024,2048]{1,0:T(8,128)(2,1)} %all-gather.9.cloned.1.call-done.refs_0_.refs_1_.refs_5_, bf16[2,2048,1024]{2,1,0:T(8,128)(2,1)} %assemble.1.refs_2_.refs_1_, bf16[1024,2048]{1,0:T(8,128)(2,1)} %get-tuple-element.48.refs_2_, ...), custom_call_target="tpu_custom_call" | custom-call | flops 15000000512 | bytes 15000001 | tf_op jit(solution)/shard_map/mlp_pre/pallas_call | solution.py:52
  280.9 22.3 %back_part.2 = (bf16[1024,2048]{1,0:T(8,128)(2,1)}, f32[8,2048]{1,0:T(8,128)}) custom-call(bf16[1024,2048]{1,0:T(8,128)(2,1)} %get-tuple-element.52.refs_0_.refs_3_, bf16[3,1024,512]{2,1,0:T(8,128)(2,1)} %get-tuple-element.51.refs_3_.refs_1_, bf16[2,2048,1024]{2,1,0:T(8,128)(2,1)} %get-tuple-element.43.refs_1_.refs_2_, ...), custom_call_target="tpu_custom_call" | custom-call | flops 24999999488 | bytes 25000000 | tf_op jit(solution)/shard_map/back_part/pallas_call | solution.py:52
  303.5 12.0 %project.6.refs_0_.refs_1_.refs_2_ = f32[1024,1536]{1,0:T(8,128)} custom-call(bf16[1024,2048]{1,0:T(8,128)(2,1)} %all-gather.7.cloned.1.call-done.refs_0_.refs_2_.refs_4_, bf16[2048,1536]{1,0:T(8,128)(2,1)} %get-tuple-element.44.refs_1_.refs_3_, bf16[1024,2048]{1,0:T(8,128)(2,1)} %get-tuple-element.53.refs_2_), custom_call_target="tpu_custom_call" | custom-call | flops 12499999744 | bytes 12500001 | tf_op jit(solution)/shard_map/project/pallas_call | solution.py:52
  315.5 17.3 %attention.3 = (bf16[1024,512]{1,0:T(8,128)(2,1)}, bf16[3,1024,512]{2,1,0:T(8,128)(2,1)}, f32[32,1024]{1,0:T(8,128)}) custom-call(f32[1024,1536]{1,0:T(8,128)} %project.6.refs_0_.refs_1_.refs_2_, f32[1024,1536]{1,0:T(8,128)} %project.6.refs_0_.refs_1_.refs_2_, f32[1024,1536]{1,0:T(8,128)} %project.6.refs_0_.refs_1_.refs_2_, f32[1,1536]{1,0:T(1,128)} %bitcast.247, ...), custom_call_target="tpu_custom_call" | custom-call | flops 24999999488 | bytes 25000000 | tf_op jit(solution)/shard_map/attention/pallas_call | solution.py:52
  332.8 17.6 %mlp_act.3 = (bf16[1024,2048]{1,0:T(8,128)(2,1)}, bf16[1024,2048]{1,0:T(8,128)(2,1)}) custom-call(bf16[1024,2048]{1,0:T(8,128)(2,1)} %all-gather.7.cloned.1.call-done.refs_0_.refs_2_.refs_4_, bf16[2,2048,1024]{2,1,0:T(8,128)(2,1)} %get-tuple-element.43.refs_1_.refs_2_, f32[1,2048]{1,0:T(1,128)} %bitcast.243, ...), custom_call_target="tpu_custom_call" | custom-call | flops 24999999488 | bytes 25000000 | tf_op jit(solution)/shard_map/mlp_act/pallas_call | solution.py:52
  353.4 14.2 %mlp_pre.3 = (bf16[1024,2048]{1,0:T(8,128)(2,1)}, f32[8,2048]{1,0:T(8,128)}) custom-call(bf16[1024,2048]{1,0:T(8,128)(2,1)} %all-gather.11.cloned.1.call-done.refs_0_.refs_2_.refs_6_, bf16[2,2048,1024]{2,1,0:T(8,128)(2,1)} %assemble.1.refs_2_.refs_1_, bf16[1024,2048]{1,0:T(8,128)(2,1)} %get-tuple-element.56.refs_2_), custom_call_target="tpu_custom_call" | custom-call | flops 15000000512 | bytes 15000001 | tf_op jit(solution)/shard_map/mlp_pre/pallas_call | solution.py:52
  367.6 25.6 %weight_grad.2 = (bf16[2,2,512,1024]{3,2,1,0:T(8,128)(2,1)}, bf16[2,2,512,1024]{3,2,1,0:T(8,128)(2,1)}) custom-call(s32[2]{0:T(128)} %pad_add_fusion.refs_0_, bf16[1024,2048]{1,0:T(8,128)(2,1)} %all-gather.5.cloned.1.call-done.refs_0_.refs_4_.refs_1_, bf16[1024,2048]{1,0:T(8,128)(2,1)} %all-gather.7.cloned.1.call-done.refs_0_.refs_2_.refs_4_, ...), custom_call_target="tpu_custom_call" | custom-call | flops 24999999488 | bytes 25000000 | tf_op jit(solution)/shard_map/weight_grad/pallas_call | solution.py:52
  394.2 25.0 %weight_grad.3 = (bf16[2,2,512,1024]{3,2,1,0:T(8,128)(2,1)}, bf16[2,2,512,1024]{3,2,1,0:T(8,128)(2,1)}) custom-call(s32[2]{0:T(128)} %pad_add_fusion.refs_0_, bf16[1024,2048]{1,0:T(8,128)(2,1)} %all-gather.9.cloned.1.call-done.refs_0_.refs_1_.refs_5_, bf16[1024,2048]{1,0:T(8,128)(2,1)} %all-gather.11.cloned.1.call-done.refs_0_.refs_2_.refs_6_, ...), custom_call_target="tpu_custom_call" | custom-call | flops 24999999488 | bytes 25000000 | tf_op jit(solution)/shard_map/weight_grad/pallas_call | solution.py:52
  429.8 16.0 %mixed_part.3.refs_1_.refs_2_ = bf16[1024,2048]{1,0:T(8,128)(2,1)} custom-call(bf16[1024,2048]{1,0:T(8,128)(2,1)} %get-tuple-element.55.refs_4_.refs_0_, bf16[1024,512]{1,0:T(8,128)(2,1)} %get-tuple-element.54.refs_3_.refs_1_.refs_2_.refs_8_, bf16[2,2048,1024]{2,1,0:T(8,128)(2,1)} %assemble.1.refs_2_.refs_1_, ...), custom_call_target="tpu_custom_call" | custom-call | flops 15000000512 | bytes 15000001 | tf_op jit(solution)/shard_map/mixed_part/pallas_call | solution.py:52
  449.6 6.0 project.7.refs_3_
  455.6 22.7 %attention_grad.3 = (bf16[3,1024,512]{2,1,0:T(8,128)(2,1)}, f32[8,512]{1,0:T(8,128)}) custom-call(bf16[3,1024,512]{2,1,0:T(8,128)(2,1)} %get-tuple-element.61.refs_0_, f32[32,1024]{1,0:T(8,128)} %get-tuple-element.62.refs_1_, bf16[1024,512]{1,0:T(8,128)(2,1)} %get-tuple-element.54.refs_3_.refs_1_.refs_2_.refs_8_, bf16[1024,512]{1,0:T(8,128)(2,1)} %project.7.refs_3_, ...), custom_call_target="tpu_custom_call" | custom-call | flops 24999999488 | bytes 25000000 | tf_op jit(solution)/shard_map/attention_grad/pallas_call | solution.py:52
  479.0 7.8 %add.171 = bf16[2,2,512,1024]{3,2,1,0:T(8,128)(2,1)} add(bf16[2,2,512,1024]{3,2,1,0:T(8,128)(2,1)} %get-tuple-element.60.refs_1_, bf16[2,2,512,1024]{3,2,1,0:T(8,128)(2,1)} %tie.42) | non-fusion elementwise | flops 2097152 | bytes 12582912 | tf_op jit(solution)/shard_map/add | solution.py:642
  495.8 8.6 %collective-permute-done.27.refs_0_ = bf16[256,1024]{1,0:T(8,128)(2,1)} collective-permute-done((bf16[256,1024]{1,0:T(8,128)(2,1)S(1)}, bf16[256,1024]{1,0:T(8,128)(2,1)}, u32[]{:S(2)}, u32[]{:S(2)}) %collective-permute-start.27) | collective-permute-done | bytes 524320 | tf_op jit(solution)/shard_map/ppermute | solution.py:527
  514.8 22.0 %back_part.3 = (bf16[1024,2048]{1,0:T(8,128)(2,1)}, f32[8,2048]{1,0:T(8,128)}) custom-call(bf16[1024,2048]{1,0:T(8,128)(2,1)} %get-tuple-element.57.refs_4_.refs_0_, bf16[3,1024,512]{2,1,0:T(8,128)(2,1)} %get-tuple-element.63.refs_1_.refs_4_, bf16[2,2048,1024]{2,1,0:T(8,128)(2,1)} %get-tuple-element.43.refs_1_.refs_2_, ...), custom_call_target="tpu_custom_call" | custom-call | flops 24999999488 | bytes 25000000 | tf_op jit(solution)/shard_map/back_part/pallas_call | solution.py:52
  547.4 28.8 %heads_grad.1 = (bf16[2,2,512,1024]{3,2,1,0:T(8,128)(2,1)}, bf16[2,2,512,1024]{3,2,1,0:T(8,128)(2,1)}) custom-call(s32[2]{0:T(128)} %pad_add_fusion.refs_0_, bf16[1024,2048]{1,0:T(8,128)(2,1)} %all-gather.5.cloned.1.call-done.refs_0_.refs_4_.refs_1_, bf16[1024,2048]{1,0:T(8,128)(2,1)} %all-gather.7.cloned.1.call-done.refs_0_.refs_2_.refs_4_, ...), custom_call_target="tpu_custom_call" | custom-call | flops 24999999488 | bytes 25000000 | tf_op jit(solution)/shard_map/heads_grad/pallas_call | solution.py:52
  582.0 6.8 collective-permute-done.31.refs_0_
  600.7 8.8 %collective-permute-done.36 = bf16[256,1024]{1,0:T(8,128)(2,1)S(1)} collective-permute-done((bf16[256,1024]{1,0:T(8,128)(2,1)S(1)}, bf16[256,1024]{1,0:T(8,128)(2,1)S(1)}, u32[]{:S(2)}, u32[]{:S(2)}) %collective-permute-start.36) | collective-permute-done | bytes 524320 | tf_op jit(solution)/shard_map/ppermute | solution.py:527
  614.2 6.7 collective-permute-done.34.refs_0_
  627.4 15.9 %collective-permute-done.38 = bf16[512,1024]{1,0:T(8,128)(2,1)} collective-permute-done((bf16[512,1024]{1,0:T(8,128)(2,1)S(1)}, bf16[512,1024]{1,0:T(8,128)(2,1)}, u32[]{:S(2)}, u32[]{:S(2)}) %collective-permute-start.38) | collective-permute-done | bytes 1048608 | tf_op jit(solution)/shard_map/ppermute | solution.py:527
  647.1 6.6 collective-permute-done.37
  685.1 7.3 %collective-permute-done.45 = bf16[128,2048]{1,0:T(8,128)(2,1)} collective-permute-done((bf16[128,2048]{1,0:T(8,128)(2,1)}, bf16[128,2048]{1,0:T(8,128)(2,1)}, u32[]{:S(2)}, u32[]{:S(2)}) %collective-permute-start.45) | collective-permute-done | bytes 524320 | tf_op jit(solution)/shard_map/ppermute | solution.py:527
  (375 shorter events, 214.6 us)
Async XLA Ops:
  7.2 147.2 %all-gather.5.cloned.1.call-start = ((), (), s32[]{:S(2)}) async-start(), calls=%async_computation.4 | async-start | bytes 5242880 | tf_op jit(solution)/shard_map/all_gather | solution.py:717
  27.2 211.0 %all-gather.9.cloned.1.call-start = ((), (), s32[]{:S(2)}) async-start(), calls=%async_computation.7 | async-start | bytes 5242880 | tf_op jit(solution)/shard_map/all_gather | solution.py:717
  45.2 46.7 %collective-permute-start.5 = (bf16[512,2048]{1,0:T(8,128)(2,1)}, bf16[512,2048]{1,0:T(8,128)(2,1)}, u32[]{:S(2)}, u32[]{:S(2)}) collective-permute-start(bf16[512,2048]{1,0:T(8,128)(2,1)} %tie.29), channel_id=1, source_target_pairs={{0,16},{16,0},{1,17},{17,1},{2,18},{18,2},{3,19},{19,3},{4,20},{20... | collective-permute-start | bytes 6291464 | tf_op jit(solution)/shard_map/ppermute | solution.py:527
  46.7 47.9 %collective-permute-start.3 = (bf16[512,2048]{1,0:T(8,128)(2,1)}, bf16[512,2048]{1,0:T(8,128)(2,1)}, u32[]{:S(2)}, u32[]{:S(2)}) collective-permute-start(bf16[512,2048]{1,0:T(8,128)(2,1)} %tie.29), channel_id=1, source_target_pairs={{0,1},{1,0},{2,3},{3,2},{4,5},{5,4},{6,7},{7,6},{8,9},{9,8},{10,11... | collective-permute-start | bytes 6291464 | tf_op jit(solution)/shard_map/ppermute | solution.py:527
  47.8 255.7 %all-gather.7.cloned.1.call-start = ((), (), s32[]{:S(2)}) async-start(), calls=%async_computation.6 | async-start | bytes 5242880 | tf_op jit(solution)/shard_map/all_gather | solution.py:717
  95.9 24.0 %collective-permute-start.8 = (bf16[256,2048]{1,0:T(8,128)(2,1)S(1)}, bf16[256,2048]{1,0:T(8,128)(2,1)S(1)}, u32[]{:S(2)}, u32[]{:S(2)}) collective-permute-start(bf16[256,2048]{1,0:T(8,128)(2,1)S(1)} %slice.448), channel_id=1, source_target_pairs={{0,16},{16,0},{1,17},{17,1},{2,18},{18,2},{3,19},{19,3},{4,20},{20... | collective-permute-start | bytes 3145736 | tf_op jit(solution)/shard_map/ppermute | solution.py:527
  97.4 37.5 %collective-permute-start.1 = (bf16[512,2048]{1,0:T(8,128)(2,1)}, bf16[512,2048]{1,0:T(8,128)(2,1)}, u32[]{:S(2)}, u32[]{:S(2)}) collective-permute-start(bf16[512,2048]{1,0:T(8,128)(2,1)} %pad_maximum_fusion.1.refs_1_), channel_id=1, source_target_pairs={{0,8},{8,0},{1,9},{9,1},{2,10},{10,2},{3,11},{11,3},{4,12},{12,4},... | collective-permute-start | bytes 6291464 | tf_op jit(solution)/shard_map/ppermute | solution.py:527
  97.4 37.5 %collective-permute-start.6 = (bf16[512,2048]{1,0:T(8,128)(2,1)}, bf16[512,2048]{1,0:T(8,128)(2,1)}, u32[]{:S(2)}, u32[]{:S(2)}) collective-permute-start(bf16[512,2048]{1,0:T(8,128)(2,1)} %tie.31.refs_5_), channel_id=1, source_target_pairs={{0,8},{8,0},{1,9},{9,1},{2,10},{10,2},{3,11},{11,3},{4,12},{12,4},... | collective-permute-start | bytes 6291464 | tf_op jit(solution)/shard_map/ppermute | solution.py:527
  97.9 37.5 %collective-permute-start.4 = (bf16[512,2048]{1,0:T(8,128)(2,1)}, bf16[512,2048]{1,0:T(8,128)(2,1)}, u32[]{:S(2)}, u32[]{:S(2)}) collective-permute-start(bf16[512,2048]{1,0:T(8,128)(2,1)} %tie.30.refs_3_), channel_id=1, source_target_pairs={{0,8},{8,0},{1,9},{9,1},{2,10},{10,2},{3,11},{11,3},{4,12},{12,4},... | collective-permute-start | bytes 6291464 | tf_op jit(solution)/shard_map/ppermute | solution.py:527
  134.9 75.5 %collective-permute-start.17 = (bf16[512,1024]{1,0:T(8,128)(2,1)}, bf16[512,1024]{1,0:T(8,128)(2,1)}, u32[]{:S(2)}, u32[]{:S(2)}) collective-permute-start(bf16[512,1024]{1,0:T(8,128)(2,1)} %bitcast.216), channel_id=1, source_target_pairs={{0,8},{8,0},{1,9},{9,1},{2,10},{10,2},{3,11},{11,3},{4,12},{12,4},... | collective-permute-start | bytes 3145736 | tf_op jit(solution)/shard_map/ppermute | solution.py:527
  134.9 33.3 %collective-permute-start.14 = (bf16[512,1024]{1,0:T(8,128)(2,1)}, bf16[512,1024]{1,0:T(8,128)(2,1)}, u32[]{:S(2)}, u32[]{:S(2)}) collective-permute-start(bf16[512,1024]{1,0:T(8,128)(2,1)} %tie.34), channel_id=1, source_target_pairs={{0,1},{1,0},{2,3},{3,2},{4,5},{5,4},{6,7},{7,6},{8,9},{9,8},{10,11... | collective-permute-start | bytes 3145736 | tf_op jit(solution)/shard_map/ppermute | solution.py:527
  135.4 30.9 %collective-permute-start.13 = (bf16[512,1024]{1,0:T(8,128)(2,1)}, bf16[512,1024]{1,0:T(8,128)(2,1)}, u32[]{:S(2)}, u32[]{:S(2)}) collective-permute-start(bf16[512,1024]{1,0:T(8,128)(2,1)} %tie.34), channel_id=1, source_target_pairs={{0,16},{16,0},{1,17},{17,1},{2,18},{18,2},{3,19},{19,3},{4,20},{20... | collective-permute-start | bytes 3145736 | tf_op jit(solution)/shard_map/ppermute | solution.py:527
  153.9 199.5 %all-gather.11.cloned.1.call-start = ((), (), s32[]{:S(2)}) async-start(), calls=%async_computation.8 | async-start | bytes 5242880 | tf_op jit(solution)/shard_map/all_gather | solution.py:717
  167.5 43.0 %collective-permute-start.19 = (bf16[512,1024]{1,0:T(8,128)(2,1)}, bf16[512,1024]{1,0:T(8,128)(2,1)}, u32[]{:S(2)}, u32[]{:S(2)}) collective-permute-start(bf16[512,1024]{1,0:T(8,128)(2,1)} %tie.35.refs_5_), channel_id=1, source_target_pairs={{0,8},{8,0},{1,9},{9,1},{2,10},{10,2},{3,11},{11,3},{4,12},{12,4},... | collective-permute-start | bytes 3145736 | tf_op jit(solution)/shard_map/ppermute | solution.py:527
  170.1 40.3 %collective-permute-start.18 = (bf16[512,1024]{1,0:T(8,128)(2,1)}, bf16[512,1024]{1,0:T(8,128)(2,1)}, u32[]{:S(2)}, u32[]{:S(2)}) collective-permute-start(bf16[512,1024]{1,0:T(8,128)(2,1)} %tie.36.refs_3_), channel_id=1, source_target_pairs={{0,8},{8,0},{1,9},{9,1},{2,10},{10,2},{3,11},{11,3},{4,12},{12,4},... | collective-permute-start | bytes 3145736 | tf_op jit(solution)/shard_map/ppermute | solution.py:527
  210.0 24.2 %collective-permute-start.21 = (bf16[128,2048]{1,0:T(8,128)(2,1)}, bf16[128,2048]{1,0:T(8,128)(2,1)}, u32[]{:S(2)}, u32[]{:S(2)}) collective-permute-start(bf16[128,2048]{1,0:T(8,128)(2,1)} %tie.37), channel_id=1, source_target_pairs={{0,1},{1,0},{2,3},{3,2},{4,5},{5,4},{6,7},{7,6},{8,9},{9,8},{10,11... | collective-permute-start | bytes 1572872 | tf_op jit(solution)/shard_map/ppermute | solution.py:527
  236.4 209.5 %reduce-scatter.5.cloned.1.call-start = ((), (), s32[]{:S(2)}) async-start(), calls=%async_computation.5 | async-start | bytes 5242880 | tf_op jit(solution)/shard_map/reduce_scatter | solution.py:735
  237.0 361.8 %reduce-scatter.9.cloned.1.call-start = ((), (), s32[]{:S(2)}) async-start(), calls=%async_computation.10 | async-start | bytes 5242880 | tf_op jit(solution)/shard_map/reduce_scatter | solution.py:735
  303.2 319.8 %reduce-scatter.7.cloned.1.call-start = ((), (), s32[]{:S(2)}) async-start(), calls=%async_computation.9 | async-start | bytes 5242880 | tf_op jit(solution)/shard_map/reduce_scatter | solution.py:735
  393.2 28.0 %collective-permute-start.22 = (bf16[2,2,512,1024]{3,2,1,0:T(8,128)(2,1)}, bf16[2,2,512,1024]{3,2,1,0:T(8,128)(2,1)}, u32[]{:S(2)}, u32[]{:S(2)}) collective-permute-start(bf16[2,2,512,1024]{3,2,1,0:T(8,128)(2,1)} %get-tuple-element.59), channel_id=1, source_target_pairs={{0,8},{8,0},{1,9},{9,1},{2,10},{10,2},{3,11},{11,3},{4,12},{12,4},... | collective-permute-start | bytes 12582920 | tf_op jit(solution)/shard_map/ppermute | solution.py:527
  419.2 59.1 %collective-permute-start.24 = (bf16[2,2,512,1024]{3,2,1,0:T(8,128)(2,1)}, bf16[2,2,512,1024]{3,2,1,0:T(8,128)(2,1)}, u32[]{:S(2)}, u32[]{:S(2)}) collective-permute-start(bf16[2,2,512,1024]{3,2,1,0:T(8,128)(2,1)} %get-tuple-element.64), channel_id=1, source_target_pairs={{0,8},{8,0},{1,9},{9,1},{2,10},{10,2},{3,11},{11,3},{4,12},{12,4},... | collective-permute-start | bytes 12582920 | tf_op jit(solution)/shard_map/ppermute | solution.py:527
  445.8 230.1 %reduce-scatter.11.cloned.1.call-start = ((), (), s32[]{:S(2)}) async-start(), calls=%async_computation.11 | async-start | bytes 5242880 | tf_op jit(solution)/shard_map/reduce_scatter | solution.py:735
  448.0 63.9 %collective-permute-start.23 = (bf16[128,2048]{1,0:T(8,128)(2,1)}, bf16[128,2048]{1,0:T(8,128)(2,1)S(1)}, u32[]{:S(2)}, u32[]{:S(2)}) collective-permute-start(bf16[128,2048]{1,0:T(8,128)(2,1)} %broadcast_select_fusion.18.refs_3_), channel_id=1, source_target_pairs={{0,1},{1,0},{2,3},{3,2},{4,5},{5,4},{6,7},{7,6},{8,9},{9,8},{10,11... | collective-permute-start | bytes 1572872 | tf_op jit(solution)/shard_map/ppermute | solution.py:527
  492.7 44.2 %collective-permute-start.28 = (bf16[256,1024]{1,0:T(8,128)(2,1)}, bf16[256,1024]{1,0:T(8,128)(2,1)S(1)}, u32[]{:S(2)}, u32[]{:S(2)}) collective-permute-start(bf16[256,1024]{1,0:T(8,128)(2,1)} %get-tuple-element.122), channel_id=1, source_target_pairs={{0,1},{1,0},{2,3},{3,2},{4,5},{5,4},{6,7},{7,6},{8,9},{9,8},{10,11... | collective-permute-start | bytes 1572872 | tf_op jit(solution)/shard_map/ppermute | solution.py:527
  494.2 43.5 %collective-permute-start.25 = (bf16[256,1024]{1,0:T(8,128)(2,1)}, bf16[256,1024]{1,0:T(8,128)(2,1)S(1)}, u32[]{:S(2)}, u32[]{:S(2)}) collective-permute-start(bf16[256,1024]{1,0:T(8,128)(2,1)} %get-tuple-element.124), channel_id=1, source_target_pairs={{0,16},{16,0},{1,17},{17,1},{2,18},{18,2},{3,19},{19,3},{4,20},{20... | collective-permute-start | bytes 1572872 | tf_op jit(solution)/shard_map/ppermute | solution.py:527
  507.8 35.8 %collective-permute-start.29 = (bf16[512,1024]{1,0:T(8,128)(2,1)}, bf16[512,1024]{1,0:T(8,128)(2,1)}, u32[]{:S(2)}, u32[]{:S(2)}) collective-permute-start(bf16[512,1024]{1,0:T(8,128)(2,1)} %pad_maximum_fusion.7.refs_5_), channel_id=1, source_target_pairs={{0,1},{1,0},{2,3},{3,2},{4,5},{5,4},{6,7},{7,6},{8,9},{9,8},{10,11... | collective-permute-start | bytes 3145736 | tf_op jit(solution)/shard_map/ppermute | solution.py:527
  510.4 33.2 %collective-permute-start.30 = (bf16[512,1024]{1,0:T(8,128)(2,1)}, bf16[512,1024]{1,0:T(8,128)(2,1)}, u32[]{:S(2)}, u32[]{:S(2)}) collective-permute-start(bf16[512,1024]{1,0:T(8,128)(2,1)} %pad_maximum_fusion.8.refs_6_), channel_id=1, source_target_pairs={{0,16},{16,0},{1,17},{17,1},{2,18},{18,2},{3,19},{19,3},{4,20},{20... | collective-permute-start | bytes 3145736 | tf_op jit(solution)/shard_map/ppermute | solution.py:527
  541.5 35.7 %collective-permute-start.32 = (bf16[512,1024]{1,0:T(8,128)(2,1)}, bf16[512,1024]{1,0:T(8,128)(2,1)S(1)}, u32[]{:S(2)}, u32[]{:S(2)}) collective-permute-start(bf16[512,1024]{1,0:T(8,128)(2,1)} %pad_maximum_fusion.9.refs_9_), channel_id=1, source_target_pairs={{0,1},{1,0},{2,3},{3,2},{4,5},{5,4},{6,7},{7,6},{8,9},{9,8},{10,11... | collective-permute-start | bytes 3145736 | tf_op jit(solution)/shard_map/ppermute | solution.py:527
  543.1 33.1 %collective-permute-start.33 = (bf16[512,1024]{1,0:T(8,128)(2,1)}, bf16[512,1024]{1,0:T(8,128)(2,1)S(1)}, u32[]{:S(2)}, u32[]{:S(2)}) collective-permute-start(bf16[512,1024]{1,0:T(8,128)(2,1)} %pad_maximum_fusion.10.refs_10_), channel_id=1, source_target_pairs={{0,16},{16,0},{1,17},{17,1},{2,18},{18,2},{3,19},{19,3},{4,20},{20... | collective-permute-start | bytes 3145736 | tf_op jit(solution)/shard_map/ppermute | solution.py:527
  611.4 31.9 %collective-permute-start.38 = (bf16[512,1024]{1,0:T(8,128)(2,1)S(1)}, bf16[512,1024]{1,0:T(8,128)(2,1)}, u32[]{:S(2)}, u32[]{:S(2)}) collective-permute-start(bf16[512,1024]{1,0:T(8,128)(2,1)S(1)} %pad_maximum_fusion.11.refs_1_), channel_id=1, source_target_pairs={{0,1},{1,0},{2,3},{3,2},{4,5},{5,4},{6,7},{7,6},{8,9},{9,8},{10,11... | collective-permute-start | bytes 3145736 | tf_op jit(solution)/shard_map/ppermute | solution.py:527
  612.6 30.7 %collective-permute-start.39 = (bf16[512,1024]{1,0:T(8,128)(2,1)S(1)}, bf16[512,1024]{1,0:T(8,128)(2,1)}, u32[]{:S(2)}, u32[]{:S(2)}) collective-permute-start(bf16[512,1024]{1,0:T(8,128)(2,1)S(1)} %pad_maximum_fusion.12.refs_2_), channel_id=1, source_target_pairs={{0,16},{16,0},{1,17},{17,1},{2,18},{18,2},{3,19},{19,3},{4,20},{20... | collective-permute-start | bytes 3145736 | tf_op jit(solution)/shard_map/ppermute | solution.py:527
  624.3 29.4 %collective-permute-start.37 = (bf16[128,2048]{1,0:T(8,128)(2,1)S(1)}, bf16[128,2048]{1,0:T(8,128)(2,1)S(1)}, u32[]{:S(2)}, u32[]{:S(2)}) collective-permute-start(bf16[128,2048]{1,0:T(8,128)(2,1)S(1)} %broadcast_select_fusion.10), channel_id=1, source_target_pairs={{0,1},{1,0},{2,3},{3,2},{4,5},{5,4},{6,7},{7,6},{8,9},{9,8},{10,11... | collective-permute-start | bytes 1572872 | tf_op jit(solution)/shard_map/ppermute | solution.py:527
  (77 other events, 598.7 us)
Sparse Core Ops, SparseCore 0:
  27.4 82.2 all-gather.4
  111.2 79.2 all-gather.8
  192.7 79.2 all-gather.6
  274.0 79.2 all-gather.10
  355.5 75.2 reduce-scatter.4
  433.1 77.2 reduce-scatter.8
  513.2 77.2 reduce-scatter.6
  592.9 77.7 reduce-scatter.10

commit v4 on v3

--- a/solution.py
+++ b/solution.py
@@ -770,30 +770,30 @@
     grad_up = grad_up.result()
     grad_heads = Scatter(*heads_grad(at, rows_n, (dp_0, dp_1), rows_c, (attn_0, attn_1), (*sends, grad_up)))
     grad_down = grad_down.result(grad_heads.keep)
-    own_heads = grad_heads.first(tie(grad_down[:8, :LANES], units=200))
-    _, finish = from_group(tie(back_sum_0, *own_heads))
-    sends = grad_heads.second()
-    back_sum_0 = finish(*sends)
-    mixed_1 = from_group(tie(mixed_1, *back_sum_0))[1]()
-    grad_down = grad_down.T
-    grad_heads = grad_heads.result()
-    grad_qkv = grad_heads[:, : parts * width].reshape(quarter, parts, width)
-    grad_dense = grad_heads[:, parts * width :].T
     sum_qkv = (db_0 + db_1)[:parts].reshape(parts, 2, width)
     sum_up = (up_0 + up_1).reshape(2, hidden)
     out_bias = jnp.sum(cotangent, (0, 1, 2), dtype=f32)
     own, other = (jnp.concatenate([sum_qkv[:, d].reshape(-1), sum_up[d]]) for d in range(2))
     rest = jnp.concatenate([(back_0 + back_1).reshape(-1), out_bias])
     size = own.shape[0]
-    sums = tie(jnp.concatenate([other, rest]), grad_heads, *mixed_1)
-    sums = jnp.concatenate([own, rest]) + flip(sums, "near")
-    for axis in FOLD:
-        sums = sums + flip(sums, axis)
-    bias_sums, rest = sums[:size], sums[size:]
+    sums = jnp.concatenate([own, rest]) + tie(flip(jnp.concatenate([other, rest]), "near"), grad_heads.keep)
+    got = flip(sums, "batch")
+    own_heads = grad_heads.first(tie(grad_down[:8, :LANES], sums, units=200))
+    sums = sums + tie(got, *own_heads)
+    _, finish = from_group(tie(back_sum_0, *own_heads))
+    sums = sums + flip(sums, "branch")
+    sends = grad_heads.second(sums)
+    back_sum_0 = finish(*sends)
+    mixed_1 = from_group(tie(mixed_1, *back_sum_0))[1]()
+    bias_sums, rest = sums[:size], tie(sums[size:], *sends)
     reach = 1
     while reach < line_size:
         rest = rest + lax.ppermute(rest, "line", [(i, i ^ reach) for i in range(line_size)])
         reach *= 2
+    grad_down = grad_down.T
+    grad_heads = grad_heads.result()
+    grad_qkv = grad_heads[:, : parts * width].reshape(quarter, parts, width)
+    grad_dense = grad_heads[:, parts * width :].T
     rest = rest.reshape(3, depth)
     shift_grad = rest[0]
     gain_grad = (rest[1] - ln_bias * shift_grad) / ln_gain

time: 717 us -> 710 us (level)
  waiting for transfers between devices: 129 us -> 114 us
  local copies, waits for them, and re-layouts: 82 us -> 89.3 us
    ppermute x44, waiting for transfers between devices: 123 us -> 102 us  [flip(): return lax.ppermute(a, axis, SWAP)]
    unnamed x124 -> x130, local copies, waits for them, and re-layouts: 34.5 us -> 39.7 us
  transfers between devices with their start and end apart: 54 -> 54, of which waited for: 19 -> 14; matrix products, arithmetic and copies ran while one was open for 20% -> 21% of each run, Pallas kernels for 50% -> 51%
where the time goes in v4:
time: 710 us; the launch traced here: 702 us
  Pallas kernels  357 us (50%)
  waiting for transfers between devices  114 us (16%)
  local copies, waits for them, and re-layouts  89.3 us (13%)
  other arithmetic  85.3 us (12%)
  starting transfers between devices  40.1 us (6%)
  between operations  15.5 us (2%)
    pallas_call x21, Pallas kernels, call(): pl.pallas_call(run, grid_spec=spec, out_shape=out_shape, compiler_params=...  357 us
    ppermute x44, waiting for transfers between devices, flip(): return lax.ppermute(a, axis, SWAP)  102 us
    unnamed x130, local copies, waits for them, and re-layouts  39.7 us
    ppermute x44, starting transfers between devices, flip(): return lax.ppermute(a, axis, SWAP)  37.7 us
    another operation x12, local copies, waits for them, and re-layouts, rope_tables(): return tuple((jnp.tile(t, (1, LANES // HEAD_DIM)) for t in (cos, sa, sb)))  21.2 us
    add x3, other arithmetic, first(): g = self.keep + (tie(self.got, *deps) if deps else self.got)  18.9 us
  transfers between devices with their start and end apart: 54, of which 14 were waited for; matrix products, arithmetic and copies ran while one was open for 21% of the time, Pallas kernels for 51%

profile of v4, /device:TPU:0, one launch (start us, length us, event | category | flops | bytes accessed | tf_op | source)
XLA Modules:
  0.0 701.6 jit_solution(4639430838498739560)
XLA Ops:
  14.1 11.9 %collective-permute-done = bf16[128,2048]{1,0:T(8,128)(2,1)S(1)} collective-permute-done((bf16[128,2048]{1,0:T(8,128)(2,1)S(1)}, bf16[128,2048]{1,0:T(8,128)(2,1)S(1)}, u32[]{:S(2)}, u32[]{:S(2)}) %collective-permute-start) | collective-permute-done | bytes 524320 | tf_op jit(solution)/shard_map/ppermute | solution.py:527
  70.9 21.0 %collective-permute-done.5.refs_0_ = bf16[512,2048]{1,0:T(8,128)(2,1)} collective-permute-done((bf16[512,2048]{1,0:T(8,128)(2,1)}, bf16[512,2048]{1,0:T(8,128)(2,1)}, u32[]{:S(2)}, u32[]{:S(2)}) %collective-permute-start.5) | collective-permute-done | bytes 2097184 | tf_op jit(solution)/shard_map/ppermute | solution.py:527
  97.9 19.6 %collective-permute-done.7.refs_1_ = bf16[256,2048]{1,0:T(8,128)(2,1)} collective-permute-done((bf16[256,2048]{1,0:T(8,128)(2,1)}, bf16[256,2048]{1,0:T(8,128)(2,1)}, u32[]{:S(2)}, u32[]{:S(2)}) %collective-permute-start.7) | collective-permute-done | bytes 1048608 | tf_op jit(solution)/shard_map/ppermute | solution.py:527
  137.0 14.6 %assemble_heads.1 = (bf16[2048,1536]{1,0:T(8,128)(2,1)}, bf16[2048,512]{1,0:T(8,128)(2,1)}, bf16[2,2048,1024]{2,1,0:T(8,128)(2,1)}) custom-call(s32[2]{0:T(128)} %pad_add_fusion.refs_0_, bf16[512,2048]{1,0:T(8,128)(2,1)} %pad_maximum_fusion.1.refs_1_, bf16[512,2048]{1,0:T(8,128)(2,1)} %collective-permute-done.1.refs_2_, bf16[512,2048]{1,0:T(8,128)(2,1)} %tie.34.refs_3_, ...), custom_call_target="tpu_custom_call" | custom-call | flops 3500000000 | bytes 3500001 | tf_op jit(solution)/shard_map/assemble_heads/pallas_call | solution.py:52
  154.4 11.9 %project.4.refs_1_.refs_0_.refs_2_ = f32[1024,1536]{1,0:T(8,128)} custom-call(bf16[1024,2048]{1,0:T(8,128)(2,1)} %all-gather.5.cloned.1.call-done.refs_0_.refs_4_.refs_1_, bf16[2048,1536]{1,0:T(8,128)(2,1)} %get-tuple-element.44.refs_1_.refs_3_), custom_call_target="tpu_custom_call" | custom-call | flops 12499999744 | bytes 12500001 | tf_op jit(solution)/shard_map/project/pallas_call | solution.py:52
  173.3 17.3 %attention.2 = (bf16[1024,512]{1,0:T(8,128)(2,1)}, bf16[3,1024,512]{2,1,0:T(8,128)(2,1)}, f32[32,1024]{1,0:T(8,128)}) custom-call(f32[1024,1536]{1,0:T(8,128)} %project.4.refs_1_.refs_0_.refs_2_, f32[1024,1536]{1,0:T(8,128)} %project.4.refs_1_.refs_0_.refs_2_, f32[1024,1536]{1,0:T(8,128)} %project.4.refs_1_.refs_0_.refs_2_, f32[1,1536]{1,0:T(1,128)} %bitcast.244, ...), custom_call_target="tpu_custom_call" | custom-call | flops 24999999488 | bytes 25000000 | tf_op jit(solution)/shard_map/attention/pallas_call | solution.py:52
  192.5 17.5 %mlp_act.2 = (bf16[1024,2048]{1,0:T(8,128)(2,1)}, bf16[1024,2048]{1,0:T(8,128)(2,1)}) custom-call(bf16[1024,2048]{1,0:T(8,128)(2,1)} %all-gather.5.cloned.1.call-done.refs_0_.refs_4_.refs_1_, bf16[2,2048,1024]{2,1,0:T(8,128)(2,1)} %get-tuple-element.43.refs_1_.refs_2_, f32[1,2048]{1,0:T(1,128)} %bitcast.242, ...), custom_call_target="tpu_custom_call" | custom-call | flops 24999999488 | bytes 25000000 | tf_op jit(solution)/shard_map/mlp_act/pallas_call | solution.py:52
  210.5 7.8 %assemble.1.refs_2_.refs_1_ = bf16[2,2048,1024]{2,1,0:T(8,128)(2,1)} custom-call(s32[2]{0:T(128)} %pad_add_fusion.refs_0_, bf16[512,1024]{1,0:T(8,128)(2,1)} %bitcast.217, bf16[512,1024]{1,0:T(8,128)(2,1)} %collective-permute-done.17.refs_2_, bf16[512,1024]{1,0:T(8,128)(2,1)} %tie.40.refs_3_, bf16[512,1024]{1,0:T(8,128)(2,1)} %collective-permute-done.18.refs_4_, ...), custom_call_target="tpu_custom_call" | custom-call | flops 2000000000 | bytes 2000001 | tf_op jit(solution)/shard_map/assemble/pallas_call | solution.py:52
  218.2 16.0 %mixed_part.2.refs_1_.refs_2_ = bf16[1024,2048]{1,0:T(8,128)(2,1)} custom-call(bf16[1024,2048]{1,0:T(8,128)(2,1)} %get-tuple-element.47.refs_9_.refs_0_.refs_1_.refs_3_, bf16[1024,512]{1,0:T(8,128)(2,1)} %get-tuple-element.46.refs_3_.refs_1_.refs_2_.refs_7_, bf16[2,2048,1024]{2,1,0:T(8,128)(2,1)} %assemble.1.refs_2_.refs_1_, ...), custom_call_target="tpu_custom_call" | custom-call | flops 15000000512 | bytes 15000001 | tf_op jit(solution)/shard_map/mixed_part/pallas_call | solution.py:52
  238.3 5.9 project.5.refs_3_
  244.2 22.8 %attention_grad.2 = (bf16[3,1024,512]{2,1,0:T(8,128)(2,1)}, f32[8,512]{1,0:T(8,128)}) custom-call(bf16[3,1024,512]{2,1,0:T(8,128)(2,1)} %get-tuple-element.49.refs_0_, f32[32,1024]{1,0:T(8,128)} %get-tuple-element.50.refs_1_, bf16[1024,512]{1,0:T(8,128)(2,1)} %get-tuple-element.46.refs_3_.refs_1_.refs_2_.refs_7_, bf16[1024,512]{1,0:T(8,128)(2,1)} %project.5.refs_3_, ...), custom_call_target="tpu_custom_call" | custom-call | flops 24999999488 | bytes 25000000 | tf_op jit(solution)/shard_map/attention_grad/pallas_call | solution.py:52
  267.0 14.0 %mlp_pre.2 = (bf16[1024,2048]{1,0:T(8,128)(2,1)}, f32[8,2048]{1,0:T(8,128)}) custom-call(bf16[1024,2048]{1,0:T(8,128)(2,1)} %all-gather.9.cloned.1.call-done.refs_0_.refs_1_.refs_5_, bf16[2,2048,1024]{2,1,0:T(8,128)(2,1)} %assemble.1.refs_2_.refs_1_, bf16[1024,2048]{1,0:T(8,128)(2,1)} %get-tuple-element.48.refs_2_, ...), custom_call_target="tpu_custom_call" | custom-call | flops 15000000512 | bytes 15000001 | tf_op jit(solution)/shard_map/mlp_pre/pallas_call | solution.py:52
  281.0 22.3 %back_part.2 = (bf16[1024,2048]{1,0:T(8,128)(2,1)}, f32[8,2048]{1,0:T(8,128)}) custom-call(bf16[1024,2048]{1,0:T(8,128)(2,1)} %get-tuple-element.52.refs_0_.refs_3_, bf16[3,1024,512]{2,1,0:T(8,128)(2,1)} %get-tuple-element.51.refs_3_.refs_1_, bf16[2,2048,1024]{2,1,0:T(8,128)(2,1)} %get-tuple-element.43.refs_1_.refs_2_, ...), custom_call_target="tpu_custom_call" | custom-call | flops 24999999488 | bytes 25000000 | tf_op jit(solution)/shard_map/back_part/pallas_call | solution.py:52
  303.6 12.0 %project.6.refs_0_.refs_1_.refs_2_ = f32[1024,1536]{1,0:T(8,128)} custom-call(bf16[1024,2048]{1,0:T(8,128)(2,1)} %all-gather.7.cloned.1.call-done.refs_0_.refs_2_.refs_4_, bf16[2048,1536]{1,0:T(8,128)(2,1)} %get-tuple-element.44.refs_1_.refs_3_, bf16[1024,2048]{1,0:T(8,128)(2,1)} %get-tuple-element.53.refs_2_), custom_call_target="tpu_custom_call" | custom-call | flops 12499999744 | bytes 12500001 | tf_op jit(solution)/shard_map/project/pallas_call | solution.py:52
  315.6 17.3 %attention.3 = (bf16[1024,512]{1,0:T(8,128)(2,1)}, bf16[3,1024,512]{2,1,0:T(8,128)(2,1)}, f32[32,1024]{1,0:T(8,128)}) custom-call(f32[1024,1536]{1,0:T(8,128)} %project.6.refs_0_.refs_1_.refs_2_, f32[1024,1536]{1,0:T(8,128)} %project.6.refs_0_.refs_1_.refs_2_, f32[1024,1536]{1,0:T(8,128)} %project.6.refs_0_.refs_1_.refs_2_, f32[1,1536]{1,0:T(1,128)} %bitcast.247, ...), custom_call_target="tpu_custom_call" | custom-call | flops 24999999488 | bytes 25000000 | tf_op jit(solution)/shard_map/attention/pallas_call | solution.py:52
  332.9 17.6 %mlp_act.3 = (bf16[1024,2048]{1,0:T(8,128)(2,1)}, bf16[1024,2048]{1,0:T(8,128)(2,1)}) custom-call(bf16[1024,2048]{1,0:T(8,128)(2,1)} %all-gather.7.cloned.1.call-done.refs_0_.refs_2_.refs_4_, bf16[2,2048,1024]{2,1,0:T(8,128)(2,1)} %get-tuple-element.43.refs_1_.refs_2_, f32[1,2048]{1,0:T(1,128)} %bitcast.243, ...), custom_call_target="tpu_custom_call" | custom-call | flops 24999999488 | bytes 25000000 | tf_op jit(solution)/shard_map/mlp_act/pallas_call | solution.py:52
  353.4 14.3 %mlp_pre.3 = (bf16[1024,2048]{1,0:T(8,128)(2,1)}, f32[8,2048]{1,0:T(8,128)}) custom-call(bf16[1024,2048]{1,0:T(8,128)(2,1)} %all-gather.11.cloned.1.call-done.refs_0_.refs_2_.refs_6_, bf16[2,2048,1024]{2,1,0:T(8,128)(2,1)} %assemble.1.refs_2_.refs_1_, bf16[1024,2048]{1,0:T(8,128)(2,1)} %get-tuple-element.56.refs_2_), custom_call_target="tpu_custom_call" | custom-call | flops 15000000512 | bytes 15000001 | tf_op jit(solution)/shard_map/mlp_pre/pallas_call | solution.py:52
  367.7 25.6 %weight_grad.2 = (bf16[2,2,512,1024]{3,2,1,0:T(8,128)(2,1)}, bf16[2,2,512,1024]{3,2,1,0:T(8,128)(2,1)}) custom-call(s32[2]{0:T(128)} %pad_add_fusion.refs_0_, bf16[1024,2048]{1,0:T(8,128)(2,1)} %all-gather.5.cloned.1.call-done.refs_0_.refs_4_.refs_1_, bf16[1024,2048]{1,0:T(8,128)(2,1)} %all-gather.7.cloned.1.call-done.refs_0_.refs_2_.refs_4_, ...), custom_call_target="tpu_custom_call" | custom-call | flops 24999999488 | bytes 25000000 | tf_op jit(solution)/shard_map/weight_grad/pallas_call | solution.py:52
  393.6 25.1 %weight_grad.3 = (bf16[2,2,512,1024]{3,2,1,0:T(8,128)(2,1)}, bf16[2,2,512,1024]{3,2,1,0:T(8,128)(2,1)}) custom-call(s32[2]{0:T(128)} %pad_add_fusion.refs_0_, bf16[1024,2048]{1,0:T(8,128)(2,1)} %all-gather.9.cloned.1.call-done.refs_0_.refs_1_.refs_5_, bf16[1024,2048]{1,0:T(8,128)(2,1)} %all-gather.11.cloned.1.call-done.refs_0_.refs_2_.refs_6_, ...), custom_call_target="tpu_custom_call" | custom-call | flops 24999999488 | bytes 25000000 | tf_op jit(solution)/shard_map/weight_grad/pallas_call | solution.py:52
  420.1 5.6 add.165
  428.7 16.0 %mixed_part.3.refs_1_.refs_2_ = bf16[1024,2048]{1,0:T(8,128)(2,1)} custom-call(bf16[1024,2048]{1,0:T(8,128)(2,1)} %get-tuple-element.55.refs_4_.refs_0_, bf16[1024,512]{1,0:T(8,128)(2,1)} %get-tuple-element.54.refs_3_.refs_1_.refs_2_.refs_8_, bf16[2,2048,1024]{2,1,0:T(8,128)(2,1)} %assemble.1.refs_2_.refs_1_, ...), custom_call_target="tpu_custom_call" | custom-call | flops 15000000512 | bytes 15000001 | tf_op jit(solution)/shard_map/mixed_part/pallas_call | solution.py:52
  448.4 6.0 project.7.refs_3_
  454.4 22.7 %attention_grad.3 = (bf16[3,1024,512]{2,1,0:T(8,128)(2,1)}, f32[8,512]{1,0:T(8,128)}) custom-call(bf16[3,1024,512]{2,1,0:T(8,128)(2,1)} %get-tuple-element.61.refs_0_, f32[32,1024]{1,0:T(8,128)} %get-tuple-element.62.refs_1_, bf16[1024,512]{1,0:T(8,128)(2,1)} %get-tuple-element.54.refs_3_.refs_1_.refs_2_.refs_8_, bf16[1024,512]{1,0:T(8,128)(2,1)} %project.7.refs_3_, ...), custom_call_target="tpu_custom_call" | custom-call | flops 24999999488 | bytes 25000000 | tf_op jit(solution)/shard_map/attention_grad/pallas_call | solution.py:52
  477.9 7.8 %add.171 = bf16[2,2,512,1024]{3,2,1,0:T(8,128)(2,1)} add(bf16[2,2,512,1024]{3,2,1,0:T(8,128)(2,1)} %get-tuple-element.60.refs_1_, bf16[2,2,512,1024]{3,2,1,0:T(8,128)(2,1)} %tie.46) | non-fusion elementwise | flops 2097152 | bytes 12582912 | tf_op jit(solution)/shard_map/add | solution.py:642
  494.8 8.6 %collective-permute-done.27.refs_0_ = bf16[256,1024]{1,0:T(8,128)(2,1)} collective-permute-done((bf16[256,1024]{1,0:T(8,128)(2,1)S(1)}, bf16[256,1024]{1,0:T(8,128)(2,1)}, u32[]{:S(2)}, u32[]{:S(2)}) %collective-permute-start.27) | collective-permute-done | bytes 524320 | tf_op jit(solution)/shard_map/ppermute | solution.py:527
  513.9 22.0 %back_part.3 = (bf16[1024,2048]{1,0:T(8,128)(2,1)}, f32[8,2048]{1,0:T(8,128)}) custom-call(bf16[1024,2048]{1,0:T(8,128)(2,1)} %get-tuple-element.57.refs_4_.refs_0_, bf16[3,1024,512]{2,1,0:T(8,128)(2,1)} %get-tuple-element.63.refs_1_.refs_4_, bf16[2,2048,1024]{2,1,0:T(8,128)(2,1)} %get-tuple-element.43.refs_1_.refs_2_, ...), custom_call_target="tpu_custom_call" | custom-call | flops 24999999488 | bytes 25000000 | tf_op jit(solution)/shard_map/back_part/pallas_call | solution.py:52
  548.9 28.8 %heads_grad.1 = (bf16[2,2,512,1024]{3,2,1,0:T(8,128)(2,1)}, bf16[2,2,512,1024]{3,2,1,0:T(8,128)(2,1)}) custom-call(s32[2]{0:T(128)} %pad_add_fusion.refs_0_, bf16[1024,2048]{1,0:T(8,128)(2,1)} %all-gather.5.cloned.1.call-done.refs_0_.refs_4_.refs_1_, bf16[1024,2048]{1,0:T(8,128)(2,1)} %all-gather.7.cloned.1.call-done.refs_0_.refs_2_.refs_4_, ...), custom_call_target="tpu_custom_call" | custom-call | flops 24999999488 | bytes 25000000 | tf_op jit(solution)/shard_map/heads_grad/pallas_call | solution.py:52
  586.4 7.5 %collective-permute-done.31.refs_0_ = bf16[2,2,512,1024]{3,2,1,0:T(8,128)(2,1)} collective-permute-done((bf16[2,2,512,1024]{3,2,1,0:T(8,128)(2,1)}, bf16[2,2,512,1024]{3,2,1,0:T(8,128)(2,1)}, u32[]{:S(2)}, u32[]{:S(2)}) %collective-permute-start.31) | collective-permute-done | bytes 4194336 | tf_op jit(solution)/shard_map/ppermute | solution.py:527
  607.6 6.9 collective-permute-done.39.refs_0_
  635.6 14.7 %collective-permute-done.44 = bf16[512,1024]{1,0:T(8,128)(2,1)} collective-permute-done((bf16[512,1024]{1,0:T(8,128)(2,1)S(1)}, bf16[512,1024]{1,0:T(8,128)(2,1)}, u32[]{:S(2)}, u32[]{:S(2)}) %collective-permute-start.44) | collective-permute-done | bytes 1048608 | tf_op jit(solution)/shard_map/ppermute | solution.py:527
  665.2 6.2 reduce-scatter.11.cloned.1.call-done.refs_0_
  678.0 8.6 %collective-permute-done.43 = bf16[128,2048]{1,0:T(8,128)(2,1)S(1)} collective-permute-done((bf16[128,2048]{1,0:T(8,128)(2,1)S(1)}, bf16[128,2048]{1,0:T(8,128)(2,1)S(1)}, u32[]{:S(2)}, u32[]{:S(2)}) %collective-permute-start.43) | collective-permute-done | bytes 524320 | tf_op jit(solution)/shard_map/ppermute | solution.py:527
  (386 shorter events, 210.4 us)
Async XLA Ops:
  7.2 147.2 %all-gather.5.cloned.1.call-start = ((), (), s32[]{:S(2)}) async-start(), calls=%async_computation.4 | async-start | bytes 5242880 | tf_op jit(solution)/shard_map/all_gather | solution.py:717
  27.2 211.1 %all-gather.9.cloned.1.call-start = ((), (), s32[]{:S(2)}) async-start(), calls=%async_computation.7 | async-start | bytes 5242880 | tf_op jit(solution)/shard_map/all_gather | solution.py:717
  45.2 46.7 %collective-permute-start.5 = (bf16[512,2048]{1,0:T(8,128)(2,1)}, bf16[512,2048]{1,0:T(8,128)(2,1)}, u32[]{:S(2)}, u32[]{:S(2)}) collective-permute-start(bf16[512,2048]{1,0:T(8,128)(2,1)} %tie.33), channel_id=1, source_target_pairs={{0,16},{16,0},{1,17},{17,1},{2,18},{18,2},{3,19},{19,3},{4,20},{20... | collective-permute-start | bytes 6291464 | tf_op jit(solution)/shard_map/ppermute | solution.py:527
  46.7 47.9 %collective-permute-start.3 = (bf16[512,2048]{1,0:T(8,128)(2,1)}, bf16[512,2048]{1,0:T(8,128)(2,1)}, u32[]{:S(2)}, u32[]{:S(2)}) collective-permute-start(bf16[512,2048]{1,0:T(8,128)(2,1)} %tie.33), channel_id=1, source_target_pairs={{0,1},{1,0},{2,3},{3,2},{4,5},{5,4},{6,7},{7,6},{8,9},{9,8},{10,11... | collective-permute-start | bytes 6291464 | tf_op jit(solution)/shard_map/ppermute | solution.py:527
  47.8 255.8 %all-gather.7.cloned.1.call-start = ((), (), s32[]{:S(2)}) async-start(), calls=%async_computation.6 | async-start | bytes 5242880 | tf_op jit(solution)/shard_map/all_gather | solution.py:717
  97.4 37.5 %collective-permute-start.1 = (bf16[512,2048]{1,0:T(8,128)(2,1)}, bf16[512,2048]{1,0:T(8,128)(2,1)}, u32[]{:S(2)}, u32[]{:S(2)}) collective-permute-start(bf16[512,2048]{1,0:T(8,128)(2,1)} %pad_maximum_fusion.1.refs_1_), channel_id=1, source_target_pairs={{0,8},{8,0},{1,9},{9,1},{2,10},{10,2},{3,11},{11,3},{4,12},{12,4},... | collective-permute-start | bytes 6291464 | tf_op jit(solution)/shard_map/ppermute | solution.py:527
  97.4 37.5 %collective-permute-start.6 = (bf16[512,2048]{1,0:T(8,128)(2,1)}, bf16[512,2048]{1,0:T(8,128)(2,1)}, u32[]{:S(2)}, u32[]{:S(2)}) collective-permute-start(bf16[512,2048]{1,0:T(8,128)(2,1)} %tie.35.refs_5_), channel_id=1, source_target_pairs={{0,8},{8,0},{1,9},{9,1},{2,10},{10,2},{3,11},{11,3},{4,12},{12,4},... | collective-permute-start | bytes 6291464 | tf_op jit(solution)/shard_map/ppermute | solution.py:527
  97.9 37.5 %collective-permute-start.4 = (bf16[512,2048]{1,0:T(8,128)(2,1)}, bf16[512,2048]{1,0:T(8,128)(2,1)}, u32[]{:S(2)}, u32[]{:S(2)}) collective-permute-start(bf16[512,2048]{1,0:T(8,128)(2,1)} %tie.34.refs_3_), channel_id=1, source_target_pairs={{0,8},{8,0},{1,9},{9,1},{2,10},{10,2},{3,11},{11,3},{4,12},{12,4},... | collective-permute-start | bytes 6291464 | tf_op jit(solution)/shard_map/ppermute | solution.py:527
  134.9 75.5 %collective-permute-start.17 = (bf16[512,1024]{1,0:T(8,128)(2,1)}, bf16[512,1024]{1,0:T(8,128)(2,1)}, u32[]{:S(2)}, u32[]{:S(2)}) collective-permute-start(bf16[512,1024]{1,0:T(8,128)(2,1)} %bitcast.216), channel_id=1, source_target_pairs={{0,8},{8,0},{1,9},{9,1},{2,10},{10,2},{3,11},{11,3},{4,12},{12,4},... | collective-permute-start | bytes 3145736 | tf_op jit(solution)/shard_map/ppermute | solution.py:527
  134.9 33.3 %collective-permute-start.14 = (bf16[512,1024]{1,0:T(8,128)(2,1)}, bf16[512,1024]{1,0:T(8,128)(2,1)}, u32[]{:S(2)}, u32[]{:S(2)}) collective-permute-start(bf16[512,1024]{1,0:T(8,128)(2,1)} %tie.38), channel_id=1, source_target_pairs={{0,1},{1,0},{2,3},{3,2},{4,5},{5,4},{6,7},{7,6},{8,9},{9,8},{10,11... | collective-permute-start | bytes 3145736 | tf_op jit(solution)/shard_map/ppermute | solution.py:527
  135.4 30.9 %collective-permute-start.13 = (bf16[512,1024]{1,0:T(8,128)(2,1)}, bf16[512,1024]{1,0:T(8,128)(2,1)}, u32[]{:S(2)}, u32[]{:S(2)}) collective-permute-start(bf16[512,1024]{1,0:T(8,128)(2,1)} %tie.38), channel_id=1, source_target_pairs={{0,16},{16,0},{1,17},{17,1},{2,18},{18,2},{3,19},{19,3},{4,20},{20... | collective-permute-start | bytes 3145736 | tf_op jit(solution)/shard_map/ppermute | solution.py:527
  153.9 199.5 %all-gather.11.cloned.1.call-start = ((), (), s32[]{:S(2)}) async-start(), calls=%async_computation.8 | async-start | bytes 5242880 | tf_op jit(solution)/shard_map/all_gather | solution.py:717
  167.5 43.0 %collective-permute-start.19 = (bf16[512,1024]{1,0:T(8,128)(2,1)}, bf16[512,1024]{1,0:T(8,128)(2,1)}, u32[]{:S(2)}, u32[]{:S(2)}) collective-permute-start(bf16[512,1024]{1,0:T(8,128)(2,1)} %tie.39.refs_5_), channel_id=1, source_target_pairs={{0,8},{8,0},{1,9},{9,1},{2,10},{10,2},{3,11},{11,3},{4,12},{12,4},... | collective-permute-start | bytes 3145736 | tf_op jit(solution)/shard_map/ppermute | solution.py:527
  170.1 40.4 %collective-permute-start.18 = (bf16[512,1024]{1,0:T(8,128)(2,1)}, bf16[512,1024]{1,0:T(8,128)(2,1)}, u32[]{:S(2)}, u32[]{:S(2)}) collective-permute-start(bf16[512,1024]{1,0:T(8,128)(2,1)} %tie.40.refs_3_), channel_id=1, source_target_pairs={{0,8},{8,0},{1,9},{9,1},{2,10},{10,2},{3,11},{11,3},{4,12},{12,4},... | collective-permute-start | bytes 3145736 | tf_op jit(solution)/shard_map/ppermute | solution.py:527
  210.0 24.2 %collective-permute-start.21 = (bf16[128,2048]{1,0:T(8,128)(2,1)}, bf16[128,2048]{1,0:T(8,128)(2,1)}, u32[]{:S(2)}, u32[]{:S(2)}) collective-permute-start(bf16[128,2048]{1,0:T(8,128)(2,1)} %tie.41), channel_id=1, source_target_pairs={{0,1},{1,0},{2,3},{3,2},{4,5},{5,4},{6,7},{7,6},{8,9},{9,8},{10,11... | collective-permute-start | bytes 1572872 | tf_op jit(solution)/shard_map/ppermute | solution.py:527
  236.5 208.3 %reduce-scatter.5.cloned.1.call-start = ((), (), s32[]{:S(2)}) async-start(), calls=%async_computation.5 | async-start | bytes 5242880 | tf_op jit(solution)/shard_map/reduce_scatter | solution.py:735
  237.1 366.9 %reduce-scatter.9.cloned.1.call-start = ((), (), s32[]{:S(2)}) async-start(), calls=%async_computation.10 | async-start | bytes 5242880 | tf_op jit(solution)/shard_map/reduce_scatter | solution.py:735
  303.3 328.8 %reduce-scatter.7.cloned.1.call-start = ((), (), s32[]{:S(2)}) async-start(), calls=%async_computation.9 | async-start | bytes 5242880 | tf_op jit(solution)/shard_map/reduce_scatter | solution.py:735
  393.3 26.8 %collective-permute-start.22 = (bf16[2,2,512,1024]{3,2,1,0:T(8,128)(2,1)}, bf16[2,2,512,1024]{3,2,1,0:T(8,128)(2,1)}, u32[]{:S(2)}, u32[]{:S(2)}) collective-permute-start(bf16[2,2,512,1024]{3,2,1,0:T(8,128)(2,1)} %get-tuple-element.59), channel_id=1, source_target_pairs={{0,8},{8,0},{1,9},{9,1},{2,10},{10,2},{3,11},{11,3},{4,12},{12,4},... | collective-permute-start | bytes 12582920 | tf_op jit(solution)/shard_map/ppermute | solution.py:527
  418.7 58.5 %collective-permute-start.24 = (bf16[2,2,512,1024]{3,2,1,0:T(8,128)(2,1)}, bf16[2,2,512,1024]{3,2,1,0:T(8,128)(2,1)}, u32[]{:S(2)}, u32[]{:S(2)}) collective-permute-start(bf16[2,2,512,1024]{3,2,1,0:T(8,128)(2,1)} %get-tuple-element.64), channel_id=1, source_target_pairs={{0,8},{8,0},{1,9},{9,1},{2,10},{10,2},{3,11},{11,3},{4,12},{12,4},... | collective-permute-start | bytes 12582920 | tf_op jit(solution)/shard_map/ppermute | solution.py:527
  444.7 226.7 %reduce-scatter.11.cloned.1.call-start = ((), (), s32[]{:S(2)}) async-start(), calls=%async_computation.11 | async-start | bytes 5242880 | tf_op jit(solution)/shard_map/reduce_scatter | solution.py:735
  446.8 64.1 %collective-permute-start.23 = (bf16[128,2048]{1,0:T(8,128)(2,1)}, bf16[128,2048]{1,0:T(8,128)(2,1)S(1)}, u32[]{:S(2)}, u32[]{:S(2)}) collective-permute-start(bf16[128,2048]{1,0:T(8,128)(2,1)} %broadcast_select_fusion.18.refs_3_), channel_id=1, source_target_pairs={{0,1},{1,0},{2,3},{3,2},{4,5},{5,4},{6,7},{7,6},{8,9},{9,8},{10,11... | collective-permute-start | bytes 1572872 | tf_op jit(solution)/shard_map/ppermute | solution.py:527
  491.8 45.8 %collective-permute-start.28 = (bf16[256,1024]{1,0:T(8,128)(2,1)}, bf16[256,1024]{1,0:T(8,128)(2,1)S(1)}, u32[]{:S(2)}, u32[]{:S(2)}) collective-permute-start(bf16[256,1024]{1,0:T(8,128)(2,1)} %get-tuple-element.122), channel_id=1, source_target_pairs={{0,1},{1,0},{2,3},{3,2},{4,5},{5,4},{6,7},{7,6},{8,9},{9,8},{10,11... | collective-permute-start | bytes 1572872 | tf_op jit(solution)/shard_map/ppermute | solution.py:527
  493.2 45.2 %collective-permute-start.25 = (bf16[256,1024]{1,0:T(8,128)(2,1)}, bf16[256,1024]{1,0:T(8,128)(2,1)S(1)}, u32[]{:S(2)}, u32[]{:S(2)}) collective-permute-start(bf16[256,1024]{1,0:T(8,128)(2,1)} %get-tuple-element.124), channel_id=1, source_target_pairs={{0,16},{16,0},{1,17},{17,1},{2,18},{18,2},{3,19},{19,3},{4,20},{20... | collective-permute-start | bytes 1572872 | tf_op jit(solution)/shard_map/ppermute | solution.py:527
  506.9 38.3 %collective-permute-start.29 = (bf16[512,1024]{1,0:T(8,128)(2,1)}, bf16[512,1024]{1,0:T(8,128)(2,1)}, u32[]{:S(2)}, u32[]{:S(2)}) collective-permute-start(bf16[512,1024]{1,0:T(8,128)(2,1)} %pad_maximum_fusion.7.refs_5_), channel_id=1, source_target_pairs={{0,1},{1,0},{2,3},{3,2},{4,5},{5,4},{6,7},{7,6},{8,9},{9,8},{10,11... | collective-permute-start | bytes 3145736 | tf_op jit(solution)/shard_map/ppermute | solution.py:527
  509.4 35.7 %collective-permute-start.30 = (bf16[512,1024]{1,0:T(8,128)(2,1)}, bf16[512,1024]{1,0:T(8,128)(2,1)}, u32[]{:S(2)}, u32[]{:S(2)}) collective-permute-start(bf16[512,1024]{1,0:T(8,128)(2,1)} %pad_maximum_fusion.8.refs_6_), channel_id=1, source_target_pairs={{0,16},{16,0},{1,17},{17,1},{2,18},{18,2},{3,19},{19,3},{4,20},{20... | collective-permute-start | bytes 3145736 | tf_op jit(solution)/shard_map/ppermute | solution.py:527
  536.8 46.0 %collective-permute-start.34 = (f32[7936]{0:T(1024)S(1)}, f32[7936]{0:T(1024)S(1)}, u32[]{:S(2)}, u32[]{:S(2)}) collective-permute-start(f32[7936]{0:T(1024)S(1)} %pad_maximum_fusion.19), channel_id=1, source_target_pairs={{0,1},{1,0},{2,3},{3,2},{4,5},{5,4},{6,7},{7,6},{8,9},{9,8},{10,11... | collective-permute-start | bytes 95240 | tf_op jit(solution)/shard_map/ppermute | solution.py:527
  542.2 36.5 %collective-permute-start.32 = (bf16[512,1024]{1,0:T(8,128)(2,1)}, bf16[512,1024]{1,0:T(8,128)(2,1)S(1)}, u32[]{:S(2)}, u32[]{:S(2)}) collective-permute-start(bf16[512,1024]{1,0:T(8,128)(2,1)} %pad_maximum_fusion.9.refs_9_), channel_id=1, source_target_pairs={{0,1},{1,0},{2,3},{3,2},{4,5},{5,4},{6,7},{7,6},{8,9},{9,8},{10,11... | collective-permute-start | bytes 3145736 | tf_op jit(solution)/shard_map/ppermute | solution.py:527
  544.7 33.1 %collective-permute-start.33 = (bf16[512,1024]{1,0:T(8,128)(2,1)}, bf16[512,1024]{1,0:T(8,128)(2,1)S(1)}, u32[]{:S(2)}, u32[]{:S(2)}) collective-permute-start(bf16[512,1024]{1,0:T(8,128)(2,1)} %pad_maximum_fusion.10.refs_10_), channel_id=1, source_target_pairs={{0,16},{16,0},{1,17},{17,1},{2,18},{18,2},{3,19},{19,3},{4,20},{20... | collective-permute-start | bytes 3145736 | tf_op jit(solution)/shard_map/ppermute | solution.py:527
  624.1 26.2 %collective-permute-start.44 = (bf16[512,1024]{1,0:T(8,128)(2,1)S(1)}, bf16[512,1024]{1,0:T(8,128)(2,1)}, u32[]{:S(2)}, u32[]{:S(2)}) collective-permute-start(bf16[512,1024]{1,0:T(8,128)(2,1)S(1)} %copy-done.12), channel_id=1, source_target_pairs={{0,1},{1,0},{2,3},{3,2},{4,5},{5,4},{6,7},{7,6},{8,9},{9,8},{10,11... | collective-permute-start | bytes 3145736 | tf_op jit(solution)/shard_map/ppermute | solution.py:527
  624.9 25.5 %collective-permute-start.45 = (bf16[512,1024]{1,0:T(8,128)(2,1)S(1)}, bf16[512,1024]{1,0:T(8,128)(2,1)}, u32[]{:S(2)}, u32[]{:S(2)}) collective-permute-start(bf16[512,1024]{1,0:T(8,128)(2,1)S(1)} %copy-done.11), channel_id=1, source_target_pairs={{0,16},{16,0},{1,17},{17,1},{2,18},{18,2},{3,19},{19,3},{4,20},{20... | collective-permute-start | bytes 3145736 | tf_op jit(solution)/shard_map/ppermute | solution.py:527
  634.2 28.9 %collective-permute-start.40 = (bf16[128,2048]{1,0:T(8,128)(2,1)}, bf16[128,2048]{1,0:T(8,128)(2,1)}, u32[]{:S(2)}, u32[]{:S(2)}) collective-permute-start(bf16[128,2048]{1,0:T(8,128)(2,1)} %broadcast_select_fusion.10), channel_id=1, source_target_pairs={{0,1},{1,0},{2,3},{3,2},{4,5},{5,4},{6,7},{7,6},{8,9},{9,8},{10,11... | collective-permute-start | bytes 1572872 | tf_op jit(solution)/shard_map/ppermute | solution.py:527
  (81 other events, 654.3 us)
Sparse Core Ops, SparseCore 0:
  27.4 82.2 all-gather.4
  111.2 79.2 all-gather.8
  192.7 79.2 all-gather.6
  274.0 79.2 all-gather.10
  355.5 75.3 reduce-scatter.4
  433.1 77.2 reduce-scatter.8
  513.3 77.2 reduce-scatter.6
  593.0 78.3 reduce-scatter.10

commit v5 on v4

--- a/solution.py
+++ b/solution.py
@@ -639,23 +639,60 @@
         self.half = keep.shape[2] // 2
 
     def first(self, *deps):
-        g = self.keep + (tie(self.got, *deps) if deps else self.got)
-        corner = g[1, 1]
-        self.own, self.to_y, self.to_x = g[0, 0], g[0, 1], g[1, 0]
+        core = tie(self.got, *deps) if deps else self.got
+        own, to_y, to_x, corner = ((self.keep[i, j], core[i, j]) for i, j in ((0, 0), (0, 1), (1, 0), (1, 1)))
+        self.own, self.to_y, self.to_x = own, to_y, to_x
+        corner = corner[0] + corner[1]
         self.got = flip(corner[: self.half], "near"), flip(corner[self.half :], "batch")
-        return (self.own,)
+        return (corner,)
 
     def second(self, *deps):
         h = self.half
         got = tuple(tie(a, *deps) for a in self.got) if deps else self.got
-        to_y = jnp.concatenate([self.to_y[:h] + got[0], self.to_y[h:]], 0)
-        to_x = jnp.concatenate([self.to_x[:h], self.to_x[h:] + got[1]], 0)
+        to_y, to_x = self.to_y[0] + self.to_y[1], self.to_x[0] + self.to_x[1]
+        to_y = jnp.concatenate([to_y[:h] + got[0], to_y[h:]], 0)
+        to_x = jnp.concatenate([to_x[:h], to_x[h:] + got[1]], 0)
         self.got = flip(to_x, "near"), flip(to_y, "batch")
         return to_x, to_y
 
     def result(self, *deps):
         got = tuple(tie(a, *deps) for a in self.got) if deps else self.got
-        return self.own.astype(f32) + got[0].astype(f32) + got[1].astype(f32)
+        return sum(a.astype(f32) for a in (*self.own, *got))
+
+
+def norm_grad(at, tokens, cotangent, kept, got, gain, s, into=None):
+    micros, seqs, shard, depth = tokens.shape
+    tile = min(64, shard)
+
+    def kernel(at_ref, x_ref, c_ref, kept_ref, got_ref, gain_ref, *refs):
+        x = x_ref[...].astype(f32)
+        centered = x - jnp.mean(x, -1, keepdims=True)
+        scale = lax.rsqrt(jnp.mean(centered * centered, -1, keepdims=True) + eps_norm)
+        unit = centered * scale
+        mine = pl.program_id(0) == at_ref[0]
+        w = jnp.where(mine, kept_ref[...].astype(f32), got_ref[...].astype(f32)) * gain_ref[...]
+        refs[-1][...] = c_ref[...].astype(f32) + scale * (
+            w - jnp.mean(w, -1, keepdims=True) - unit * jnp.mean(w * unit, -1, keepdims=True)
+        )
+
+    block = pl.BlockSpec((None, None, tile, depth), lambda m, i, at: (m, s, i, 0))
+    rows = pl.BlockSpec((tile, depth), lambda m, i, at: (i, 0))
+    extra = [] if into is None else [into]
+    return pl.pallas_call(
+        kernel,
+        grid_spec=pltpu.PrefetchScalarGridSpec(
+            num_scalar_prefetch=1,
+            grid=(micros, shard // tile),
+            in_specs=[block, block, rows, rows, pl.BlockSpec((1, depth), lambda m, i, at: (0, 0))]
+            + [pl.BlockSpec(memory_space=pl.ANY)] * len(extra),
+            out_specs=block,
+        ),
+        out_shape=jax.ShapeDtypeStruct(tokens.shape, f32),
+        input_output_aliases={6: 0} if extra else {},
+        compiler_params=pltpu.CompilerParams(vmem_limit_bytes=VMEM),
+        cost_estimate=cost(3),
+        name="norm_grad",
+    )(at, tokens, cotangent, kept, got, gain.reshape(1, -1), *extra)
 
 
 def body(
@@ -694,9 +731,11 @@
         send = jnp.where(first, hi, lo)
         got = flip(send, "near")
 
-        def finish(*deps):
+        def finish(*deps, by_micro=True):
             other = tie(got, *deps) if deps else got
             kept = jnp.where(first, lo, hi)
+            if not by_micro:
+                return kept, other
             return jnp.where(first, kept, other), jnp.where(first, other, kept)
 
         return send, finish
@@ -742,14 +781,15 @@
     act_0, slope = mlp_act(rows_n[0], up, bias_up, (attn_0, *late.corner))
     down_t = assemble(late.third(), at, (act_0,))
     part = mixed_part(act_0, attn_0, down_t, dense_t)
-    mixed_0 = scatter_rows(part)
+    both = [part]
     c_1 = to_group(cotangent[:, 1], (act_0,), (part,))
     rows_c.append(gather_rows(c_1))
     grad_attn = project(rows_c[0], dense_t, bf16, (part, c_1))
     dp_0, db_0 = attention_grad(keep, log, attn_0, grad_attn, tables[0], segment[0])
     pre_0, up_0 = mlp_pre(rows_c[0], down_t, slope, (dp_0,))
     part, back_0 = back_part(pre_0, dp_0, up, qkv, rows_n[0])
-    back_sum_0 = scatter_rows(part)
+    both = jnp.stack([a.reshape(line_size, 2 * shard, depth) for a in (*both, part)], 1)
+    mixed_0, back_sum_0 = lax.psum_scatter(both, "line", scatter_dimension=0, tiled=False)
     proj = project(rows_n[1], qkv, f32, (part,))
     attn_1, keep, log = attention(proj, bias_qkv, tables[1], segment[1])
     act_1, slope = mlp_act(rows_n[1], up, bias_up, (attn_1,))
@@ -759,12 +799,10 @@
     sends = grad_up.first(grad_down.keep)
     part = mixed_part(act_1, attn_1, down_t, dense_t, sends)
     mixed_1 = scatter_rows(part)
-    send, finish = from_group(tie(mixed_0, part))
-    grad_attn = project(rows_c[1], dense_t, bf16, (part, send))
+    grad_attn = project(rows_c[1], dense_t, bf16, (part,))
     dp_1, db_1 = attention_grad(keep, log, attn_1, grad_attn, tables[1], segment[1])
-    mixed_0 = finish(dp_1)
     sends = (*grad_up.second(dp_1), *grad_down.first(dp_1))
-    part, back_1 = back_part(pre_1, dp_1, up, qkv, rows_n[1], (*sends, *mixed_0))
+    part, back_1 = back_part(pre_1, dp_1, up, qkv, rows_n[1], sends)
     back_sum_1 = scatter_rows(part)
     sends = grad_down.second(part)
     grad_up = grad_up.result()
@@ -780,10 +818,12 @@
     got = flip(sums, "batch")
     own_heads = grad_heads.first(tie(grad_down[:8, :LANES], sums, units=200))
     sums = sums + tie(got, *own_heads)
+    _, finish_m = from_group(tie(mixed_0, *own_heads))
     _, finish = from_group(tie(back_sum_0, *own_heads))
     sums = sums + flip(sums, "branch")
     sends = grad_heads.second(sums)
-    back_sum_0 = finish(*sends)
+    mixed_0 = finish_m(*sends)
+    back_sum_0 = finish(*sends, by_micro=False)
     mixed_1 = from_group(tie(mixed_1, *back_sum_0))[1]()
     bias_sums, rest = sums[:size], tie(sums[size:], *sends)
     reach = 1
@@ -798,20 +838,18 @@
     shift_grad = rest[0]
     gain_grad = (rest[1] - ln_bias * shift_grad) / ln_gain
 
-    mixed, tokens_grad = [], []
-    back_sum_1 = from_group(tie(back_sum_1, *mixed_1, rest))[1]()
-    for s, (m, g) in enumerate(((mixed_0, back_sum_0), (mixed_1, back_sum_1))):
-        mixed.append((tokens[:, s].astype(f32) + jnp.stack(m, 0).astype(f32) + dense_bias + down_bias).astype(bf16))
-        w = jnp.stack(g, 0).astype(f32) * ln_gain
-        u = units[s]
-        tokens_grad.append(
-            cotangent[:, s].astype(f32)
-            + scales[s] * (w - jnp.mean(w, -1, keepdims=True) - u * jnp.mean(w * u, -1, keepdims=True))
-        )
+    near_at = x.astype(jnp.int32).reshape(1)
+    tokens_grad = norm_grad(near_at, tokens, cotangent, *back_sum_0, ln_gain, 0)
+    back_sum_1 = from_group(tie(back_sum_1, *mixed_1, rest))[1](by_micro=False)
+    tokens_grad = norm_grad(near_at, tokens, cotangent, *back_sum_1, ln_gain, 1, tokens_grad)
+    mixed = [
+        (tokens[:, s].astype(f32) + jnp.stack(m, 0).astype(f32) + dense_bias + down_bias).astype(bf16)
+        for s, m in enumerate((mixed_0, mixed_1))
+    ]
 
     return (
         jnp.stack(mixed, 1),
-        jnp.stack(tokens_grad, 1),
+        tokens_grad,
         gain_grad,
         shift_grad,
         grad_qkv,

time: 710 us -> 700 us (0.986)
  waiting for transfers between devices: 114 us -> 92.9 us
  Pallas kernels: 357 us -> 369 us
    ppermute x44, waiting for transfers between devices: 102 us -> 88.6 us  [flip(): return lax.ppermute(a, axis, SWAP)]
    pallas_call x0 -> x2, Pallas kernels: none -> 9.99 us  [norm_grad(): pl.pallas_call(kernel, grid_spec=pltpu.PrefetchScalarGridSpec(num_scalar_...]
    another operation x3 -> x2, other arithmetic: 0.69 us -> 9.79 us  [the longest x1 7.6 us: body(): jnp.stack([a.reshape(line_size, 2 * shard, depth) for a in (*both, part)]...]
    add x10 -> x12, other arithmetic: 34.5 us -> 28.6 us  [the longest x3 11.5 us: second(): to_y, to_x = (self.to_y[0] + self.to_y[1], self.to_x[0] + self.to_x[1])]
    unnamed x130 -> x115, local copies, waits for them, and re-layouts: 39.7 us -> 34.2 us
  transfers between devices with their start and end apart: 54 -> 53, of which waited for: 14 -> 11; matrix products, arithmetic and copies ran while one was open for 21% -> 22% of each run, Pallas kernels for 51% -> 53%
where the time goes in v5:
time: 700 us; the launch traced here: 691 us
  Pallas kernels  369 us (53%)
  waiting for transfers between devices  92.9 us (13%)
  local copies, waits for them, and re-layouts  87.8 us (13%)
  other arithmetic  86.1 us (12%)
  starting transfers between devices  40 us (6%)
  between operations  15.1 us (2%)
    pallas_call x21, Pallas kernels, call(): pl.pallas_call(run, grid_spec=spec, out_shape=out_shape, compiler_params=...  359 us
    ppermute x44, waiting for transfers between devices, flip(): return lax.ppermute(a, axis, SWAP)  88.6 us
    ppermute x44, starting transfers between devices, flip(): return lax.ppermute(a, axis, SWAP)  35.7 us
    unnamed x115, local copies, waits for them, and re-layouts  34.2 us
    another operation x12, local copies, waits for them, and re-layouts, rope_tables(): return tuple((jnp.tile(t, (1, LANES // HEAD_DIM)) for t in (cos, sa, sb)))  21.2 us
  transfers between devices with their start and end apart: 53, of which 11 were waited for; matrix products, arithmetic and copies ran while one was open for 22% of the time, Pallas kernels for 53%

profile of v5, /device:TPU:0, one launch (start us, length us, event | category | flops | bytes accessed | tf_op | source)
XLA Modules:
  0.0 690.8 jit_solution(17099495282473107296)
XLA Ops:
  15.0 11.9 %collective-permute-done = bf16[128,2048]{1,0:T(8,128)(2,1)S(1)} collective-permute-done((bf16[128,2048]{1,0:T(8,128)(2,1)S(1)}, bf16[128,2048]{1,0:T(8,128)(2,1)S(1)}, u32[]{:S(2)}, u32[]{:S(2)}) %collective-permute-start) | collective-permute-done | bytes 524320 | tf_op jit(solution)/shard_map/ppermute | solution.py:527
  71.7 21.0 %collective-permute-done.5.refs_0_ = bf16[512,2048]{1,0:T(8,128)(2,1)} collective-permute-done((bf16[512,2048]{1,0:T(8,128)(2,1)}, bf16[512,2048]{1,0:T(8,128)(2,1)}, u32[]{:S(2)}, u32[]{:S(2)}) %collective-permute-start.5) | collective-permute-done | bytes 2097184 | tf_op jit(solution)/shard_map/ppermute | solution.py:527
  98.8 19.6 %collective-permute-done.7.refs_1_ = bf16[256,2048]{1,0:T(8,128)(2,1)} collective-permute-done((bf16[256,2048]{1,0:T(8,128)(2,1)}, bf16[256,2048]{1,0:T(8,128)(2,1)}, u32[]{:S(2)}, u32[]{:S(2)}) %collective-permute-start.7) | collective-permute-done | bytes 1048608 | tf_op jit(solution)/shard_map/ppermute | solution.py:527
  137.8 14.6 %assemble_heads.1 = (bf16[2048,1536]{1,0:T(8,128)(2,1)}, bf16[2048,512]{1,0:T(8,128)(2,1)}, bf16[2,2048,1024]{2,1,0:T(8,128)(2,1)}) custom-call(s32[2]{0:T(128)} %pad_add_fusion.refs_0_, bf16[512,2048]{1,0:T(8,128)(2,1)} %pad_maximum_fusion.1.refs_1_, bf16[512,2048]{1,0:T(8,128)(2,1)} %collective-permute-done.1.refs_2_, bf16[512,2048]{1,0:T(8,128)(2,1)} %tie.34.refs_3_, ...), custom_call_target="tpu_custom_call" | custom-call | flops 3500000000 | bytes 3500001 | tf_op jit(solution)/shard_map/assemble_heads/pallas_call | solution.py:52
  155.0 12.0 %project.4.refs_1_.refs_0_.refs_2_ = f32[1024,1536]{1,0:T(8,128)} custom-call(bf16[1024,2048]{1,0:T(8,128)(2,1)} %all-gather.5.cloned.1.call-done.refs_0_.refs_4_.refs_1_, bf16[2048,1536]{1,0:T(8,128)(2,1)} %get-tuple-element.44.refs_1_.refs_3_), custom_call_target="tpu_custom_call" | custom-call | flops 12499999744 | bytes 12500001 | tf_op jit(solution)/shard_map/project/pallas_call | solution.py:52
  174.1 17.3 %attention.2 = (bf16[1024,512]{1,0:T(8,128)(2,1)}, bf16[3,1024,512]{2,1,0:T(8,128)(2,1)}, f32[32,1024]{1,0:T(8,128)}) custom-call(f32[1024,1536]{1,0:T(8,128)} %project.4.refs_1_.refs_0_.refs_2_, f32[1024,1536]{1,0:T(8,128)} %project.4.refs_1_.refs_0_.refs_2_, f32[1024,1536]{1,0:T(8,128)} %project.4.refs_1_.refs_0_.refs_2_, f32[1,1536]{1,0:T(1,128)} %bitcast.215, ...), custom_call_target="tpu_custom_call" | custom-call | flops 24999999488 | bytes 25000000 | tf_op jit(solution)/shard_map/attention/pallas_call | solution.py:52
  193.3 17.5 %mlp_act.2 = (bf16[1024,2048]{1,0:T(8,128)(2,1)}, bf16[1024,2048]{1,0:T(8,128)(2,1)}) custom-call(bf16[1024,2048]{1,0:T(8,128)(2,1)} %all-gather.5.cloned.1.call-done.refs_0_.refs_4_.refs_1_, bf16[2,2048,1024]{2,1,0:T(8,128)(2,1)} %get-tuple-element.43.refs_1_.refs_2_, f32[1,2048]{1,0:T(1,128)} %bitcast.213, ...), custom_call_target="tpu_custom_call" | custom-call | flops 24999999488 | bytes 25000000 | tf_op jit(solution)/shard_map/mlp_act/pallas_call | solution.py:52
  211.3 7.9 %assemble.1.refs_2_.refs_1_ = bf16[2,2048,1024]{2,1,0:T(8,128)(2,1)} custom-call(s32[2]{0:T(128)} %pad_add_fusion.refs_0_, bf16[512,1024]{1,0:T(8,128)(2,1)} %bitcast.189, bf16[512,1024]{1,0:T(8,128)(2,1)} %collective-permute-done.17.refs_2_, bf16[512,1024]{1,0:T(8,128)(2,1)} %tie.40.refs_3_, bf16[512,1024]{1,0:T(8,128)(2,1)} %collective-permute-done.18.refs_4_, ...), custom_call_target="tpu_custom_call" | custom-call | flops 2000000000 | bytes 2000001 | tf_op jit(solution)/shard_map/assemble/pallas_call | solution.py:52
  219.2 16.0 %mixed_part.2.refs_1_.refs_2_ = bf16[1024,2048]{1,0:T(8,128)(2,1)} custom-call(bf16[1024,2048]{1,0:T(8,128)(2,1)} %get-tuple-element.47.refs_9_.refs_0_.refs_1_.refs_3_, bf16[1024,512]{1,0:T(8,128)(2,1)} %get-tuple-element.46.refs_3_.refs_1_.refs_2_.refs_7_, bf16[2,2048,1024]{2,1,0:T(8,128)(2,1)} %assemble.1.refs_2_.refs_1_, ...), custom_call_target="tpu_custom_call" | custom-call | flops 15000000512 | bytes 15000001 | tf_op jit(solution)/shard_map/mixed_part/pallas_call | solution.py:52
  237.9 5.9 project.5.refs_3_
  243.8 22.7 %attention_grad.2 = (bf16[3,1024,512]{2,1,0:T(8,128)(2,1)}, f32[8,512]{1,0:T(8,128)}) custom-call(bf16[3,1024,512]{2,1,0:T(8,128)(2,1)} %get-tuple-element.49.refs_0_, f32[32,1024]{1,0:T(8,128)} %get-tuple-element.50.refs_1_, bf16[1024,512]{1,0:T(8,128)(2,1)} %get-tuple-element.46.refs_3_.refs_1_.refs_2_.refs_7_, bf16[1024,512]{1,0:T(8,128)(2,1)} %project.5.refs_3_, ...), custom_call_target="tpu_custom_call" | custom-call | flops 24999999488 | bytes 25000000 | tf_op jit(solution)/shard_map/attention_grad/pallas_call | solution.py:52
  266.6 14.0 %mlp_pre.2 = (bf16[1024,2048]{1,0:T(8,128)(2,1)}, f32[8,2048]{1,0:T(8,128)}) custom-call(bf16[1024,2048]{1,0:T(8,128)(2,1)} %all-gather.7.cloned.1.call-done.refs_0_.refs_1_.refs_5_, bf16[2,2048,1024]{2,1,0:T(8,128)(2,1)} %assemble.1.refs_2_.refs_1_, bf16[1024,2048]{1,0:T(8,128)(2,1)} %get-tuple-element.48.refs_2_, ...), custom_call_target="tpu_custom_call" | custom-call | flops 15000000512 | bytes 15000001 | tf_op jit(solution)/shard_map/mlp_pre/pallas_call | solution.py:52
  280.6 22.5 %back_part.2 = (bf16[1024,2048]{1,0:T(8,128)(2,1)}, f32[8,2048]{1,0:T(8,128)}) custom-call(bf16[1024,2048]{1,0:T(8,128)(2,1)} %get-tuple-element.52.refs_0_.refs_3_, bf16[3,1024,512]{2,1,0:T(8,128)(2,1)} %get-tuple-element.51.refs_3_.refs_1_, bf16[2,2048,1024]{2,1,0:T(8,128)(2,1)} %get-tuple-element.43.refs_1_.refs_2_, ...), custom_call_target="tpu_custom_call" | custom-call | flops 24999999488 | bytes 25000000 | tf_op jit(solution)/shard_map/back_part/pallas_call | solution.py:52
  303.1 7.6 %pad_maximum_fusion = bf16[4,2,256,2048]{3,2,1,0:T(8,128)(2,1)} fusion(bf16[4,1,256,2048]{3,2,1,0:T(8,128)(2,1)} %bitcast.196, bf16[4,1,256,2048]{3,2,1,0:T(8,128)(2,1)} %bitcast.186), kind=kLoop, calls=%fused_computation | loop fusion | flops 4194304 | bytes 16777216 | tf_op jit(solution)/shard_map/stack | solution.py:791
  312.4 11.9 %project.6.refs_0_.refs_1_.refs_2_ = f32[1024,1536]{1,0:T(8,128)} custom-call(bf16[1024,2048]{1,0:T(8,128)(2,1)} %all-gather.9.cloned.1.call-done.refs_0_.refs_2_.refs_4_, bf16[2048,1536]{1,0:T(8,128)(2,1)} %get-tuple-element.44.refs_1_.refs_3_, bf16[1024,2048]{1,0:T(8,128)(2,1)} %get-tuple-element.53.refs_2_), custom_call_target="tpu_custom_call" | custom-call | flops 12499999744 | bytes 12500001 | tf_op jit(solution)/shard_map/project/pallas_call | solution.py:52
  324.3 17.3 %attention.3 = (bf16[1024,512]{1,0:T(8,128)(2,1)}, bf16[3,1024,512]{2,1,0:T(8,128)(2,1)}, f32[32,1024]{1,0:T(8,128)}) custom-call(f32[1024,1536]{1,0:T(8,128)} %project.6.refs_0_.refs_1_.refs_2_, f32[1024,1536]{1,0:T(8,128)} %project.6.refs_0_.refs_1_.refs_2_, f32[1024,1536]{1,0:T(8,128)} %project.6.refs_0_.refs_1_.refs_2_, f32[1,1536]{1,0:T(1,128)} %bitcast.218, ...), custom_call_target="tpu_custom_call" | custom-call | flops 24999999488 | bytes 25000000 | tf_op jit(solution)/shard_map/attention/pallas_call | solution.py:52
  341.6 17.5 %mlp_act.3 = (bf16[1024,2048]{1,0:T(8,128)(2,1)}, bf16[1024,2048]{1,0:T(8,128)(2,1)}) custom-call(bf16[1024,2048]{1,0:T(8,128)(2,1)} %all-gather.9.cloned.1.call-done.refs_0_.refs_2_.refs_4_, bf16[2,2048,1024]{2,1,0:T(8,128)(2,1)} %get-tuple-element.43.refs_1_.refs_2_, f32[1,2048]{1,0:T(1,128)} %bitcast.214, ...), custom_call_target="tpu_custom_call" | custom-call | flops 24999999488 | bytes 25000000 | tf_op jit(solution)/shard_map/mlp_act/pallas_call | solution.py:52
  359.1 14.8 %mlp_pre.3 = (bf16[1024,2048]{1,0:T(8,128)(2,1)}, f32[8,2048]{1,0:T(8,128)}) custom-call(bf16[1024,2048]{1,0:T(8,128)(2,1)} %all-gather.11.cloned.1.call-done.refs_0_.refs_2_.refs_6_, bf16[2,2048,1024]{2,1,0:T(8,128)(2,1)} %assemble.1.refs_2_.refs_1_, bf16[1024,2048]{1,0:T(8,128)(2,1)} %get-tuple-element.58.refs_2_), custom_call_target="tpu_custom_call" | custom-call | flops 15000000512 | bytes 15000001 | tf_op jit(solution)/shard_map/mlp_pre/pallas_call | solution.py:52
  374.0 25.5 %weight_grad.2 = (bf16[2,2,512,1024]{3,2,1,0:T(8,128)(2,1)}, bf16[2,2,512,1024]{3,2,1,0:T(8,128)(2,1)}) custom-call(s32[2]{0:T(128)} %pad_add_fusion.refs_0_, bf16[1024,2048]{1,0:T(8,128)(2,1)} %all-gather.5.cloned.1.call-done.refs_0_.refs_4_.refs_1_, bf16[1024,2048]{1,0:T(8,128)(2,1)} %all-gather.9.cloned.1.call-done.refs_0_.refs_2_.refs_4_, ...), custom_call_target="tpu_custom_call" | custom-call | flops 24999999488 | bytes 25000000 | tf_op jit(solution)/shard_map/weight_grad/pallas_call | solution.py:52
  399.9 25.1 %weight_grad.3 = (bf16[2,2,512,1024]{3,2,1,0:T(8,128)(2,1)}, bf16[2,2,512,1024]{3,2,1,0:T(8,128)(2,1)}) custom-call(s32[2]{0:T(128)} %pad_add_fusion.refs_0_, bf16[1024,2048]{1,0:T(8,128)(2,1)} %all-gather.7.cloned.1.call-done.refs_0_.refs_1_.refs_5_, bf16[1024,2048]{1,0:T(8,128)(2,1)} %all-gather.11.cloned.1.call-done.refs_0_.refs_2_.refs_6_, ...), custom_call_target="tpu_custom_call" | custom-call | flops 24999999488 | bytes 25000000 | tf_op jit(solution)/shard_map/weight_grad/pallas_call | solution.py:52
  430.5 16.7 %mixed_part.3.refs_2_ = bf16[1024,2048]{1,0:T(8,128)(2,1)} custom-call(bf16[1024,2048]{1,0:T(8,128)(2,1)} %get-tuple-element.57.refs_4_.refs_0_, bf16[1024,512]{1,0:T(8,128)(2,1)} %get-tuple-element.56.refs_3_.refs_1_.refs_2_.refs_8_, bf16[2,2048,1024]{2,1,0:T(8,128)(2,1)} %assemble.1.refs_2_.refs_1_, bf16[2048,512]{1,0:T(8,128)(2,1)} %get-tuple-element.45.refs_1_.refs_3_, ...), custom_call_target="tpu_custom_call" | custom-call | flops 15000000512 | bytes 15000001 | tf_op jit(solution)/shard_map/mixed_part/pallas_call | solution.py:52
  450.6 6.2 project.7.refs_3_
  456.8 22.9 %attention_grad.3 = (bf16[3,1024,512]{2,1,0:T(8,128)(2,1)}, f32[8,512]{1,0:T(8,128)}) custom-call(bf16[3,1024,512]{2,1,0:T(8,128)(2,1)} %get-tuple-element.54.refs_0_, f32[32,1024]{1,0:T(8,128)} %get-tuple-element.55.refs_1_, bf16[1024,512]{1,0:T(8,128)(2,1)} %get-tuple-element.56.refs_3_.refs_1_.refs_2_.refs_8_, bf16[1024,512]{1,0:T(8,128)(2,1)} %project.7.refs_3_, ...), custom_call_target="tpu_custom_call" | custom-call | flops 24999999488 | bytes 25000000 | tf_op jit(solution)/shard_map/attention_grad/pallas_call | solution.py:52
  498.1 21.9 %back_part.3 = (bf16[1024,2048]{1,0:T(8,128)(2,1)}, f32[8,2048]{1,0:T(8,128)}) custom-call(bf16[1024,2048]{1,0:T(8,128)(2,1)} %get-tuple-element.59.refs_4_.refs_0_, bf16[3,1024,512]{2,1,0:T(8,128)(2,1)} %get-tuple-element.63.refs_1_.refs_4_, bf16[2,2048,1024]{2,1,0:T(8,128)(2,1)} %get-tuple-element.43.refs_1_.refs_2_, ...), custom_call_target="tpu_custom_call" | custom-call | flops 24999999488 | bytes 25000000 | tf_op jit(solution)/shard_map/back_part/pallas_call | solution.py:52
  528.8 4.3 fusion.23.refs_11_
  533.2 28.6 %heads_grad.1 = (bf16[2,2,512,1024]{3,2,1,0:T(8,128)(2,1)}, bf16[2,2,512,1024]{3,2,1,0:T(8,128)(2,1)}) custom-call(s32[2]{0:T(128)} %pad_add_fusion.refs_0_, bf16[1024,2048]{1,0:T(8,128)(2,1)} %all-gather.5.cloned.1.call-done.refs_0_.refs_4_.refs_1_, bf16[1024,2048]{1,0:T(8,128)(2,1)} %all-gather.9.cloned.1.call-done.refs_0_.refs_2_.refs_4_, ...), custom_call_target="tpu_custom_call" | custom-call | flops 24999999488 | bytes 25000000 | tf_op jit(solution)/shard_map/heads_grad/pallas_call | solution.py:52
  571.2 6.8 collective-permute-done.30.refs_0_
  578.0 4.2 slice_add_fusion
  624.9 5.0 norm_grad.2.refs_0_
  634.3 12.3 %collective-permute-done.44 = bf16[512,1024]{1,0:T(8,128)(2,1)} collective-permute-done((bf16[512,1024]{1,0:T(8,128)(2,1)S(1)}, bf16[512,1024]{1,0:T(8,128)(2,1)}, u32[]{:S(2)}, u32[]{:S(2)}) %collective-permute-start.44) | collective-permute-done | bytes 1048608 | tf_op jit(solution)/shard_map/ppermute | solution.py:527
  667.1 10.3 %collective-permute-done.43.got_ref = bf16[128,2048]{1,0:T(8,128)(2,1)S(1)} collective-permute-done((bf16[128,2048]{1,0:T(8,128)(2,1)S(1)}, bf16[128,2048]{1,0:T(8,128)(2,1)S(1)}, u32[]{:S(2)}, u32[]{:S(2)}) %collective-permute-start.43) | collective-permute-done | bytes 524320 | tf_op jit(solution)/shard_map/ppermute | solution.py:527
  678.2 4.9 norm_grad.3
  (369 shorter events, 208.8 us)
Async XLA Ops:
  7.2 147.8 %all-gather.5.cloned.1.call-start = ((), (), s32[]{:S(2)}) async-start(), calls=%async_computation.3 | async-start | bytes 5242880 | tf_op jit(solution)/shard_map/all_gather | solution.py:756
  28.1 209.8 %all-gather.7.cloned.1.call-start = ((), (), s32[]{:S(2)}) async-start(), calls=%async_computation.4 | async-start | bytes 5242880 | tf_op jit(solution)/shard_map/all_gather | solution.py:756
  46.0 46.7 %collective-permute-start.5 = (bf16[512,2048]{1,0:T(8,128)(2,1)}, bf16[512,2048]{1,0:T(8,128)(2,1)}, u32[]{:S(2)}, u32[]{:S(2)}) collective-permute-start(bf16[512,2048]{1,0:T(8,128)(2,1)} %tie.33), channel_id=1, source_target_pairs={{0,16},{16,0},{1,17},{17,1},{2,18},{18,2},{3,19},{19,3},{4,20},{20... | collective-permute-start | bytes 6291464 | tf_op jit(solution)/shard_map/ppermute | solution.py:527
  47.6 47.9 %collective-permute-start.3 = (bf16[512,2048]{1,0:T(8,128)(2,1)}, bf16[512,2048]{1,0:T(8,128)(2,1)}, u32[]{:S(2)}, u32[]{:S(2)}) collective-permute-start(bf16[512,2048]{1,0:T(8,128)(2,1)} %tie.33), channel_id=1, source_target_pairs={{0,1},{1,0},{2,3},{3,2},{4,5},{5,4},{6,7},{7,6},{8,9},{9,8},{10,11... | collective-permute-start | bytes 6291464 | tf_op jit(solution)/shard_map/ppermute | solution.py:527
  48.6 263.7 %all-gather.9.cloned.1.call-start = ((), (), s32[]{:S(2)}) async-start(), calls=%async_computation.6 | async-start | bytes 5242880 | tf_op jit(solution)/shard_map/all_gather | solution.py:756
  98.3 37.5 %collective-permute-start.1 = (bf16[512,2048]{1,0:T(8,128)(2,1)}, bf16[512,2048]{1,0:T(8,128)(2,1)}, u32[]{:S(2)}, u32[]{:S(2)}) collective-permute-start(bf16[512,2048]{1,0:T(8,128)(2,1)} %pad_maximum_fusion.1.refs_1_), channel_id=1, source_target_pairs={{0,8},{8,0},{1,9},{9,1},{2,10},{10,2},{3,11},{11,3},{4,12},{12,4},... | collective-permute-start | bytes 6291464 | tf_op jit(solution)/shard_map/ppermute | solution.py:527
  98.3 37.5 %collective-permute-start.6 = (bf16[512,2048]{1,0:T(8,128)(2,1)}, bf16[512,2048]{1,0:T(8,128)(2,1)}, u32[]{:S(2)}, u32[]{:S(2)}) collective-permute-start(bf16[512,2048]{1,0:T(8,128)(2,1)} %tie.35.refs_5_), channel_id=1, source_target_pairs={{0,8},{8,0},{1,9},{9,1},{2,10},{10,2},{3,11},{11,3},{4,12},{12,4},... | collective-permute-start | bytes 6291464 | tf_op jit(solution)/shard_map/ppermute | solution.py:527
  98.8 37.5 %collective-permute-start.4 = (bf16[512,2048]{1,0:T(8,128)(2,1)}, bf16[512,2048]{1,0:T(8,128)(2,1)}, u32[]{:S(2)}, u32[]{:S(2)}) collective-permute-start(bf16[512,2048]{1,0:T(8,128)(2,1)} %tie.34.refs_3_), channel_id=1, source_target_pairs={{0,8},{8,0},{1,9},{9,1},{2,10},{10,2},{3,11},{11,3},{4,12},{12,4},... | collective-permute-start | bytes 6291464 | tf_op jit(solution)/shard_map/ppermute | solution.py:527
  135.8 75.5 %collective-permute-start.17 = (bf16[512,1024]{1,0:T(8,128)(2,1)}, bf16[512,1024]{1,0:T(8,128)(2,1)}, u32[]{:S(2)}, u32[]{:S(2)}) collective-permute-start(bf16[512,1024]{1,0:T(8,128)(2,1)} %bitcast.188), channel_id=1, source_target_pairs={{0,8},{8,0},{1,9},{9,1},{2,10},{10,2},{3,11},{11,3},{4,12},{12,4},... | collective-permute-start | bytes 3145736 | tf_op jit(solution)/shard_map/ppermute | solution.py:527
  135.8 33.3 %collective-permute-start.14 = (bf16[512,1024]{1,0:T(8,128)(2,1)}, bf16[512,1024]{1,0:T(8,128)(2,1)}, u32[]{:S(2)}, u32[]{:S(2)}) collective-permute-start(bf16[512,1024]{1,0:T(8,128)(2,1)} %tie.38), channel_id=1, source_target_pairs={{0,1},{1,0},{2,3},{3,2},{4,5},{5,4},{6,7},{7,6},{8,9},{9,8},{10,11... | collective-permute-start | bytes 3145736 | tf_op jit(solution)/shard_map/ppermute | solution.py:527
  136.3 30.7 %collective-permute-start.13 = (bf16[512,1024]{1,0:T(8,128)(2,1)}, bf16[512,1024]{1,0:T(8,128)(2,1)}, u32[]{:S(2)}, u32[]{:S(2)}) collective-permute-start(bf16[512,1024]{1,0:T(8,128)(2,1)} %tie.38), channel_id=1, source_target_pairs={{0,16},{16,0},{1,17},{17,1},{2,18},{18,2},{3,19},{19,3},{4,20},{20... | collective-permute-start | bytes 3145736 | tf_op jit(solution)/shard_map/ppermute | solution.py:527
  154.7 204.4 %all-gather.11.cloned.1.call-start = ((), (), s32[]{:S(2)}) async-start(), calls=%async_computation.7 | async-start | bytes 5242880 | tf_op jit(solution)/shard_map/all_gather | solution.py:756
  168.1 43.2 %collective-permute-start.19 = (bf16[512,1024]{1,0:T(8,128)(2,1)}, bf16[512,1024]{1,0:T(8,128)(2,1)}, u32[]{:S(2)}, u32[]{:S(2)}) collective-permute-start(bf16[512,1024]{1,0:T(8,128)(2,1)} %tie.39.refs_5_), channel_id=1, source_target_pairs={{0,8},{8,0},{1,9},{9,1},{2,10},{10,2},{3,11},{11,3},{4,12},{12,4},... | collective-permute-start | bytes 3145736 | tf_op jit(solution)/shard_map/ppermute | solution.py:527
  170.9 40.4 %collective-permute-start.18 = (bf16[512,1024]{1,0:T(8,128)(2,1)}, bf16[512,1024]{1,0:T(8,128)(2,1)}, u32[]{:S(2)}, u32[]{:S(2)}) collective-permute-start(bf16[512,1024]{1,0:T(8,128)(2,1)} %tie.40.refs_3_), channel_id=1, source_target_pairs={{0,8},{8,0},{1,9},{9,1},{2,10},{10,2},{3,11},{11,3},{4,12},{12,4},... | collective-permute-start | bytes 3145736 | tf_op jit(solution)/shard_map/ppermute | solution.py:527
  237.4 351.4 %reduce-scatter.4.cloned.1.call-start = ((), (), s32[]{:S(2)}) async-start(), calls=%async_computation.5 | async-start | bytes 10485760 | tf_op jit(solution)/shard_map/reduce_scatter | solution.py:792
  310.7 321.4 %reduce-scatter.6.cloned.1.call-start = ((), (), s32[]{:S(2)}) async-start(), calls=%async_computation.8 | async-start | bytes 5242880 | tf_op jit(solution)/shard_map/reduce_scatter | solution.py:774
  399.5 26.8 %collective-permute-start.22 = (bf16[2,2,512,1024]{3,2,1,0:T(8,128)(2,1)}, bf16[2,2,512,1024]{3,2,1,0:T(8,128)(2,1)}, u32[]{:S(2)}, u32[]{:S(2)}) collective-permute-start(bf16[2,2,512,1024]{3,2,1,0:T(8,128)(2,1)} %get-tuple-element.61), channel_id=1, source_target_pairs={{0,8},{8,0},{1,9},{9,1},{2,10},{10,2},{3,11},{11,3},{4,12},{12,4},... | collective-permute-start | bytes 12582920 | tf_op jit(solution)/shard_map/ppermute | solution.py:527
  424.9 54.8 %collective-permute-start.23 = (bf16[2,2,512,1024]{3,2,1,0:T(8,128)(2,1)}, bf16[2,2,512,1024]{3,2,1,0:T(8,128)(2,1)}, u32[]{:S(2)}, u32[]{:S(2)}) collective-permute-start(bf16[2,2,512,1024]{3,2,1,0:T(8,128)(2,1)} %get-tuple-element.64), channel_id=1, source_target_pairs={{0,8},{8,0},{1,9},{9,1},{2,10},{10,2},{3,11},{11,3},{4,12},{12,4},... | collective-permute-start | bytes 12582920 | tf_op jit(solution)/shard_map/ppermute | solution.py:527
  448.2 46.0 %collective-permute-start.26 = (bf16[256,1024]{1,0:T(8,128)(2,1)}, bf16[256,1024]{1,0:T(8,128)(2,1)}, u32[]{:S(2)}, u32[]{:S(2)}) collective-permute-start(bf16[256,1024]{1,0:T(8,128)(2,1)} %get-tuple-element.141), channel_id=1, source_target_pairs={{0,1},{1,0},{2,3},{3,2},{4,5},{5,4},{6,7},{7,6},{8,9},{9,8},{10,11... | collective-permute-start | bytes 1572872 | tf_op jit(solution)/shard_map/ppermute | solution.py:527
  449.8 39.3 %collective-permute-start.25 = (bf16[256,1024]{1,0:T(8,128)(2,1)}, bf16[256,1024]{1,0:T(8,128)(2,1)}, u32[]{:S(2)}, u32[]{:S(2)}) collective-permute-start(bf16[256,1024]{1,0:T(8,128)(2,1)} %get-tuple-element.142), channel_id=1, source_target_pairs={{0,16},{16,0},{1,17},{17,1},{2,18},{18,2},{3,19},{19,3},{4,20},{20... | collective-permute-start | bytes 1572872 | tf_op jit(solution)/shard_map/ppermute | solution.py:527
  450.5 211.5 %reduce-scatter.8.cloned.1.call-start = ((), (), s32[]{:S(2)}) async-start(), calls=%async_computation.9 | async-start | bytes 5242880 | tf_op jit(solution)/shard_map/reduce_scatter | solution.py:774
  487.4 37.9 %collective-permute-start.27 = (bf16[256,1024]{1,0:T(8,128)(2,1)}, bf16[256,1024]{1,0:T(8,128)(2,1)}, u32[]{:S(2)}, u32[]{:S(2)}) collective-permute-start(bf16[256,1024]{1,0:T(8,128)(2,1)} %get-tuple-element.139), channel_id=1, source_target_pairs={{0,1},{1,0},{2,3},{3,2},{4,5},{5,4},{6,7},{7,6},{8,9},{9,8},{10,11... | collective-permute-start | bytes 1572872 | tf_op jit(solution)/shard_map/ppermute | solution.py:527
  487.8 33.5 %collective-permute-start.24 = (bf16[256,1024]{1,0:T(8,128)(2,1)}, bf16[256,1024]{1,0:T(8,128)(2,1)}, u32[]{:S(2)}, u32[]{:S(2)}) collective-permute-start(bf16[256,1024]{1,0:T(8,128)(2,1)} %get-tuple-element.140), channel_id=1, source_target_pairs={{0,16},{16,0},{1,17},{17,1},{2,18},{18,2},{3,19},{19,3},{4,20},{20... | collective-permute-start | bytes 1572872 | tf_op jit(solution)/shard_map/ppermute | solution.py:527
  492.5 36.3 %collective-permute-start.28 = (bf16[512,1024]{1,0:T(8,128)(2,1)}, bf16[512,1024]{1,0:T(8,128)(2,1)}, u32[]{:S(2)}, u32[]{:S(2)}) collective-permute-start(bf16[512,1024]{1,0:T(8,128)(2,1)} %pad_maximum_fusion.7.refs_5_), channel_id=1, source_target_pairs={{0,1},{1,0},{2,3},{3,2},{4,5},{5,4},{6,7},{7,6},{8,9},{9,8},{10,11... | collective-permute-start | bytes 3145736 | tf_op jit(solution)/shard_map/ppermute | solution.py:527
  497.4 31.4 %collective-permute-start.29 = (bf16[512,1024]{1,0:T(8,128)(2,1)}, bf16[512,1024]{1,0:T(8,128)(2,1)}, u32[]{:S(2)}, u32[]{:S(2)}) collective-permute-start(bf16[512,1024]{1,0:T(8,128)(2,1)} %pad_maximum_fusion.8.refs_6_), channel_id=1, source_target_pairs={{0,16},{16,0},{1,17},{17,1},{2,18},{18,2},{3,19},{19,3},{4,20},{20... | collective-permute-start | bytes 3145736 | tf_op jit(solution)/shard_map/ppermute | solution.py:527
  520.9 40.8 %collective-permute-start.33 = (f32[7936]{0:T(1024)S(1)}, f32[7936]{0:T(1024)S(1)}, u32[]{:S(2)}, u32[]{:S(2)}) collective-permute-start(f32[7936]{0:T(1024)S(1)} %pad_maximum_fusion.17), channel_id=1, source_target_pairs={{0,1},{1,0},{2,3},{3,2},{4,5},{5,4},{6,7},{7,6},{8,9},{9,8},{10,11... | collective-permute-start | bytes 95240 | tf_op jit(solution)/shard_map/ppermute | solution.py:527
  523.6 40.9 %collective-permute-start.31 = (bf16[512,1024]{1,0:T(8,128)(2,1)}, bf16[512,1024]{1,0:T(8,128)(2,1)S(1)}, u32[]{:S(2)}, u32[]{:S(2)}) collective-permute-start(bf16[512,1024]{1,0:T(8,128)(2,1)} %pad_maximum_fusion.9.refs_9_), channel_id=1, source_target_pairs={{0,1},{1,0},{2,3},{3,2},{4,5},{5,4},{6,7},{7,6},{8,9},{9,8},{10,11... | collective-permute-start | bytes 3145736 | tf_op jit(solution)/shard_map/ppermute | solution.py:527
  527.5 38.0 %collective-permute-start.32 = (bf16[512,1024]{1,0:T(8,128)(2,1)}, bf16[512,1024]{1,0:T(8,128)(2,1)S(1)}, u32[]{:S(2)}, u32[]{:S(2)}) collective-permute-start(bf16[512,1024]{1,0:T(8,128)(2,1)} %pad_maximum_fusion.10.refs_10_), channel_id=1, source_target_pairs={{0,16},{16,0},{1,17},{17,1},{2,18},{18,2},{3,19},{19,3},{4,20},{20... | collective-permute-start | bytes 3145736 | tf_op jit(solution)/shard_map/ppermute | solution.py:527
  594.0 30.8 %collective-permute-start.34 = (bf16[128,2048]{1,0:T(8,128)(2,1)}, bf16[128,2048]{1,0:T(8,128)(2,1)}, u32[]{:S(2)}, u32[]{:S(2)}) collective-permute-start(bf16[128,2048]{1,0:T(8,128)(2,1)} %broadcast_select_fusion.12), channel_id=1, source_target_pairs={{0,1},{1,0},{2,3},{3,2},{4,5},{5,4},{6,7},{7,6},{8,9},{9,8},{10,11... | collective-permute-start | bytes 1572872 | tf_op jit(solution)/shard_map/ppermute | solution.py:527
  598.0 26.0 %collective-permute-start.39 = (bf16[128,2048]{1,0:T(8,128)(2,1)}, bf16[128,2048]{1,0:T(8,128)(2,1)S(1)}, u32[]{:S(2)}, u32[]{:S(2)}) collective-permute-start(bf16[128,2048]{1,0:T(8,128)(2,1)} %get-tuple-element.137), channel_id=1, source_target_pairs={{0,1},{1,0},{2,3},{3,2},{4,5},{5,4},{6,7},{7,6},{8,9},{9,8},{10,11... | collective-permute-start | bytes 1572872 | tf_op jit(solution)/shard_map/ppermute | solution.py:527
  619.6 27.1 %collective-permute-start.44 = (bf16[512,1024]{1,0:T(8,128)(2,1)S(1)}, bf16[512,1024]{1,0:T(8,128)(2,1)}, u32[]{:S(2)}, u32[]{:S(2)}) collective-permute-start(bf16[512,1024]{1,0:T(8,128)(2,1)S(1)} %copy-done.6), channel_id=1, source_target_pairs={{0,1},{1,0},{2,3},{3,2},{4,5},{5,4},{6,7},{7,6},{8,9},{9,8},{10,11... | collective-permute-start | bytes 3145736 | tf_op jit(solution)/shard_map/ppermute | solution.py:527
  620.7 26.0 %collective-permute-start.45 = (bf16[512,1024]{1,0:T(8,128)(2,1)S(1)}, bf16[512,1024]{1,0:T(8,128)(2,1)}, u32[]{:S(2)}, u32[]{:S(2)}) collective-permute-start(bf16[512,1024]{1,0:T(8,128)(2,1)S(1)} %copy-done.5), channel_id=1, source_target_pairs={{0,16},{16,0},{1,17},{17,1},{2,18},{18,2},{3,19},{19,3},{4,20},{20... | collective-permute-start | bytes 3145736 | tf_op jit(solution)/shard_map/ppermute | solution.py:527
  (73 other events, 672.8 us)
Sparse Core Ops, SparseCore 0:
  28.2 82.2 all-gather.4
  112.1 79.2 all-gather.6
  193.6 79.2 all-gather.8
  274.9 79.2 all-gather.10
  356.4 143.0 reduce-scatter.3
  501.6 77.4 reduce-scatter.5
  581.5 78.2 reduce-scatter.7

commit v6 on v5

--- a/solution.py
+++ b/solution.py
@@ -661,7 +661,10 @@
 
 
 def norm_grad(at, tokens, cotangent, kept, got, gain, s, into=None):
-    micros, seqs, shard, depth = tokens.shape
+    shard, depth = tokens.shape[2:]
+    both = kept is not None and got is not None
+    at = jnp.concatenate([at, at if got is None else 1 - at])
+    kept, got = (got if kept is None else kept), (kept if got is None else got)
     tile = min(64, shard)
 
     def kernel(at_ref, x_ref, c_ref, kept_ref, got_ref, gain_ref, *refs):
@@ -669,20 +672,22 @@
         centered = x - jnp.mean(x, -1, keepdims=True)
         scale = lax.rsqrt(jnp.mean(centered * centered, -1, keepdims=True) + eps_norm)
         unit = centered * scale
-        mine = pl.program_id(0) == at_ref[0]
-        w = jnp.where(mine, kept_ref[...].astype(f32), got_ref[...].astype(f32)) * gain_ref[...]
+        grad = kept_ref[...].astype(f32)
+        if both:
+            grad = jnp.where(pl.program_id(0) == at_ref[0], grad, got_ref[...].astype(f32))
+        w = grad * gain_ref[...]
         refs[-1][...] = c_ref[...].astype(f32) + scale * (
             w - jnp.mean(w, -1, keepdims=True) - unit * jnp.mean(w * unit, -1, keepdims=True)
         )
 
-    block = pl.BlockSpec((None, None, tile, depth), lambda m, i, at: (m, s, i, 0))
+    block = pl.BlockSpec((None, None, tile, depth), lambda m, i, at: (m if both else at[1], s, i, 0))
     rows = pl.BlockSpec((tile, depth), lambda m, i, at: (i, 0))
     extra = [] if into is None else [into]
     return pl.pallas_call(
         kernel,
         grid_spec=pltpu.PrefetchScalarGridSpec(
             num_scalar_prefetch=1,
-            grid=(micros, shard // tile),
+            grid=(2 if both else 1, shard // tile),
             in_specs=[block, block, rows, rows, pl.BlockSpec((1, depth), lambda m, i, at: (0, 0))]
             + [pl.BlockSpec(memory_space=pl.ANY)] * len(extra),
             out_specs=block,
@@ -841,7 +846,8 @@
     near_at = x.astype(jnp.int32).reshape(1)
     tokens_grad = norm_grad(near_at, tokens, cotangent, *back_sum_0, ln_gain, 0)
     back_sum_1 = from_group(tie(back_sum_1, *mixed_1, rest))[1](by_micro=False)
-    tokens_grad = norm_grad(near_at, tokens, cotangent, *back_sum_1, ln_gain, 1, tokens_grad)
+    tokens_grad = norm_grad(near_at, tokens, cotangent, back_sum_1[0], None, ln_gain, 1, tokens_grad)
+    tokens_grad = norm_grad(near_at, tokens, cotangent, None, back_sum_1[1], ln_gain, 1, tokens_grad)
     mixed = [
         (tokens[:, s].astype(f32) + jnp.stack(m, 0).astype(f32) + dense_bias + down_bias).astype(bf16)
         for s, m in enumerate((mixed_0, mixed_1))

time: 700 us -> 698 us (level)
  waiting for transfers between devices: 92.9 us -> 85.1 us
    ppermute x44, waiting for transfers between devices: 88.6 us -> 81.4 us  [flip(): return lax.ppermute(a, axis, SWAP)]
    unnamed x115 -> x117, local copies, waits for them, and re-layouts: 34.2 us -> 33.2 us
  transfers between devices with their start and end apart: 53 -> 53, of which waited for: 11 -> 11; matrix products, arithmetic and copies ran while one was open for 22% -> 23% of each run, Pallas kernels for 53% -> 53%
where the time goes in v6:
time: 698 us; the launch traced here: 689 us
  Pallas kernels  372 us (53%)
  other arithmetic  88.8 us (13%)
  local copies, waits for them, and re-layouts  86.8 us (12%)
  waiting for transfers between devices  85.1 us (12%)
  starting transfers between devices  41 us (6%)
  between operations  15.1 us (2%)
    pallas_call x21, Pallas kernels, call(): pl.pallas_call(run, grid_spec=spec, out_shape=out_shape, compiler_params=...  359 us
    ppermute x44, waiting for transfers between devices, flip(): return lax.ppermute(a, axis, SWAP)  81.4 us
    ppermute x44, starting transfers between devices, flip(): return lax.ppermute(a, axis, SWAP)  36.8 us
    unnamed x117, local copies, waits for them, and re-layouts  33.2 us
    another operation x12, local copies, waits for them, and re-layouts, rope_tables(): return tuple((jnp.tile(t, (1, LANES // HEAD_DIM)) for t in (cos, sa, sb)))  21.2 us
  transfers between devices with their start and end apart: 53, of which 11 were waited for; matrix products, arithmetic and copies ran while one was open for 23% of the time, Pallas kernels for 53%

profile of v6, /device:TPU:0, one launch (start us, length us, event | category | flops | bytes accessed | tf_op | source)
XLA Modules:
  0.0 689.0 jit_solution(8472341423621102971)
XLA Ops:
  15.0 11.9 %collective-permute-done = bf16[128,2048]{1,0:T(8,128)(2,1)S(1)} collective-permute-done((bf16[128,2048]{1,0:T(8,128)(2,1)S(1)}, bf16[128,2048]{1,0:T(8,128)(2,1)S(1)}, u32[]{:S(2)}, u32[]{:S(2)}) %collective-permute-start) | collective-permute-done | bytes 524320 | tf_op jit(solution)/shard_map/ppermute | solution.py:527
  71.7 21.0 %collective-permute-done.5.refs_0_ = bf16[512,2048]{1,0:T(8,128)(2,1)} collective-permute-done((bf16[512,2048]{1,0:T(8,128)(2,1)}, bf16[512,2048]{1,0:T(8,128)(2,1)}, u32[]{:S(2)}, u32[]{:S(2)}) %collective-permute-start.5) | collective-permute-done | bytes 2097184 | tf_op jit(solution)/shard_map/ppermute | solution.py:527
  98.8 19.6 %collective-permute-done.7.refs_1_ = bf16[256,2048]{1,0:T(8,128)(2,1)} collective-permute-done((bf16[256,2048]{1,0:T(8,128)(2,1)}, bf16[256,2048]{1,0:T(8,128)(2,1)}, u32[]{:S(2)}, u32[]{:S(2)}) %collective-permute-start.7) | collective-permute-done | bytes 1048608 | tf_op jit(solution)/shard_map/ppermute | solution.py:527
  137.8 14.7 %assemble_heads.1 = (bf16[2048,1536]{1,0:T(8,128)(2,1)}, bf16[2048,512]{1,0:T(8,128)(2,1)}, bf16[2,2048,1024]{2,1,0:T(8,128)(2,1)}) custom-call(s32[2]{0:T(128)} %pad_add_fusion.refs_0_, bf16[512,2048]{1,0:T(8,128)(2,1)} %pad_maximum_fusion.1.refs_1_, bf16[512,2048]{1,0:T(8,128)(2,1)} %collective-permute-done.1.refs_2_, bf16[512,2048]{1,0:T(8,128)(2,1)} %tie.34.refs_3_, ...), custom_call_target="tpu_custom_call" | custom-call | flops 3500000000 | bytes 3500001 | tf_op jit(solution)/shard_map/assemble_heads/pallas_call | solution.py:52
  155.1 11.9 %project.4.refs_1_.refs_0_.refs_2_ = f32[1024,1536]{1,0:T(8,128)} custom-call(bf16[1024,2048]{1,0:T(8,128)(2,1)} %all-gather.5.cloned.1.call-done.refs_0_.refs_4_.refs_1_, bf16[2048,1536]{1,0:T(8,128)(2,1)} %get-tuple-element.44.refs_1_.refs_3_), custom_call_target="tpu_custom_call" | custom-call | flops 12499999744 | bytes 12500001 | tf_op jit(solution)/shard_map/project/pallas_call | solution.py:52
  174.1 17.3 %attention.2 = (bf16[1024,512]{1,0:T(8,128)(2,1)}, bf16[3,1024,512]{2,1,0:T(8,128)(2,1)}, f32[32,1024]{1,0:T(8,128)}) custom-call(f32[1024,1536]{1,0:T(8,128)} %project.4.refs_1_.refs_0_.refs_2_, f32[1024,1536]{1,0:T(8,128)} %project.4.refs_1_.refs_0_.refs_2_, f32[1024,1536]{1,0:T(8,128)} %project.4.refs_1_.refs_0_.refs_2_, f32[1,1536]{1,0:T(1,128)} %bitcast.216, ...), custom_call_target="tpu_custom_call" | custom-call | flops 24999999488 | bytes 25000000 | tf_op jit(solution)/shard_map/attention/pallas_call | solution.py:52
  193.3 17.5 %mlp_act.2 = (bf16[1024,2048]{1,0:T(8,128)(2,1)}, bf16[1024,2048]{1,0:T(8,128)(2,1)}) custom-call(bf16[1024,2048]{1,0:T(8,128)(2,1)} %all-gather.5.cloned.1.call-done.refs_0_.refs_4_.refs_1_, bf16[2,2048,1024]{2,1,0:T(8,128)(2,1)} %get-tuple-element.43.refs_1_.refs_2_, f32[1,2048]{1,0:T(1,128)} %bitcast.214, ...), custom_call_target="tpu_custom_call" | custom-call | flops 24999999488 | bytes 25000000 | tf_op jit(solution)/shard_map/mlp_act/pallas_call | solution.py:52
  211.3 7.9 %assemble.1.refs_2_.refs_1_ = bf16[2,2048,1024]{2,1,0:T(8,128)(2,1)} custom-call(s32[2]{0:T(128)} %pad_add_fusion.refs_0_, bf16[512,1024]{1,0:T(8,128)(2,1)} %bitcast.189, bf16[512,1024]{1,0:T(8,128)(2,1)} %collective-permute-done.17.refs_2_, bf16[512,1024]{1,0:T(8,128)(2,1)} %tie.40.refs_3_, bf16[512,1024]{1,0:T(8,128)(2,1)} %collective-permute-done.18.refs_4_, ...), custom_call_target="tpu_custom_call" | custom-call | flops 2000000000 | bytes 2000001 | tf_op jit(solution)/shard_map/assemble/pallas_call | solution.py:52
  219.2 16.0 %mixed_part.2.refs_1_.refs_2_ = bf16[1024,2048]{1,0:T(8,128)(2,1)} custom-call(bf16[1024,2048]{1,0:T(8,128)(2,1)} %get-tuple-element.47.refs_9_.refs_0_.refs_1_.refs_3_, bf16[1024,512]{1,0:T(8,128)(2,1)} %get-tuple-element.46.refs_3_.refs_1_.refs_2_.refs_7_, bf16[2,2048,1024]{2,1,0:T(8,128)(2,1)} %assemble.1.refs_2_.refs_1_, ...), custom_call_target="tpu_custom_call" | custom-call | flops 15000000512 | bytes 15000001 | tf_op jit(solution)/shard_map/mixed_part/pallas_call | solution.py:52
  237.9 5.9 project.5.refs_3_
  243.8 22.7 %attention_grad.2 = (bf16[3,1024,512]{2,1,0:T(8,128)(2,1)}, f32[8,512]{1,0:T(8,128)}) custom-call(bf16[3,1024,512]{2,1,0:T(8,128)(2,1)} %get-tuple-element.49.refs_0_, f32[32,1024]{1,0:T(8,128)} %get-tuple-element.50.refs_1_, bf16[1024,512]{1,0:T(8,128)(2,1)} %get-tuple-element.46.refs_3_.refs_1_.refs_2_.refs_7_, bf16[1024,512]{1,0:T(8,128)(2,1)} %project.5.refs_3_, ...), custom_call_target="tpu_custom_call" | custom-call | flops 24999999488 | bytes 25000000 | tf_op jit(solution)/shard_map/attention_grad/pallas_call | solution.py:52
  266.5 14.0 %mlp_pre.2 = (bf16[1024,2048]{1,0:T(8,128)(2,1)}, f32[8,2048]{1,0:T(8,128)}) custom-call(bf16[1024,2048]{1,0:T(8,128)(2,1)} %all-gather.7.cloned.1.call-done.refs_0_.refs_1_.refs_5_, bf16[2,2048,1024]{2,1,0:T(8,128)(2,1)} %assemble.1.refs_2_.refs_1_, bf16[1024,2048]{1,0:T(8,128)(2,1)} %get-tuple-element.48.refs_2_, ...), custom_call_target="tpu_custom_call" | custom-call | flops 15000000512 | bytes 15000001 | tf_op jit(solution)/shard_map/mlp_pre/pallas_call | solution.py:52
  280.5 22.5 %back_part.2 = (bf16[1024,2048]{1,0:T(8,128)(2,1)}, f32[8,2048]{1,0:T(8,128)}) custom-call(bf16[1024,2048]{1,0:T(8,128)(2,1)} %get-tuple-element.52.refs_0_.refs_3_, bf16[3,1024,512]{2,1,0:T(8,128)(2,1)} %get-tuple-element.51.refs_3_.refs_1_, bf16[2,2048,1024]{2,1,0:T(8,128)(2,1)} %get-tuple-element.43.refs_1_.refs_2_, ...), custom_call_target="tpu_custom_call" | custom-call | flops 24999999488 | bytes 25000000 | tf_op jit(solution)/shard_map/back_part/pallas_call | solution.py:52
  303.0 7.6 %pad_maximum_fusion = bf16[4,2,256,2048]{3,2,1,0:T(8,128)(2,1)} fusion(bf16[4,1,256,2048]{3,2,1,0:T(8,128)(2,1)} %bitcast.196, bf16[4,1,256,2048]{3,2,1,0:T(8,128)(2,1)} %bitcast.186), kind=kLoop, calls=%fused_computation | loop fusion | flops 4194304 | bytes 16777216 | tf_op jit(solution)/shard_map/stack | solution.py:796
  312.3 11.9 %project.6.refs_0_.refs_1_.refs_2_ = f32[1024,1536]{1,0:T(8,128)} custom-call(bf16[1024,2048]{1,0:T(8,128)(2,1)} %all-gather.9.cloned.1.call-done.refs_0_.refs_2_.refs_4_, bf16[2048,1536]{1,0:T(8,128)(2,1)} %get-tuple-element.44.refs_1_.refs_3_, bf16[1024,2048]{1,0:T(8,128)(2,1)} %get-tuple-element.53.refs_2_), custom_call_target="tpu_custom_call" | custom-call | flops 12499999744 | bytes 12500001 | tf_op jit(solution)/shard_map/project/pallas_call | solution.py:52
  324.3 17.3 %attention.3 = (bf16[1024,512]{1,0:T(8,128)(2,1)}, bf16[3,1024,512]{2,1,0:T(8,128)(2,1)}, f32[32,1024]{1,0:T(8,128)}) custom-call(f32[1024,1536]{1,0:T(8,128)} %project.6.refs_0_.refs_1_.refs_2_, f32[1024,1536]{1,0:T(8,128)} %project.6.refs_0_.refs_1_.refs_2_, f32[1024,1536]{1,0:T(8,128)} %project.6.refs_0_.refs_1_.refs_2_, f32[1,1536]{1,0:T(1,128)} %bitcast.219, ...), custom_call_target="tpu_custom_call" | custom-call | flops 24999999488 | bytes 25000000 | tf_op jit(solution)/shard_map/attention/pallas_call | solution.py:52
  341.6 17.6 %mlp_act.3 = (bf16[1024,2048]{1,0:T(8,128)(2,1)}, bf16[1024,2048]{1,0:T(8,128)(2,1)}) custom-call(bf16[1024,2048]{1,0:T(8,128)(2,1)} %all-gather.9.cloned.1.call-done.refs_0_.refs_2_.refs_4_, bf16[2,2048,1024]{2,1,0:T(8,128)(2,1)} %get-tuple-element.43.refs_1_.refs_2_, f32[1,2048]{1,0:T(1,128)} %bitcast.215, ...), custom_call_target="tpu_custom_call" | custom-call | flops 24999999488 | bytes 25000000 | tf_op jit(solution)/shard_map/mlp_act/pallas_call | solution.py:52
  359.1 14.8 %mlp_pre.3 = (bf16[1024,2048]{1,0:T(8,128)(2,1)}, f32[8,2048]{1,0:T(8,128)}) custom-call(bf16[1024,2048]{1,0:T(8,128)(2,1)} %all-gather.11.cloned.1.call-done.refs_0_.refs_2_.refs_6_, bf16[2,2048,1024]{2,1,0:T(8,128)(2,1)} %assemble.1.refs_2_.refs_1_, bf16[1024,2048]{1,0:T(8,128)(2,1)} %get-tuple-element.58.refs_2_), custom_call_target="tpu_custom_call" | custom-call | flops 15000000512 | bytes 15000001 | tf_op jit(solution)/shard_map/mlp_pre/pallas_call | solution.py:52
  373.9 25.5 %weight_grad.2 = (bf16[2,2,512,1024]{3,2,1,0:T(8,128)(2,1)}, bf16[2,2,512,1024]{3,2,1,0:T(8,128)(2,1)}) custom-call(s32[2]{0:T(128)} %pad_add_fusion.refs_0_, bf16[1024,2048]{1,0:T(8,128)(2,1)} %all-gather.5.cloned.1.call-done.refs_0_.refs_4_.refs_1_, bf16[1024,2048]{1,0:T(8,128)(2,1)} %all-gather.9.cloned.1.call-done.refs_0_.refs_2_.refs_4_, ...), custom_call_target="tpu_custom_call" | custom-call | flops 24999999488 | bytes 25000000 | tf_op jit(solution)/shard_map/weight_grad/pallas_call | solution.py:52
  399.8 25.1 %weight_grad.3 = (bf16[2,2,512,1024]{3,2,1,0:T(8,128)(2,1)}, bf16[2,2,512,1024]{3,2,1,0:T(8,128)(2,1)}) custom-call(s32[2]{0:T(128)} %pad_add_fusion.refs_0_, bf16[1024,2048]{1,0:T(8,128)(2,1)} %all-gather.7.cloned.1.call-done.refs_0_.refs_1_.refs_5_, bf16[1024,2048]{1,0:T(8,128)(2,1)} %all-gather.11.cloned.1.call-done.refs_0_.refs_2_.refs_6_, ...), custom_call_target="tpu_custom_call" | custom-call | flops 24999999488 | bytes 25000000 | tf_op jit(solution)/shard_map/weight_grad/pallas_call | solution.py:52
  426.3 4.1 slice_add_fusion.4
  430.4 16.7 %mixed_part.3.refs_2_ = bf16[1024,2048]{1,0:T(8,128)(2,1)} custom-call(bf16[1024,2048]{1,0:T(8,128)(2,1)} %get-tuple-element.57.refs_4_.refs_0_, bf16[1024,512]{1,0:T(8,128)(2,1)} %get-tuple-element.56.refs_3_.refs_1_.refs_2_.refs_8_, bf16[2,2048,1024]{2,1,0:T(8,128)(2,1)} %assemble.1.refs_2_.refs_1_, bf16[2048,512]{1,0:T(8,128)(2,1)} %get-tuple-element.45.refs_1_.refs_3_, ...), custom_call_target="tpu_custom_call" | custom-call | flops 15000000512 | bytes 15000001 | tf_op jit(solution)/shard_map/mixed_part/pallas_call | solution.py:52
  450.5 6.2 project.7.refs_3_
  456.7 22.9 %attention_grad.3 = (bf16[3,1024,512]{2,1,0:T(8,128)(2,1)}, f32[8,512]{1,0:T(8,128)}) custom-call(bf16[3,1024,512]{2,1,0:T(8,128)(2,1)} %get-tuple-element.54.refs_0_, f32[32,1024]{1,0:T(8,128)} %get-tuple-element.55.refs_1_, bf16[1024,512]{1,0:T(8,128)(2,1)} %get-tuple-element.56.refs_3_.refs_1_.refs_2_.refs_8_, bf16[1024,512]{1,0:T(8,128)(2,1)} %project.7.refs_3_, ...), custom_call_target="tpu_custom_call" | custom-call | flops 24999999488 | bytes 25000000 | tf_op jit(solution)/shard_map/attention_grad/pallas_call | solution.py:52
  498.0 21.9 %back_part.3 = (bf16[1024,2048]{1,0:T(8,128)(2,1)}, f32[8,2048]{1,0:T(8,128)}) custom-call(bf16[1024,2048]{1,0:T(8,128)(2,1)} %get-tuple-element.59.refs_4_.refs_0_, bf16[3,1024,512]{2,1,0:T(8,128)(2,1)} %get-tuple-element.63.refs_1_.refs_4_, bf16[2,2048,1024]{2,1,0:T(8,128)(2,1)} %get-tuple-element.43.refs_1_.refs_2_, ...), custom_call_target="tpu_custom_call" | custom-call | flops 24999999488 | bytes 25000000 | tf_op jit(solution)/shard_map/back_part/pallas_call | solution.py:52
  528.8 4.3 fusion.23.refs_11_
  533.1 28.6 %heads_grad.1 = (bf16[2,2,512,1024]{3,2,1,0:T(8,128)(2,1)}, bf16[2,2,512,1024]{3,2,1,0:T(8,128)(2,1)}) custom-call(s32[2]{0:T(128)} %pad_add_fusion.refs_0_, bf16[1024,2048]{1,0:T(8,128)(2,1)} %all-gather.5.cloned.1.call-done.refs_0_.refs_4_.refs_1_, bf16[1024,2048]{1,0:T(8,128)(2,1)} %all-gather.9.cloned.1.call-done.refs_0_.refs_2_.refs_4_, ...), custom_call_target="tpu_custom_call" | custom-call | flops 24999999488 | bytes 25000000 | tf_op jit(solution)/shard_map/heads_grad/pallas_call | solution.py:52
  571.1 6.8 collective-permute-done.30.refs_0_
  578.0 4.2 slice_add_fusion
  624.8 5.8 norm_grad.3.refs_0_
  635.4 11.2 %collective-permute-done.44 = bf16[512,1024]{1,0:T(8,128)(2,1)} collective-permute-done((bf16[512,1024]{1,0:T(8,128)(2,1)S(1)}, bf16[512,1024]{1,0:T(8,128)(2,1)}, u32[]{:S(2)}, u32[]{:S(2)}) %collective-permute-start.44) | collective-permute-done | bytes 1048608 | tf_op jit(solution)/shard_map/ppermute | solution.py:527
  672.9 4.8 collective-permute-done.43.kept_ref.got_ref
  (374 shorter events, 213.6 us)
Async XLA Ops:
  7.2 147.9 %all-gather.5.cloned.1.call-start = ((), (), s32[]{:S(2)}) async-start(), calls=%async_computation.3 | async-start | bytes 5242880 | tf_op jit(solution)/shard_map/all_gather | solution.py:761
  28.1 209.8 %all-gather.7.cloned.1.call-start = ((), (), s32[]{:S(2)}) async-start(), calls=%async_computation.4 | async-start | bytes 5242880 | tf_op jit(solution)/shard_map/all_gather | solution.py:761
  46.0 46.7 %collective-permute-start.5 = (bf16[512,2048]{1,0:T(8,128)(2,1)}, bf16[512,2048]{1,0:T(8,128)(2,1)}, u32[]{:S(2)}, u32[]{:S(2)}) collective-permute-start(bf16[512,2048]{1,0:T(8,128)(2,1)} %tie.33), channel_id=1, source_target_pairs={{0,16},{16,0},{1,17},{17,1},{2,18},{18,2},{3,19},{19,3},{4,20},{20... | collective-permute-start | bytes 6291464 | tf_op jit(solution)/shard_map/ppermute | solution.py:527
  47.6 47.9 %collective-permute-start.3 = (bf16[512,2048]{1,0:T(8,128)(2,1)}, bf16[512,2048]{1,0:T(8,128)(2,1)}, u32[]{:S(2)}, u32[]{:S(2)}) collective-permute-start(bf16[512,2048]{1,0:T(8,128)(2,1)} %tie.33), channel_id=1, source_target_pairs={{0,1},{1,0},{2,3},{3,2},{4,5},{5,4},{6,7},{7,6},{8,9},{9,8},{10,11... | collective-permute-start | bytes 6291464 | tf_op jit(solution)/shard_map/ppermute | solution.py:527
  48.6 263.7 %all-gather.9.cloned.1.call-start = ((), (), s32[]{:S(2)}) async-start(), calls=%async_computation.6 | async-start | bytes 5242880 | tf_op jit(solution)/shard_map/all_gather | solution.py:761
  98.3 37.5 %collective-permute-start.1 = (bf16[512,2048]{1,0:T(8,128)(2,1)}, bf16[512,2048]{1,0:T(8,128)(2,1)}, u32[]{:S(2)}, u32[]{:S(2)}) collective-permute-start(bf16[512,2048]{1,0:T(8,128)(2,1)} %pad_maximum_fusion.1.refs_1_), channel_id=1, source_target_pairs={{0,8},{8,0},{1,9},{9,1},{2,10},{10,2},{3,11},{11,3},{4,12},{12,4},... | collective-permute-start | bytes 6291464 | tf_op jit(solution)/shard_map/ppermute | solution.py:527
  98.3 37.5 %collective-permute-start.6 = (bf16[512,2048]{1,0:T(8,128)(2,1)}, bf16[512,2048]{1,0:T(8,128)(2,1)}, u32[]{:S(2)}, u32[]{:S(2)}) collective-permute-start(bf16[512,2048]{1,0:T(8,128)(2,1)} %tie.35.refs_5_), channel_id=1, source_target_pairs={{0,8},{8,0},{1,9},{9,1},{2,10},{10,2},{3,11},{11,3},{4,12},{12,4},... | collective-permute-start | bytes 6291464 | tf_op jit(solution)/shard_map/ppermute | solution.py:527
  98.8 37.5 %collective-permute-start.4 = (bf16[512,2048]{1,0:T(8,128)(2,1)}, bf16[512,2048]{1,0:T(8,128)(2,1)}, u32[]{:S(2)}, u32[]{:S(2)}) collective-permute-start(bf16[512,2048]{1,0:T(8,128)(2,1)} %tie.34.refs_3_), channel_id=1, source_target_pairs={{0,8},{8,0},{1,9},{9,1},{2,10},{10,2},{3,11},{11,3},{4,12},{12,4},... | collective-permute-start | bytes 6291464 | tf_op jit(solution)/shard_map/ppermute | solution.py:527
  135.8 75.5 %collective-permute-start.17 = (bf16[512,1024]{1,0:T(8,128)(2,1)}, bf16[512,1024]{1,0:T(8,128)(2,1)}, u32[]{:S(2)}, u32[]{:S(2)}) collective-permute-start(bf16[512,1024]{1,0:T(8,128)(2,1)} %bitcast.188), channel_id=1, source_target_pairs={{0,8},{8,0},{1,9},{9,1},{2,10},{10,2},{3,11},{11,3},{4,12},{12,4},... | collective-permute-start | bytes 3145736 | tf_op jit(solution)/shard_map/ppermute | solution.py:527
  135.8 33.3 %collective-permute-start.14 = (bf16[512,1024]{1,0:T(8,128)(2,1)}, bf16[512,1024]{1,0:T(8,128)(2,1)}, u32[]{:S(2)}, u32[]{:S(2)}) collective-permute-start(bf16[512,1024]{1,0:T(8,128)(2,1)} %tie.38), channel_id=1, source_target_pairs={{0,1},{1,0},{2,3},{3,2},{4,5},{5,4},{6,7},{7,6},{8,9},{9,8},{10,11... | collective-permute-start | bytes 3145736 | tf_op jit(solution)/shard_map/ppermute | solution.py:527
  136.3 30.7 %collective-permute-start.13 = (bf16[512,1024]{1,0:T(8,128)(2,1)}, bf16[512,1024]{1,0:T(8,128)(2,1)}, u32[]{:S(2)}, u32[]{:S(2)}) collective-permute-start(bf16[512,1024]{1,0:T(8,128)(2,1)} %tie.38), channel_id=1, source_target_pairs={{0,16},{16,0},{1,17},{17,1},{2,18},{18,2},{3,19},{19,3},{4,20},{20... | collective-permute-start | bytes 3145736 | tf_op jit(solution)/shard_map/ppermute | solution.py:527
  154.8 204.3 %all-gather.11.cloned.1.call-start = ((), (), s32[]{:S(2)}) async-start(), calls=%async_computation.7 | async-start | bytes 5242880 | tf_op jit(solution)/shard_map/all_gather | solution.py:761
  168.1 43.2 %collective-permute-start.19 = (bf16[512,1024]{1,0:T(8,128)(2,1)}, bf16[512,1024]{1,0:T(8,128)(2,1)}, u32[]{:S(2)}, u32[]{:S(2)}) collective-permute-start(bf16[512,1024]{1,0:T(8,128)(2,1)} %tie.39.refs_5_), channel_id=1, source_target_pairs={{0,8},{8,0},{1,9},{9,1},{2,10},{10,2},{3,11},{11,3},{4,12},{12,4},... | collective-permute-start | bytes 3145736 | tf_op jit(solution)/shard_map/ppermute | solution.py:527
  170.9 40.4 %collective-permute-start.18 = (bf16[512,1024]{1,0:T(8,128)(2,1)}, bf16[512,1024]{1,0:T(8,128)(2,1)}, u32[]{:S(2)}, u32[]{:S(2)}) collective-permute-start(bf16[512,1024]{1,0:T(8,128)(2,1)} %tie.40.refs_3_), channel_id=1, source_target_pairs={{0,8},{8,0},{1,9},{9,1},{2,10},{10,2},{3,11},{11,3},{4,12},{12,4},... | collective-permute-start | bytes 3145736 | tf_op jit(solution)/shard_map/ppermute | solution.py:527
  237.4 351.4 %reduce-scatter.4.cloned.1.call-start = ((), (), s32[]{:S(2)}) async-start(), calls=%async_computation.5 | async-start | bytes 10485760 | tf_op jit(solution)/shard_map/reduce_scatter | solution.py:797
  310.6 322.1 %reduce-scatter.6.cloned.1.call-start = ((), (), s32[]{:S(2)}) async-start(), calls=%async_computation.8 | async-start | bytes 5242880 | tf_op jit(solution)/shard_map/reduce_scatter | solution.py:779
  399.5 26.8 %collective-permute-start.22 = (bf16[2,2,512,1024]{3,2,1,0:T(8,128)(2,1)}, bf16[2,2,512,1024]{3,2,1,0:T(8,128)(2,1)}, u32[]{:S(2)}, u32[]{:S(2)}) collective-permute-start(bf16[2,2,512,1024]{3,2,1,0:T(8,128)(2,1)} %get-tuple-element.61), channel_id=1, source_target_pairs={{0,8},{8,0},{1,9},{9,1},{2,10},{10,2},{3,11},{11,3},{4,12},{12,4},... | collective-permute-start | bytes 12582920 | tf_op jit(solution)/shard_map/ppermute | solution.py:527
  424.9 54.7 %collective-permute-start.23 = (bf16[2,2,512,1024]{3,2,1,0:T(8,128)(2,1)}, bf16[2,2,512,1024]{3,2,1,0:T(8,128)(2,1)}, u32[]{:S(2)}, u32[]{:S(2)}) collective-permute-start(bf16[2,2,512,1024]{3,2,1,0:T(8,128)(2,1)} %get-tuple-element.64), channel_id=1, source_target_pairs={{0,8},{8,0},{1,9},{9,1},{2,10},{10,2},{3,11},{11,3},{4,12},{12,4},... | collective-permute-start | bytes 12582920 | tf_op jit(solution)/shard_map/ppermute | solution.py:527
  448.2 46.0 %collective-permute-start.26 = (bf16[256,1024]{1,0:T(8,128)(2,1)}, bf16[256,1024]{1,0:T(8,128)(2,1)}, u32[]{:S(2)}, u32[]{:S(2)}) collective-permute-start(bf16[256,1024]{1,0:T(8,128)(2,1)} %get-tuple-element.141), channel_id=1, source_target_pairs={{0,1},{1,0},{2,3},{3,2},{4,5},{5,4},{6,7},{7,6},{8,9},{9,8},{10,11... | collective-permute-start | bytes 1572872 | tf_op jit(solution)/shard_map/ppermute | solution.py:527
  449.8 39.3 %collective-permute-start.25 = (bf16[256,1024]{1,0:T(8,128)(2,1)}, bf16[256,1024]{1,0:T(8,128)(2,1)}, u32[]{:S(2)}, u32[]{:S(2)}) collective-permute-start(bf16[256,1024]{1,0:T(8,128)(2,1)} %get-tuple-element.142), channel_id=1, source_target_pairs={{0,16},{16,0},{1,17},{17,1},{2,18},{18,2},{3,19},{19,3},{4,20},{20... | collective-permute-start | bytes 1572872 | tf_op jit(solution)/shard_map/ppermute | solution.py:527
  450.4 211.6 %reduce-scatter.8.cloned.1.call-start = ((), (), s32[]{:S(2)}) async-start(), calls=%async_computation.9 | async-start | bytes 5242880 | tf_op jit(solution)/shard_map/reduce_scatter | solution.py:779
  487.3 37.9 %collective-permute-start.27 = (bf16[256,1024]{1,0:T(8,128)(2,1)}, bf16[256,1024]{1,0:T(8,128)(2,1)}, u32[]{:S(2)}, u32[]{:S(2)}) collective-permute-start(bf16[256,1024]{1,0:T(8,128)(2,1)} %get-tuple-element.139), channel_id=1, source_target_pairs={{0,1},{1,0},{2,3},{3,2},{4,5},{5,4},{6,7},{7,6},{8,9},{9,8},{10,11... | collective-permute-start | bytes 1572872 | tf_op jit(solution)/shard_map/ppermute | solution.py:527
  487.7 33.5 %collective-permute-start.24 = (bf16[256,1024]{1,0:T(8,128)(2,1)}, bf16[256,1024]{1,0:T(8,128)(2,1)}, u32[]{:S(2)}, u32[]{:S(2)}) collective-permute-start(bf16[256,1024]{1,0:T(8,128)(2,1)} %get-tuple-element.140), channel_id=1, source_target_pairs={{0,16},{16,0},{1,17},{17,1},{2,18},{18,2},{3,19},{19,3},{4,20},{20... | collective-permute-start | bytes 1572872 | tf_op jit(solution)/shard_map/ppermute | solution.py:527
  492.5 36.3 %collective-permute-start.28 = (bf16[512,1024]{1,0:T(8,128)(2,1)}, bf16[512,1024]{1,0:T(8,128)(2,1)}, u32[]{:S(2)}, u32[]{:S(2)}) collective-permute-start(bf16[512,1024]{1,0:T(8,128)(2,1)} %pad_maximum_fusion.7.refs_5_), channel_id=1, source_target_pairs={{0,1},{1,0},{2,3},{3,2},{4,5},{5,4},{6,7},{7,6},{8,9},{9,8},{10,11... | collective-permute-start | bytes 3145736 | tf_op jit(solution)/shard_map/ppermute | solution.py:527
  497.3 31.4 %collective-permute-start.29 = (bf16[512,1024]{1,0:T(8,128)(2,1)}, bf16[512,1024]{1,0:T(8,128)(2,1)}, u32[]{:S(2)}, u32[]{:S(2)}) collective-permute-start(bf16[512,1024]{1,0:T(8,128)(2,1)} %pad_maximum_fusion.8.refs_6_), channel_id=1, source_target_pairs={{0,16},{16,0},{1,17},{17,1},{2,18},{18,2},{3,19},{19,3},{4,20},{20... | collective-permute-start | bytes 3145736 | tf_op jit(solution)/shard_map/ppermute | solution.py:527
  520.8 40.9 %collective-permute-start.33 = (f32[7936]{0:T(1024)S(1)}, f32[7936]{0:T(1024)S(1)}, u32[]{:S(2)}, u32[]{:S(2)}) collective-permute-start(f32[7936]{0:T(1024)S(1)} %pad_maximum_fusion.17), channel_id=1, source_target_pairs={{0,1},{1,0},{2,3},{3,2},{4,5},{5,4},{6,7},{7,6},{8,9},{9,8},{10,11... | collective-permute-start | bytes 95240 | tf_op jit(solution)/shard_map/ppermute | solution.py:527
  523.5 41.0 %collective-permute-start.31 = (bf16[512,1024]{1,0:T(8,128)(2,1)}, bf16[512,1024]{1,0:T(8,128)(2,1)S(1)}, u32[]{:S(2)}, u32[]{:S(2)}) collective-permute-start(bf16[512,1024]{1,0:T(8,128)(2,1)} %pad_maximum_fusion.9.refs_9_), channel_id=1, source_target_pairs={{0,1},{1,0},{2,3},{3,2},{4,5},{5,4},{6,7},{7,6},{8,9},{9,8},{10,11... | collective-permute-start | bytes 3145736 | tf_op jit(solution)/shard_map/ppermute | solution.py:527
  527.4 38.0 %collective-permute-start.32 = (bf16[512,1024]{1,0:T(8,128)(2,1)}, bf16[512,1024]{1,0:T(8,128)(2,1)S(1)}, u32[]{:S(2)}, u32[]{:S(2)}) collective-permute-start(bf16[512,1024]{1,0:T(8,128)(2,1)} %pad_maximum_fusion.10.refs_10_), channel_id=1, source_target_pairs={{0,16},{16,0},{1,17},{17,1},{2,18},{18,2},{3,19},{19,3},{4,20},{20... | collective-permute-start | bytes 3145736 | tf_op jit(solution)/shard_map/ppermute | solution.py:527
  594.0 30.8 %collective-permute-start.34 = (bf16[128,2048]{1,0:T(8,128)(2,1)}, bf16[128,2048]{1,0:T(8,128)(2,1)}, u32[]{:S(2)}, u32[]{:S(2)}) collective-permute-start(bf16[128,2048]{1,0:T(8,128)(2,1)} %broadcast_select_fusion.12), channel_id=1, source_target_pairs={{0,1},{1,0},{2,3},{3,2},{4,5},{5,4},{6,7},{7,6},{8,9},{9,8},{10,11... | collective-permute-start | bytes 1572872 | tf_op jit(solution)/shard_map/ppermute | solution.py:527
  598.0 26.0 %collective-permute-start.39 = (bf16[128,2048]{1,0:T(8,128)(2,1)}, bf16[128,2048]{1,0:T(8,128)(2,1)S(1)}, u32[]{:S(2)}, u32[]{:S(2)}) collective-permute-start(bf16[128,2048]{1,0:T(8,128)(2,1)} %get-tuple-element.137), channel_id=1, source_target_pairs={{0,1},{1,0},{2,3},{3,2},{4,5},{5,4},{6,7},{7,6},{8,9},{9,8},{10,11... | collective-permute-start | bytes 1572872 | tf_op jit(solution)/shard_map/ppermute | solution.py:527
  620.1 26.5 %collective-permute-start.44 = (bf16[512,1024]{1,0:T(8,128)(2,1)S(1)}, bf16[512,1024]{1,0:T(8,128)(2,1)}, u32[]{:S(2)}, u32[]{:S(2)}) collective-permute-start(bf16[512,1024]{1,0:T(8,128)(2,1)S(1)} %copy-done.6), channel_id=1, source_target_pairs={{0,1},{1,0},{2,3},{3,2},{4,5},{5,4},{6,7},{7,6},{8,9},{9,8},{10,11... | collective-permute-start | bytes 3145736 | tf_op jit(solution)/shard_map/ppermute | solution.py:527
  621.2 25.4 %collective-permute-start.45 = (bf16[512,1024]{1,0:T(8,128)(2,1)S(1)}, bf16[512,1024]{1,0:T(8,128)(2,1)}, u32[]{:S(2)}, u32[]{:S(2)}) collective-permute-start(bf16[512,1024]{1,0:T(8,128)(2,1)S(1)} %copy-done.5), channel_id=1, source_target_pairs={{0,16},{16,0},{1,17},{17,1},{2,18},{18,2},{3,19},{19,3},{4,20},{20... | collective-permute-start | bytes 3145736 | tf_op jit(solution)/shard_map/ppermute | solution.py:527
  (74 other events, 684.7 us)
Sparse Core Ops, SparseCore 0:
  28.2 82.2 all-gather.4
  112.1 79.2 all-gather.6
  193.6 79.2 all-gather.8
  274.9 79.2 all-gather.10
  356.4 143.0 reduce-scatter.3
  501.6 77.4 reduce-scatter.5
  581.5 78.2 reduce-scatter.7

commit v7 on v6

--- a/solution.py
+++ b/solution.py
@@ -665,7 +665,7 @@
     both = kept is not None and got is not None
     at = jnp.concatenate([at, at if got is None else 1 - at])
     kept, got = (got if kept is None else kept), (kept if got is None else got)
-    tile = min(64, shard)
+    tile = min(32, shard)
 
     def kernel(at_ref, x_ref, c_ref, kept_ref, got_ref, gain_ref, *refs):
         x = x_ref[...].astype(f32)

time: 698 us -> 699 us (level)
  transfers between devices with their start and end apart: 53 -> 53, of which waited for: 11 -> 11; matrix products, arithmetic and copies ran while one was open for 23% -> 23% of each run, Pallas kernels for 53% -> 54%
where the time goes in v7:
time: 699 us; the launch traced here: 690 us
  Pallas kernels  377 us (54%)
  other arithmetic  88.8 us (13%)
  local copies, waits for them, and re-layouts  86.8 us (12%)
  waiting for transfers between devices  81.5 us (12%)
  starting transfers between devices  41 us (6%)
  between operations  15.1 us (2%)
    pallas_call x21, Pallas kernels, call(): pl.pallas_call(run, grid_spec=spec, out_shape=out_shape, compiler_params=...  359 us
    ppermute x44, waiting for transfers between devices, flip(): return lax.ppermute(a, axis, SWAP)  77.8 us
    ppermute x44, starting transfers between devices, flip(): return lax.ppermute(a, axis, SWAP)  36.7 us
    unnamed x117, local copies, waits for them, and re-layouts  33.2 us
    another operation x12, local copies, waits for them, and re-layouts, rope_tables(): return tuple((jnp.tile(t, (1, LANES // HEAD_DIM)) for t in (cos, sa, sb)))  21.2 us
    pallas_call x3, Pallas kernels, norm_grad(): pl.pallas_call(kernel, grid_spec=pltpu.PrefetchScalarGridSpec(num_scalar_...  18.2 us
  transfers between devices with their start and end apart: 53, of which 11 were waited for; matrix products, arithmetic and copies ran while one was open for 23% of the time, Pallas kernels for 54%

profile of v7, /device:TPU:0, one launch (start us, length us, event | category | flops | bytes accessed | tf_op | source)
XLA Modules:
  0.0 690.3 jit_solution(6966654342403589354)
XLA Ops:
  15.0 11.9 %collective-permute-done = bf16[128,2048]{1,0:T(8,128)(2,1)S(1)} collective-permute-done((bf16[128,2048]{1,0:T(8,128)(2,1)S(1)}, bf16[128,2048]{1,0:T(8,128)(2,1)S(1)}, u32[]{:S(2)}, u32[]{:S(2)}) %collective-permute-start) | collective-permute-done | bytes 524320 | tf_op jit(solution)/shard_map/ppermute | solution.py:527
  71.7 21.0 %collective-permute-done.5.refs_0_ = bf16[512,2048]{1,0:T(8,128)(2,1)} collective-permute-done((bf16[512,2048]{1,0:T(8,128)(2,1)}, bf16[512,2048]{1,0:T(8,128)(2,1)}, u32[]{:S(2)}, u32[]{:S(2)}) %collective-permute-start.5) | collective-permute-done | bytes 2097184 | tf_op jit(solution)/shard_map/ppermute | solution.py:527
  98.8 19.6 %collective-permute-done.7.refs_1_ = bf16[256,2048]{1,0:T(8,128)(2,1)} collective-permute-done((bf16[256,2048]{1,0:T(8,128)(2,1)}, bf16[256,2048]{1,0:T(8,128)(2,1)}, u32[]{:S(2)}, u32[]{:S(2)}) %collective-permute-start.7) | collective-permute-done | bytes 1048608 | tf_op jit(solution)/shard_map/ppermute | solution.py:527
  137.8 14.7 %assemble_heads.1 = (bf16[2048,1536]{1,0:T(8,128)(2,1)}, bf16[2048,512]{1,0:T(8,128)(2,1)}, bf16[2,2048,1024]{2,1,0:T(8,128)(2,1)}) custom-call(s32[2]{0:T(128)} %pad_add_fusion.refs_0_, bf16[512,2048]{1,0:T(8,128)(2,1)} %pad_maximum_fusion.1.refs_1_, bf16[512,2048]{1,0:T(8,128)(2,1)} %collective-permute-done.1.refs_2_, bf16[512,2048]{1,0:T(8,128)(2,1)} %tie.34.refs_3_, ...), custom_call_target="tpu_custom_call" | custom-call | flops 3500000000 | bytes 3500001 | tf_op jit(solution)/shard_map/assemble_heads/pallas_call | solution.py:52
  155.1 11.9 %project.4.refs_1_.refs_0_.refs_2_ = f32[1024,1536]{1,0:T(8,128)} custom-call(bf16[1024,2048]{1,0:T(8,128)(2,1)} %all-gather.5.cloned.1.call-done.refs_0_.refs_4_.refs_1_, bf16[2048,1536]{1,0:T(8,128)(2,1)} %get-tuple-element.44.refs_1_.refs_3_), custom_call_target="tpu_custom_call" | custom-call | flops 12499999744 | bytes 12500001 | tf_op jit(solution)/shard_map/project/pallas_call | solution.py:52
  174.1 17.3 %attention.2 = (bf16[1024,512]{1,0:T(8,128)(2,1)}, bf16[3,1024,512]{2,1,0:T(8,128)(2,1)}, f32[32,1024]{1,0:T(8,128)}) custom-call(f32[1024,1536]{1,0:T(8,128)} %project.4.refs_1_.refs_0_.refs_2_, f32[1024,1536]{1,0:T(8,128)} %project.4.refs_1_.refs_0_.refs_2_, f32[1024,1536]{1,0:T(8,128)} %project.4.refs_1_.refs_0_.refs_2_, f32[1,1536]{1,0:T(1,128)} %bitcast.216, ...), custom_call_target="tpu_custom_call" | custom-call | flops 24999999488 | bytes 25000000 | tf_op jit(solution)/shard_map/attention/pallas_call | solution.py:52
  193.3 17.5 %mlp_act.2 = (bf16[1024,2048]{1,0:T(8,128)(2,1)}, bf16[1024,2048]{1,0:T(8,128)(2,1)}) custom-call(bf16[1024,2048]{1,0:T(8,128)(2,1)} %all-gather.5.cloned.1.call-done.refs_0_.refs_4_.refs_1_, bf16[2,2048,1024]{2,1,0:T(8,128)(2,1)} %get-tuple-element.43.refs_1_.refs_2_, f32[1,2048]{1,0:T(1,128)} %bitcast.214, ...), custom_call_target="tpu_custom_call" | custom-call | flops 24999999488 | bytes 25000000 | tf_op jit(solution)/shard_map/mlp_act/pallas_call | solution.py:52
  211.3 7.9 %assemble.1.refs_2_.refs_1_ = bf16[2,2048,1024]{2,1,0:T(8,128)(2,1)} custom-call(s32[2]{0:T(128)} %pad_add_fusion.refs_0_, bf16[512,1024]{1,0:T(8,128)(2,1)} %bitcast.189, bf16[512,1024]{1,0:T(8,128)(2,1)} %collective-permute-done.17.refs_2_, bf16[512,1024]{1,0:T(8,128)(2,1)} %tie.40.refs_3_, bf16[512,1024]{1,0:T(8,128)(2,1)} %collective-permute-done.18.refs_4_, ...), custom_call_target="tpu_custom_call" | custom-call | flops 2000000000 | bytes 2000001 | tf_op jit(solution)/shard_map/assemble/pallas_call | solution.py:52
  219.2 16.0 %mixed_part.2.refs_1_.refs_2_ = bf16[1024,2048]{1,0:T(8,128)(2,1)} custom-call(bf16[1024,2048]{1,0:T(8,128)(2,1)} %get-tuple-element.47.refs_9_.refs_0_.refs_1_.refs_3_, bf16[1024,512]{1,0:T(8,128)(2,1)} %get-tuple-element.46.refs_3_.refs_1_.refs_2_.refs_7_, bf16[2,2048,1024]{2,1,0:T(8,128)(2,1)} %assemble.1.refs_2_.refs_1_, ...), custom_call_target="tpu_custom_call" | custom-call | flops 15000000512 | bytes 15000001 | tf_op jit(solution)/shard_map/mixed_part/pallas_call | solution.py:52
  237.9 5.9 project.5.refs_3_
  243.8 22.7 %attention_grad.2 = (bf16[3,1024,512]{2,1,0:T(8,128)(2,1)}, f32[8,512]{1,0:T(8,128)}) custom-call(bf16[3,1024,512]{2,1,0:T(8,128)(2,1)} %get-tuple-element.49.refs_0_, f32[32,1024]{1,0:T(8,128)} %get-tuple-element.50.refs_1_, bf16[1024,512]{1,0:T(8,128)(2,1)} %get-tuple-element.46.refs_3_.refs_1_.refs_2_.refs_7_, bf16[1024,512]{1,0:T(8,128)(2,1)} %project.5.refs_3_, ...), custom_call_target="tpu_custom_call" | custom-call | flops 24999999488 | bytes 25000000 | tf_op jit(solution)/shard_map/attention_grad/pallas_call | solution.py:52
  266.5 14.0 %mlp_pre.2 = (bf16[1024,2048]{1,0:T(8,128)(2,1)}, f32[8,2048]{1,0:T(8,128)}) custom-call(bf16[1024,2048]{1,0:T(8,128)(2,1)} %all-gather.7.cloned.1.call-done.refs_0_.refs_1_.refs_5_, bf16[2,2048,1024]{2,1,0:T(8,128)(2,1)} %assemble.1.refs_2_.refs_1_, bf16[1024,2048]{1,0:T(8,128)(2,1)} %get-tuple-element.48.refs_2_, ...), custom_call_target="tpu_custom_call" | custom-call | flops 15000000512 | bytes 15000001 | tf_op jit(solution)/shard_map/mlp_pre/pallas_call | solution.py:52
  280.5 22.5 %back_part.2 = (bf16[1024,2048]{1,0:T(8,128)(2,1)}, f32[8,2048]{1,0:T(8,128)}) custom-call(bf16[1024,2048]{1,0:T(8,128)(2,1)} %get-tuple-element.52.refs_0_.refs_3_, bf16[3,1024,512]{2,1,0:T(8,128)(2,1)} %get-tuple-element.51.refs_3_.refs_1_, bf16[2,2048,1024]{2,1,0:T(8,128)(2,1)} %get-tuple-element.43.refs_1_.refs_2_, ...), custom_call_target="tpu_custom_call" | custom-call | flops 24999999488 | bytes 25000000 | tf_op jit(solution)/shard_map/back_part/pallas_call | solution.py:52
  303.0 7.6 %pad_maximum_fusion = bf16[4,2,256,2048]{3,2,1,0:T(8,128)(2,1)} fusion(bf16[4,1,256,2048]{3,2,1,0:T(8,128)(2,1)} %bitcast.196, bf16[4,1,256,2048]{3,2,1,0:T(8,128)(2,1)} %bitcast.186), kind=kLoop, calls=%fused_computation | loop fusion | flops 4194304 | bytes 16777216 | tf_op jit(solution)/shard_map/stack | solution.py:796
  312.3 11.9 %project.6.refs_0_.refs_1_.refs_2_ = f32[1024,1536]{1,0:T(8,128)} custom-call(bf16[1024,2048]{1,0:T(8,128)(2,1)} %all-gather.9.cloned.1.call-done.refs_0_.refs_2_.refs_4_, bf16[2048,1536]{1,0:T(8,128)(2,1)} %get-tuple-element.44.refs_1_.refs_3_, bf16[1024,2048]{1,0:T(8,128)(2,1)} %get-tuple-element.53.refs_2_), custom_call_target="tpu_custom_call" | custom-call | flops 12499999744 | bytes 12500001 | tf_op jit(solution)/shard_map/project/pallas_call | solution.py:52
  324.3 17.3 %attention.3 = (bf16[1024,512]{1,0:T(8,128)(2,1)}, bf16[3,1024,512]{2,1,0:T(8,128)(2,1)}, f32[32,1024]{1,0:T(8,128)}) custom-call(f32[1024,1536]{1,0:T(8,128)} %project.6.refs_0_.refs_1_.refs_2_, f32[1024,1536]{1,0:T(8,128)} %project.6.refs_0_.refs_1_.refs_2_, f32[1024,1536]{1,0:T(8,128)} %project.6.refs_0_.refs_1_.refs_2_, f32[1,1536]{1,0:T(1,128)} %bitcast.219, ...), custom_call_target="tpu_custom_call" | custom-call | flops 24999999488 | bytes 25000000 | tf_op jit(solution)/shard_map/attention/pallas_call | solution.py:52
  341.6 17.6 %mlp_act.3 = (bf16[1024,2048]{1,0:T(8,128)(2,1)}, bf16[1024,2048]{1,0:T(8,128)(2,1)}) custom-call(bf16[1024,2048]{1,0:T(8,128)(2,1)} %all-gather.9.cloned.1.call-done.refs_0_.refs_2_.refs_4_, bf16[2,2048,1024]{2,1,0:T(8,128)(2,1)} %get-tuple-element.43.refs_1_.refs_2_, f32[1,2048]{1,0:T(1,128)} %bitcast.215, ...), custom_call_target="tpu_custom_call" | custom-call | flops 24999999488 | bytes 25000000 | tf_op jit(solution)/shard_map/mlp_act/pallas_call | solution.py:52
  359.1 14.8 %mlp_pre.3 = (bf16[1024,2048]{1,0:T(8,128)(2,1)}, f32[8,2048]{1,0:T(8,128)}) custom-call(bf16[1024,2048]{1,0:T(8,128)(2,1)} %all-gather.11.cloned.1.call-done.refs_0_.refs_2_.refs_6_, bf16[2,2048,1024]{2,1,0:T(8,128)(2,1)} %assemble.1.refs_2_.refs_1_, bf16[1024,2048]{1,0:T(8,128)(2,1)} %get-tuple-element.58.refs_2_), custom_call_target="tpu_custom_call" | custom-call | flops 15000000512 | bytes 15000001 | tf_op jit(solution)/shard_map/mlp_pre/pallas_call | solution.py:52
  373.9 25.5 %weight_grad.2 = (bf16[2,2,512,1024]{3,2,1,0:T(8,128)(2,1)}, bf16[2,2,512,1024]{3,2,1,0:T(8,128)(2,1)}) custom-call(s32[2]{0:T(128)} %pad_add_fusion.refs_0_, bf16[1024,2048]{1,0:T(8,128)(2,1)} %all-gather.5.cloned.1.call-done.refs_0_.refs_4_.refs_1_, bf16[1024,2048]{1,0:T(8,128)(2,1)} %all-gather.9.cloned.1.call-done.refs_0_.refs_2_.refs_4_, ...), custom_call_target="tpu_custom_call" | custom-call | flops 24999999488 | bytes 25000000 | tf_op jit(solution)/shard_map/weight_grad/pallas_call | solution.py:52
  399.8 25.1 %weight_grad.3 = (bf16[2,2,512,1024]{3,2,1,0:T(8,128)(2,1)}, bf16[2,2,512,1024]{3,2,1,0:T(8,128)(2,1)}) custom-call(s32[2]{0:T(128)} %pad_add_fusion.refs_0_, bf16[1024,2048]{1,0:T(8,128)(2,1)} %all-gather.7.cloned.1.call-done.refs_0_.refs_1_.refs_5_, bf16[1024,2048]{1,0:T(8,128)(2,1)} %all-gather.11.cloned.1.call-done.refs_0_.refs_2_.refs_6_, ...), custom_call_target="tpu_custom_call" | custom-call | flops 24999999488 | bytes 25000000 | tf_op jit(solution)/shard_map/weight_grad/pallas_call | solution.py:52
  430.4 16.7 %mixed_part.3.refs_2_ = bf16[1024,2048]{1,0:T(8,128)(2,1)} custom-call(bf16[1024,2048]{1,0:T(8,128)(2,1)} %get-tuple-element.57.refs_4_.refs_0_, bf16[1024,512]{1,0:T(8,128)(2,1)} %get-tuple-element.56.refs_3_.refs_1_.refs_2_.refs_8_, bf16[2,2048,1024]{2,1,0:T(8,128)(2,1)} %assemble.1.refs_2_.refs_1_, bf16[2048,512]{1,0:T(8,128)(2,1)} %get-tuple-element.45.refs_1_.refs_3_, ...), custom_call_target="tpu_custom_call" | custom-call | flops 15000000512 | bytes 15000001 | tf_op jit(solution)/shard_map/mixed_part/pallas_call | solution.py:52
  450.5 6.2 project.7.refs_3_
  456.7 22.9 %attention_grad.3 = (bf16[3,1024,512]{2,1,0:T(8,128)(2,1)}, f32[8,512]{1,0:T(8,128)}) custom-call(bf16[3,1024,512]{2,1,0:T(8,128)(2,1)} %get-tuple-element.54.refs_0_, f32[32,1024]{1,0:T(8,128)} %get-tuple-element.55.refs_1_, bf16[1024,512]{1,0:T(8,128)(2,1)} %get-tuple-element.56.refs_3_.refs_1_.refs_2_.refs_8_, bf16[1024,512]{1,0:T(8,128)(2,1)} %project.7.refs_3_, ...), custom_call_target="tpu_custom_call" | custom-call | flops 24999999488 | bytes 25000000 | tf_op jit(solution)/shard_map/attention_grad/pallas_call | solution.py:52
  498.0 21.9 %back_part.3 = (bf16[1024,2048]{1,0:T(8,128)(2,1)}, f32[8,2048]{1,0:T(8,128)}) custom-call(bf16[1024,2048]{1,0:T(8,128)(2,1)} %get-tuple-element.59.refs_4_.refs_0_, bf16[3,1024,512]{2,1,0:T(8,128)(2,1)} %get-tuple-element.63.refs_1_.refs_4_, bf16[2,2048,1024]{2,1,0:T(8,128)(2,1)} %get-tuple-element.43.refs_1_.refs_2_, ...), custom_call_target="tpu_custom_call" | custom-call | flops 24999999488 | bytes 25000000 | tf_op jit(solution)/shard_map/back_part/pallas_call | solution.py:52
  528.8 4.3 fusion.23.refs_11_
  533.1 28.6 %heads_grad.1 = (bf16[2,2,512,1024]{3,2,1,0:T(8,128)(2,1)}, bf16[2,2,512,1024]{3,2,1,0:T(8,128)(2,1)}) custom-call(s32[2]{0:T(128)} %pad_add_fusion.refs_0_, bf16[1024,2048]{1,0:T(8,128)(2,1)} %all-gather.5.cloned.1.call-done.refs_0_.refs_4_.refs_1_, bf16[1024,2048]{1,0:T(8,128)(2,1)} %all-gather.9.cloned.1.call-done.refs_0_.refs_2_.refs_4_, ...), custom_call_target="tpu_custom_call" | custom-call | flops 24999999488 | bytes 25000000 | tf_op jit(solution)/shard_map/heads_grad/pallas_call | solution.py:52
  571.1 6.8 collective-permute-done.30.refs_0_
  578.0 4.2 slice_add_fusion
  624.8 8.2 %norm_grad.3.refs_0_ = f32[2,2,128,2048]{3,2,1,0:T(8,128)} custom-call(s32[2]{0:T(128)} %pad_add_fusion.1.at_ref, bf16[2,2,128,2048]{3,2,1,0:T(8,128)(2,1)} %x_ref.5, bf16[2,2,128,2048]{3,2,1,0:T(8,128)(2,1)} %c_ref.5, bf16[128,2048]{1,0:T(8,128)(2,1)} %get-tuple-element.138.refs_1_.kept_ref, bf16[128,2048]{1,0:T(8,128)(2,1)} %tie.60.refs_2_.got_ref, ...), custom_call_target="tpu_custom_call" | custom-call | flops 750000000 | bytes 750001 | tf_op jit(solution)/shard_map/norm_grad/pallas_call | solution.py:686
  637.7 8.9 %collective-permute-done.44 = bf16[512,1024]{1,0:T(8,128)(2,1)} collective-permute-done((bf16[512,1024]{1,0:T(8,128)(2,1)S(1)}, bf16[512,1024]{1,0:T(8,128)(2,1)}, u32[]{:S(2)}, u32[]{:S(2)}) %collective-permute-start.44) | collective-permute-done | bytes 1048608 | tf_op jit(solution)/shard_map/ppermute | solution.py:527
  667.6 5.1 norm_grad.4.refs_0_
  677.7 5.0 norm_grad.5
  (374 shorter events, 213.8 us)
Async XLA Ops:
  7.2 147.9 %all-gather.5.cloned.1.call-start = ((), (), s32[]{:S(2)}) async-start(), calls=%async_computation.3 | async-start | bytes 5242880 | tf_op jit(solution)/shard_map/all_gather | solution.py:761
  28.1 209.8 %all-gather.7.cloned.1.call-start = ((), (), s32[]{:S(2)}) async-start(), calls=%async_computation.4 | async-start | bytes 5242880 | tf_op jit(solution)/shard_map/all_gather | solution.py:761
  46.0 46.7 %collective-permute-start.5 = (bf16[512,2048]{1,0:T(8,128)(2,1)}, bf16[512,2048]{1,0:T(8,128)(2,1)}, u32[]{:S(2)}, u32[]{:S(2)}) collective-permute-start(bf16[512,2048]{1,0:T(8,128)(2,1)} %tie.33), channel_id=1, source_target_pairs={{0,16},{16,0},{1,17},{17,1},{2,18},{18,2},{3,19},{19,3},{4,20},{20... | collective-permute-start | bytes 6291464 | tf_op jit(solution)/shard_map/ppermute | solution.py:527
  47.6 47.9 %collective-permute-start.3 = (bf16[512,2048]{1,0:T(8,128)(2,1)}, bf16[512,2048]{1,0:T(8,128)(2,1)}, u32[]{:S(2)}, u32[]{:S(2)}) collective-permute-start(bf16[512,2048]{1,0:T(8,128)(2,1)} %tie.33), channel_id=1, source_target_pairs={{0,1},{1,0},{2,3},{3,2},{4,5},{5,4},{6,7},{7,6},{8,9},{9,8},{10,11... | collective-permute-start | bytes 6291464 | tf_op jit(solution)/shard_map/ppermute | solution.py:527
  48.6 263.7 %all-gather.9.cloned.1.call-start = ((), (), s32[]{:S(2)}) async-start(), calls=%async_computation.6 | async-start | bytes 5242880 | tf_op jit(solution)/shard_map/all_gather | solution.py:761
  98.3 37.5 %collective-permute-start.1 = (bf16[512,2048]{1,0:T(8,128)(2,1)}, bf16[512,2048]{1,0:T(8,128)(2,1)}, u32[]{:S(2)}, u32[]{:S(2)}) collective-permute-start(bf16[512,2048]{1,0:T(8,128)(2,1)} %pad_maximum_fusion.1.refs_1_), channel_id=1, source_target_pairs={{0,8},{8,0},{1,9},{9,1},{2,10},{10,2},{3,11},{11,3},{4,12},{12,4},... | collective-permute-start | bytes 6291464 | tf_op jit(solution)/shard_map/ppermute | solution.py:527
  98.3 37.5 %collective-permute-start.6 = (bf16[512,2048]{1,0:T(8,128)(2,1)}, bf16[512,2048]{1,0:T(8,128)(2,1)}, u32[]{:S(2)}, u32[]{:S(2)}) collective-permute-start(bf16[512,2048]{1,0:T(8,128)(2,1)} %tie.35.refs_5_), channel_id=1, source_target_pairs={{0,8},{8,0},{1,9},{9,1},{2,10},{10,2},{3,11},{11,3},{4,12},{12,4},... | collective-permute-start | bytes 6291464 | tf_op jit(solution)/shard_map/ppermute | solution.py:527
  98.8 37.5 %collective-permute-start.4 = (bf16[512,2048]{1,0:T(8,128)(2,1)}, bf16[512,2048]{1,0:T(8,128)(2,1)}, u32[]{:S(2)}, u32[]{:S(2)}) collective-permute-start(bf16[512,2048]{1,0:T(8,128)(2,1)} %tie.34.refs_3_), channel_id=1, source_target_pairs={{0,8},{8,0},{1,9},{9,1},{2,10},{10,2},{3,11},{11,3},{4,12},{12,4},... | collective-permute-start | bytes 6291464 | tf_op jit(solution)/shard_map/ppermute | solution.py:527
  135.8 75.5 %collective-permute-start.17 = (bf16[512,1024]{1,0:T(8,128)(2,1)}, bf16[512,1024]{1,0:T(8,128)(2,1)}, u32[]{:S(2)}, u32[]{:S(2)}) collective-permute-start(bf16[512,1024]{1,0:T(8,128)(2,1)} %bitcast.188), channel_id=1, source_target_pairs={{0,8},{8,0},{1,9},{9,1},{2,10},{10,2},{3,11},{11,3},{4,12},{12,4},... | collective-permute-start | bytes 3145736 | tf_op jit(solution)/shard_map/ppermute | solution.py:527
  135.8 33.3 %collective-permute-start.14 = (bf16[512,1024]{1,0:T(8,128)(2,1)}, bf16[512,1024]{1,0:T(8,128)(2,1)}, u32[]{:S(2)}, u32[]{:S(2)}) collective-permute-start(bf16[512,1024]{1,0:T(8,128)(2,1)} %tie.38), channel_id=1, source_target_pairs={{0,1},{1,0},{2,3},{3,2},{4,5},{5,4},{6,7},{7,6},{8,9},{9,8},{10,11... | collective-permute-start | bytes 3145736 | tf_op jit(solution)/shard_map/ppermute | solution.py:527
  136.3 30.7 %collective-permute-start.13 = (bf16[512,1024]{1,0:T(8,128)(2,1)}, bf16[512,1024]{1,0:T(8,128)(2,1)}, u32[]{:S(2)}, u32[]{:S(2)}) collective-permute-start(bf16[512,1024]{1,0:T(8,128)(2,1)} %tie.38), channel_id=1, source_target_pairs={{0,16},{16,0},{1,17},{17,1},{2,18},{18,2},{3,19},{19,3},{4,20},{20... | collective-permute-start | bytes 3145736 | tf_op jit(solution)/shard_map/ppermute | solution.py:527
  154.8 204.3 %all-gather.11.cloned.1.call-start = ((), (), s32[]{:S(2)}) async-start(), calls=%async_computation.7 | async-start | bytes 5242880 | tf_op jit(solution)/shard_map/all_gather | solution.py:761
  168.1 43.2 %collective-permute-start.19 = (bf16[512,1024]{1,0:T(8,128)(2,1)}, bf16[512,1024]{1,0:T(8,128)(2,1)}, u32[]{:S(2)}, u32[]{:S(2)}) collective-permute-start(bf16[512,1024]{1,0:T(8,128)(2,1)} %tie.39.refs_5_), channel_id=1, source_target_pairs={{0,8},{8,0},{1,9},{9,1},{2,10},{10,2},{3,11},{11,3},{4,12},{12,4},... | collective-permute-start | bytes 3145736 | tf_op jit(solution)/shard_map/ppermute | solution.py:527
  170.9 40.4 %collective-permute-start.18 = (bf16[512,1024]{1,0:T(8,128)(2,1)}, bf16[512,1024]{1,0:T(8,128)(2,1)}, u32[]{:S(2)}, u32[]{:S(2)}) collective-permute-start(bf16[512,1024]{1,0:T(8,128)(2,1)} %tie.40.refs_3_), channel_id=1, source_target_pairs={{0,8},{8,0},{1,9},{9,1},{2,10},{10,2},{3,11},{11,3},{4,12},{12,4},... | collective-permute-start | bytes 3145736 | tf_op jit(solution)/shard_map/ppermute | solution.py:527
  237.4 351.4 %reduce-scatter.4.cloned.1.call-start = ((), (), s32[]{:S(2)}) async-start(), calls=%async_computation.5 | async-start | bytes 10485760 | tf_op jit(solution)/shard_map/reduce_scatter | solution.py:797
  310.6 324.5 %reduce-scatter.6.cloned.1.call-start = ((), (), s32[]{:S(2)}) async-start(), calls=%async_computation.8 | async-start | bytes 5242880 | tf_op jit(solution)/shard_map/reduce_scatter | solution.py:779
  399.5 26.8 %collective-permute-start.22 = (bf16[2,2,512,1024]{3,2,1,0:T(8,128)(2,1)}, bf16[2,2,512,1024]{3,2,1,0:T(8,128)(2,1)}, u32[]{:S(2)}, u32[]{:S(2)}) collective-permute-start(bf16[2,2,512,1024]{3,2,1,0:T(8,128)(2,1)} %get-tuple-element.61), channel_id=1, source_target_pairs={{0,8},{8,0},{1,9},{9,1},{2,10},{10,2},{3,11},{11,3},{4,12},{12,4},... | collective-permute-start | bytes 12582920 | tf_op jit(solution)/shard_map/ppermute | solution.py:527
  424.9 54.7 %collective-permute-start.23 = (bf16[2,2,512,1024]{3,2,1,0:T(8,128)(2,1)}, bf16[2,2,512,1024]{3,2,1,0:T(8,128)(2,1)}, u32[]{:S(2)}, u32[]{:S(2)}) collective-permute-start(bf16[2,2,512,1024]{3,2,1,0:T(8,128)(2,1)} %get-tuple-element.64), channel_id=1, source_target_pairs={{0,8},{8,0},{1,9},{9,1},{2,10},{10,2},{3,11},{11,3},{4,12},{12,4},... | collective-permute-start | bytes 12582920 | tf_op jit(solution)/shard_map/ppermute | solution.py:527
  448.2 46.0 %collective-permute-start.26 = (bf16[256,1024]{1,0:T(8,128)(2,1)}, bf16[256,1024]{1,0:T(8,128)(2,1)}, u32[]{:S(2)}, u32[]{:S(2)}) collective-permute-start(bf16[256,1024]{1,0:T(8,128)(2,1)} %get-tuple-element.141), channel_id=1, source_target_pairs={{0,1},{1,0},{2,3},{3,2},{4,5},{5,4},{6,7},{7,6},{8,9},{9,8},{10,11... | collective-permute-start | bytes 1572872 | tf_op jit(solution)/shard_map/ppermute | solution.py:527
  449.8 39.3 %collective-permute-start.25 = (bf16[256,1024]{1,0:T(8,128)(2,1)}, bf16[256,1024]{1,0:T(8,128)(2,1)}, u32[]{:S(2)}, u32[]{:S(2)}) collective-permute-start(bf16[256,1024]{1,0:T(8,128)(2,1)} %get-tuple-element.142), channel_id=1, source_target_pairs={{0,16},{16,0},{1,17},{17,1},{2,18},{18,2},{3,19},{19,3},{4,20},{20... | collective-permute-start | bytes 1572872 | tf_op jit(solution)/shard_map/ppermute | solution.py:527
  450.4 211.6 %reduce-scatter.8.cloned.1.call-start = ((), (), s32[]{:S(2)}) async-start(), calls=%async_computation.9 | async-start | bytes 5242880 | tf_op jit(solution)/shard_map/reduce_scatter | solution.py:779
  487.3 37.9 %collective-permute-start.27 = (bf16[256,1024]{1,0:T(8,128)(2,1)}, bf16[256,1024]{1,0:T(8,128)(2,1)}, u32[]{:S(2)}, u32[]{:S(2)}) collective-permute-start(bf16[256,1024]{1,0:T(8,128)(2,1)} %get-tuple-element.139), channel_id=1, source_target_pairs={{0,1},{1,0},{2,3},{3,2},{4,5},{5,4},{6,7},{7,6},{8,9},{9,8},{10,11... | collective-permute-start | bytes 1572872 | tf_op jit(solution)/shard_map/ppermute | solution.py:527
  487.7 33.5 %collective-permute-start.24 = (bf16[256,1024]{1,0:T(8,128)(2,1)}, bf16[256,1024]{1,0:T(8,128)(2,1)}, u32[]{:S(2)}, u32[]{:S(2)}) collective-permute-start(bf16[256,1024]{1,0:T(8,128)(2,1)} %get-tuple-element.140), channel_id=1, source_target_pairs={{0,16},{16,0},{1,17},{17,1},{2,18},{18,2},{3,19},{19,3},{4,20},{20... | collective-permute-start | bytes 1572872 | tf_op jit(solution)/shard_map/ppermute | solution.py:527
  492.5 36.3 %collective-permute-start.28 = (bf16[512,1024]{1,0:T(8,128)(2,1)}, bf16[512,1024]{1,0:T(8,128)(2,1)}, u32[]{:S(2)}, u32[]{:S(2)}) collective-permute-start(bf16[512,1024]{1,0:T(8,128)(2,1)} %pad_maximum_fusion.7.refs_5_), channel_id=1, source_target_pairs={{0,1},{1,0},{2,3},{3,2},{4,5},{5,4},{6,7},{7,6},{8,9},{9,8},{10,11... | collective-permute-start | bytes 3145736 | tf_op jit(solution)/shard_map/ppermute | solution.py:527
  497.3 31.4 %collective-permute-start.29 = (bf16[512,1024]{1,0:T(8,128)(2,1)}, bf16[512,1024]{1,0:T(8,128)(2,1)}, u32[]{:S(2)}, u32[]{:S(2)}) collective-permute-start(bf16[512,1024]{1,0:T(8,128)(2,1)} %pad_maximum_fusion.8.refs_6_), channel_id=1, source_target_pairs={{0,16},{16,0},{1,17},{17,1},{2,18},{18,2},{3,19},{19,3},{4,20},{20... | collective-permute-start | bytes 3145736 | tf_op jit(solution)/shard_map/ppermute | solution.py:527
  520.8 40.9 %collective-permute-start.33 = (f32[7936]{0:T(1024)S(1)}, f32[7936]{0:T(1024)S(1)}, u32[]{:S(2)}, u32[]{:S(2)}) collective-permute-start(f32[7936]{0:T(1024)S(1)} %pad_maximum_fusion.17), channel_id=1, source_target_pairs={{0,1},{1,0},{2,3},{3,2},{4,5},{5,4},{6,7},{7,6},{8,9},{9,8},{10,11... | collective-permute-start | bytes 95240 | tf_op jit(solution)/shard_map/ppermute | solution.py:527
  523.5 41.0 %collective-permute-start.31 = (bf16[512,1024]{1,0:T(8,128)(2,1)}, bf16[512,1024]{1,0:T(8,128)(2,1)S(1)}, u32[]{:S(2)}, u32[]{:S(2)}) collective-permute-start(bf16[512,1024]{1,0:T(8,128)(2,1)} %pad_maximum_fusion.9.refs_9_), channel_id=1, source_target_pairs={{0,1},{1,0},{2,3},{3,2},{4,5},{5,4},{6,7},{7,6},{8,9},{9,8},{10,11... | collective-permute-start | bytes 3145736 | tf_op jit(solution)/shard_map/ppermute | solution.py:527
  527.4 38.0 %collective-permute-start.32 = (bf16[512,1024]{1,0:T(8,128)(2,1)}, bf16[512,1024]{1,0:T(8,128)(2,1)S(1)}, u32[]{:S(2)}, u32[]{:S(2)}) collective-permute-start(bf16[512,1024]{1,0:T(8,128)(2,1)} %pad_maximum_fusion.10.refs_10_), channel_id=1, source_target_pairs={{0,16},{16,0},{1,17},{17,1},{2,18},{18,2},{3,19},{19,3},{4,20},{20... | collective-permute-start | bytes 3145736 | tf_op jit(solution)/shard_map/ppermute | solution.py:527
  594.0 30.8 %collective-permute-start.34 = (bf16[128,2048]{1,0:T(8,128)(2,1)}, bf16[128,2048]{1,0:T(8,128)(2,1)}, u32[]{:S(2)}, u32[]{:S(2)}) collective-permute-start(bf16[128,2048]{1,0:T(8,128)(2,1)} %broadcast_select_fusion.12), channel_id=1, source_target_pairs={{0,1},{1,0},{2,3},{3,2},{4,5},{5,4},{6,7},{7,6},{8,9},{9,8},{10,11... | collective-permute-start | bytes 1572872 | tf_op jit(solution)/shard_map/ppermute | solution.py:527
  598.0 26.0 %collective-permute-start.39 = (bf16[128,2048]{1,0:T(8,128)(2,1)}, bf16[128,2048]{1,0:T(8,128)(2,1)S(1)}, u32[]{:S(2)}, u32[]{:S(2)}) collective-permute-start(bf16[128,2048]{1,0:T(8,128)(2,1)} %get-tuple-element.137), channel_id=1, source_target_pairs={{0,1},{1,0},{2,3},{3,2},{4,5},{5,4},{6,7},{7,6},{8,9},{9,8},{10,11... | collective-permute-start | bytes 1572872 | tf_op jit(solution)/shard_map/ppermute | solution.py:527
  620.1 26.5 %collective-permute-start.44 = (bf16[512,1024]{1,0:T(8,128)(2,1)S(1)}, bf16[512,1024]{1,0:T(8,128)(2,1)}, u32[]{:S(2)}, u32[]{:S(2)}) collective-permute-start(bf16[512,1024]{1,0:T(8,128)(2,1)S(1)} %copy-done.6), channel_id=1, source_target_pairs={{0,1},{1,0},{2,3},{3,2},{4,5},{5,4},{6,7},{7,6},{8,9},{9,8},{10,11... | collective-permute-start | bytes 3145736 | tf_op jit(solution)/shard_map/ppermute | solution.py:527
  621.2 25.4 %collective-permute-start.45 = (bf16[512,1024]{1,0:T(8,128)(2,1)S(1)}, bf16[512,1024]{1,0:T(8,128)(2,1)}, u32[]{:S(2)}, u32[]{:S(2)}) collective-permute-start(bf16[512,1024]{1,0:T(8,128)(2,1)S(1)} %copy-done.5), channel_id=1, source_target_pairs={{0,16},{16,0},{1,17},{17,1},{2,18},{18,2},{3,19},{19,3},{4,20},{20... | collective-permute-start | bytes 3145736 | tf_op jit(solution)/shard_map/ppermute | solution.py:527
  (74 other events, 688.6 us)
Sparse Core Ops, SparseCore 0:
  28.2 82.2 all-gather.4
  112.1 79.2 all-gather.6
  193.6 79.2 all-gather.8
  274.9 79.2 all-gather.10
  356.4 143.0 reduce-scatter.3
  501.6 77.4 reduce-scatter.5
  581.5 78.2 reduce-scatter.7
